TPU v7x, 256 devices: a whole 4x4x8 slice. The times are simulated.
256 devices in a mesh: pts: 128 (over z, y, x), rep: 2 (over core).
Axes of the slice: x: 4, y: 4, z: 8, core: 2. Of those that a mesh axis runs over, the one named last changes fastest.
Arguments:
- feats: bfloat16 [2, 64, 131072], P('rep', None, 'pts'), may hold values from -6 to 6
- hilbert_of_z: int32 [2, 131072], P('rep', 'pts'), may hold values from 0 to 131071, as said below
- pool_owner: int32 [2, 131072, 1], P('rep', 'pts'), may hold values from 0 to 127; in each aligned block of 1024 rows (0 to 1023, 1024 to 2047, ..., all dimensions but the last counted through in order) at most 16 rows name the same one
- pool_slot: int32 [2, 131072], P('rep', 'pts'), may hold values from 0 to 255
- qkv_weight: bfloat16 [192, 64], replicated, may hold values from -0.75 to 0.75
- out_weight: bfloat16 [64, 64], replicated, may hold values from -0.75 to 0.75
- pool_weight: bfloat16 [128, 64], replicated, may hold values from -0.75 to 0.75
- norm_gain: float32 [64], replicated, may hold values from 0.1 to 1.9
- pooled_grad: bfloat16 [2, 128, 32768], P('rep', None, 'pts'), may hold values from -6 to 6
Outputs:
- pooled: bfloat16 [2, 128, 32768], P('rep', None, 'pts')
- feat_grad: bfloat16 [2, 64, 131072], P('rep', None, 'pts')
- qkv_grad: float32 [192, 64], replicated
- out_grad: float32 [64, 64], replicated
- pool_grad: float32 [128, 64], replicated
- gain_grad: float32 [64], replicated
Inputs may be any that keep to these rules, and one draw needn't show every extreme that they name: For each window, hilbert_of_z is a permutation of the 131072 positions; the 1024 z-order points of each shard land on each Hilbert shard of 1024 positions exactly 1024 // 128 times. `pool_owner`: within the 1024 points of one device, no owner is named more than 16 times, a bound that some block reaches.
All inputs are finite; a program needn't handle non-finite values.
Results may differ from a plain program's by a relative error of at most 0.0084.
Values may be sent and summed in bfloat16 or wider, within the bound.
No kernel may reach another device: no remote copies, remote signals or barrier semaphores. Data moves between devices by JAX's collectives and lax.ppermute only.
A program may use at most 64 MiB of HBM per device.

v0:
```python
import jax
import jax.numpy as jnp
from jax import lax
from jax.sharding import PartitionSpec as P

HEADS = 4
PATCH = 1024
HEAD_DIM = 16


NORM_EPS = 1e-05


def layer_norm(inputs, norm_gain):
    floats = inputs.astype(jnp.float32)
    centred = floats - jnp.mean(floats, axis=0, keepdims=True)
    inverse_std = lax.rsqrt(jnp.mean(centred * centred, axis=0, keepdims=True) + NORM_EPS)
    normed = centred * inverse_std
    hidden = (norm_gain[:, None] * normed).astype(jnp.bfloat16)
    return (floats, normed, inverse_std, hidden)


def probabilities(queries, key_rows):
    scores = jnp.dot(queries.T, key_rows, preferred_element_type=jnp.float32) * HEAD_DIM ** (-0.5)
    weights = jnp.exp(scores)
    return weights / jnp.sum(weights, axis=1, keepdims=True)


def attend_forward(triple):
    rounded = probabilities(triple[0], triple[1]).astype(jnp.bfloat16)
    return jnp.dot(triple[2], rounded.T, preferred_element_type=jnp.float32).astype(jnp.bfloat16)


def attend_backward(inputs):
    triple, upstream = inputs
    queries, key_rows, values = (triple[0], triple[1], triple[2])
    probs = probabilities(queries, key_rows)
    rounded = probs.astype(jnp.bfloat16)
    grad_values = jnp.dot(upstream, rounded, preferred_element_type=jnp.float32)
    grad_probs = jnp.dot(upstream.T, values, preferred_element_type=jnp.float32)
    grad_scores = (
        probs
        * (grad_probs - jnp.sum(probs * grad_probs, axis=1, keepdims=True))
        * HEAD_DIM ** (-0.5)
    )
    grad_scores = grad_scores.astype(jnp.bfloat16)
    grad_queries = jnp.dot(key_rows, grad_scores.T, preferred_element_type=jnp.float32)
    grad_keys = jnp.dot(queries, grad_scores, preferred_element_type=jnp.float32)
    return jnp.stack([grad_queries, grad_keys, grad_values]).astype(jnp.bfloat16)


def split_heads(qkv_rows):
    patches = qkv_rows.shape[1] // PATCH
    shaped = qkv_rows.reshape(3, HEADS, HEAD_DIM, patches, PATCH).transpose(3, 1, 0, 2, 4)
    return shaped.reshape(patches * HEADS, 3, HEAD_DIM, PATCH)


def split_single(head_rows):
    patches = head_rows.shape[1] // PATCH
    shaped = head_rows.reshape(HEADS, HEAD_DIM, patches, PATCH).transpose(2, 0, 1, 3)
    return shaped.reshape(patches * HEADS, HEAD_DIM, PATCH)


def merge_heads(items, length):
    patches = length // PATCH
    return (
        items.reshape(patches, HEADS, HEAD_DIM, PATCH)
        .transpose(1, 2, 0, 3)
        .reshape(HEADS * HEAD_DIM, length)
    )


def merge_triples(items, length):
    patches = length // PATCH
    shaped = items.reshape(patches, HEADS, 3, HEAD_DIM, PATCH).transpose(2, 1, 3, 0, 4)
    return shaped.reshape(3 * HEADS * HEAD_DIM, length)


def block_forward(hilbert_rows, qkv_weight, out_weight, norm_gain):
    floats, normed, inverse_std, hidden = layer_norm(hilbert_rows, norm_gain)
    qkv_rows = jnp.dot(qkv_weight, hidden, preferred_element_type=jnp.float32).astype(jnp.bfloat16)
    triples = split_heads(qkv_rows)
    attended = merge_heads(lax.map(attend_forward, triples), hilbert_rows.shape[1])
    mixed = (floats + jnp.dot(out_weight, attended, preferred_element_type=jnp.float32)).astype(
        jnp.bfloat16
    )
    return (mixed, (normed, inverse_std, hidden, triples, attended))


def block_backward(upstream, saved, qkv_weight, out_weight, norm_gain):
    normed, inverse_std, hidden, triples, attended = saved
    length = upstream.shape[1]
    grad_out_weight = jnp.dot(upstream, attended.T, preferred_element_type=jnp.float32)
    grad_attended = jnp.dot(out_weight.T, upstream, preferred_element_type=jnp.float32).astype(
        jnp.bfloat16
    )
    grad_triples = lax.map(attend_backward, (triples, split_single(grad_attended)))
    grad_qkv = merge_triples(grad_triples, length)
    grad_qkv_weight = jnp.dot(grad_qkv, hidden.T, preferred_element_type=jnp.float32)
    grad_hidden = jnp.dot(qkv_weight.T, grad_qkv, preferred_element_type=jnp.float32)
    grad_gain = jnp.sum(grad_hidden * normed, axis=1)
    grad_normed = grad_hidden * norm_gain[:, None]
    grad_norm_in = inverse_std * (
        grad_normed
        - jnp.mean(grad_normed, axis=0, keepdims=True)
        - normed * jnp.mean(grad_normed * normed, axis=0, keepdims=True)
    )
    grad_rows = (upstream.astype(jnp.float32) + grad_norm_in).astype(jnp.bfloat16)
    return (grad_rows, grad_qkv_weight, grad_out_weight, grad_gain)


def pack_blocks(columns, shard_count):
    channels, total = columns.shape
    width = total // shard_count
    return (
        columns.reshape(channels, shard_count, width)
        .transpose(1, 0, 2)
        .reshape(shard_count, channels * width)
    )


def unpack_blocks(packed, channels):
    shard_count, flat = packed.shape
    width = flat // channels
    return (
        packed.reshape(shard_count, channels, width)
        .transpose(1, 0, 2)
        .reshape(channels, shard_count * width)
    )


def body(
    feats,
    hilbert_of_z,
    pool_owner,
    pool_slot,
    qkv_weight,
    out_weight,
    pool_weight,
    norm_gain,
    pooled_grad,
):
    source_rows = feats[0]
    channels, length = source_rows.shape
    shard_count = lax.axis_size("pts")
    per_peer = length // shard_count
    capacity = 2 * length // shard_count
    clusters_dev = pooled_grad.shape[2]
    positions = hilbert_of_z[0]
    sort_order = jnp.argsort(positions)
    outgoing = pack_blocks(source_rows[:, sort_order], shard_count)
    outgoing_pos = (positions[sort_order] % length).reshape(shard_count, per_peer)
    arrived, arrived_pos = (
        lax.all_to_all(outgoing, "pts", split_axis=0, concat_axis=0, tiled=True),
        lax.all_to_all(outgoing_pos, "pts", split_axis=0, concat_axis=0, tiled=True),
    )
    arrived_flat = arrived_pos.reshape(length)
    hilbert_rows = unpack_blocks(arrived, channels)[:, jnp.argsort(arrived_flat)]
    owner_ids = pool_owner[0, :, 0]
    cluster_slots = pool_slot[0]
    row_range = jnp.arange(length, dtype=jnp.int32)
    by_owner = jnp.argsort(owner_ids * length + row_range)
    owner_counts = jnp.sum(
        (owner_ids[:, None] == jnp.arange(shard_count, dtype=jnp.int32)[None, :]).astype(jnp.int32),
        axis=0,
    )
    owner_starts = jnp.cumsum(owner_counts) - owner_counts
    rank_sorted = row_range - owner_starts[owner_ids[by_owner]]
    buffer_index = owner_ids * capacity + rank_sorted[jnp.argsort(by_owner)]
    buffer_range = jnp.arange(shard_count * capacity, dtype=jnp.int32)
    buffer_owner = buffer_range // capacity
    buffer_rank = buffer_range % capacity
    filled = buffer_rank < owner_counts[buffer_owner]
    source_row = by_owner[jnp.clip(owner_starts[buffer_owner] + buffer_rank, 0, length - 1)]
    outgoing_ids = jnp.where(filled, cluster_slots[source_row], -1).reshape(shard_count, capacity)
    upstream_pool = pooled_grad[0]
    mixed, saved = block_forward(hilbert_rows, qkv_weight, out_weight, norm_gain)
    picked = jnp.where(filled[None, :], mixed[:, source_row], jnp.zeros((), jnp.bfloat16))
    arrived_rows = lax.all_to_all(
        pack_blocks(picked, shard_count), "pts", split_axis=0, concat_axis=0, tiled=True
    )
    arrived_ids = lax.all_to_all(outgoing_ids, "pts", split_axis=0, concat_axis=0, tiled=True)
    matches = arrived_ids.reshape(-1)[:, None] == jnp.arange(clusters_dev, dtype=jnp.int32)[None, :]
    counts = jnp.sum(matches.astype(jnp.float32), axis=0)
    onehot = matches.astype(jnp.bfloat16)
    denom = jnp.maximum(counts, 1.0)
    grad_mean = (
        jnp.dot(pool_weight.T, upstream_pool, preferred_element_type=jnp.float32) / denom[None, :]
    ).astype(jnp.bfloat16)
    per_slot = jnp.dot(grad_mean, onehot.T, preferred_element_type=jnp.float32).astype(jnp.bfloat16)
    came_back = lax.all_to_all(
        pack_blocks(per_slot, shard_count), "pts", split_axis=0, concat_axis=0, tiled=True
    )
    grad_mixed = unpack_blocks(came_back, channels)[:, buffer_index]
    sums = jnp.dot(
        unpack_blocks(arrived_rows, channels), onehot, preferred_element_type=jnp.float32
    )
    pooled_mean = (sums / denom[None, :]).astype(jnp.bfloat16)
    pooled = jnp.dot(pool_weight, pooled_mean, preferred_element_type=jnp.float32).astype(
        jnp.bfloat16
    )
    grad_pool_weight = jnp.dot(upstream_pool, pooled_mean.T, preferred_element_type=jnp.float32)
    pool_total = lax.psum(grad_pool_weight, ("pts", "rep"))
    grad_rows, grad_qkv_weight, grad_out_weight, grad_gain = block_backward(
        grad_mixed, saved, qkv_weight, out_weight, norm_gain
    )
    out_total = lax.psum(grad_out_weight, ("pts", "rep"))
    qkv_total, gain_total = lax.psum((grad_qkv_weight, grad_gain), ("pts", "rep"))
    returned = lax.all_to_all(
        pack_blocks(grad_rows[:, arrived_flat], shard_count),
        "pts",
        split_axis=0,
        concat_axis=0,
        tiled=True,
    )
    feat_grad = unpack_blocks(returned, channels)[:, jnp.argsort(sort_order)]
    factor = float(lax.axis_size("rep") * shard_count * length) ** (-0.5)
    return (
        pooled[None],
        feat_grad[None],
        qkv_total * factor,
        out_total * factor,
        pool_total * factor,
        gain_total * factor,
    )


def solution(mesh):
    return jax.shard_map(
        body,
        mesh=mesh,
        in_specs=(
            P("rep", None, "pts"),
            P("rep", "pts"),
            P("rep", "pts", None),
            P("rep", "pts"),
            P(),
            P(),
            P(),
            P(),
            P("rep", None, "pts"),
        ),
        out_specs=(P("rep", None, "pts"), P("rep", None, "pts"), P(), P(), P(), P()),
        check_vma=False,
    )
```

profile of v0, /device:TPU:1, one launch (start us, length us, event | category | flops | bytes accessed | tf_op | source)
XLA Modules:
  0.0 508.1 jit_solution(11141108230724056223)
XLA Ops:
  7.2 5.1 sort.73
  12.3 5.7 %gather_fusion.2 = s32[1024]{0:T(1024)S(1)} fusion(s32[1024]{0:T(1024)} %bitcast.232, s32[1024]{0:T(1024)S(1)} %fusion.75), kind=kCustom, calls=%fused_computation.2 | custom fusion | bytes 12288 | tf_op jit(solution)/shard_map/gather | solution.py:152
  18.7 16.3 %all-to-all-start.1 = ((s32[128,1,8]{2,1,0:T(1,128)}), s32[128,1,8]{2,1,0:T(1,128)S(1)}, u32[]{:S(2)}, u32[]{:S(2)}) async-start(s32[128,1,8]{2,1,0:T(1,128)} %bitcast.22), calls=%async_computation.1 | async-start | bytes 131072 | tf_op jit(solution)/shard_map/all_to_all | solution.py:155
  35.4 12.6 %gather_fusion = s32[2048]{0:T(1024)S(1)} fusion(s32[128]{0:T(128)S(1)} %convert_reduce_fusion.1, s32[2048]{0:T(1024)S(1)} %broadcast_clamp_fusion.2), kind=kCustom, calls=%fused_computation | custom fusion | bytes 24576 | tf_op jit(solution)/shard_map/gather | solution.py:173
  48.2 4.4 sort.75
  52.5 4.5 gather_fusion.8
  57.1 4.4 sort.77
  61.5 4.4 sort.76
  66.3 12.6 %gather_fusion.4 = s32[2048]{0:T(1024)S(1)} fusion(s32[128]{0:T(128)S(1)} %sub.44, s32[2048]{0:T(1024)S(1)} %broadcast_clamp_fusion.2), kind=kCustom, calls=%fused_computation.4 | custom fusion | bytes 24576 | tf_op jit(solution)/shard_map/gather | solution.py:174
  78.9 6.6 %gather_fusion.9 = s32[1024]{0:T(1024)S(1)} fusion(s32[128]{0:T(128)S(1)} %sub.44, s32[1024]{0:T(1024)S(1)} %broadcast_clamp_fusion.4), kind=kCustom, calls=%fused_computation.9 | custom fusion | bytes 12288 | tf_op jit(solution)/shard_map/gather | solution.py:168
  85.5 8.6 %gather_fusion.5 = s32[2048]{0:T(1024)S(1)} fusion(s32[1024]{0:T(1024)S(1)} %get-tuple-element.53, s32[2048]{0:T(1024)S(1)} %broadcast_clamp_fusion.1), kind=kCustom, calls=%fused_computation.5 | custom fusion | bytes 24576 | tf_op jit(solution)/shard_map/gather | solution.py:174
  94.2 4.5 gather_fusion.10
  98.8 8.6 %gather_fusion.7 = s32[2048]{0:T(1024)S(1)} fusion(s32[1024]{0:T(1024)S(1)} %bitcast.227, s32[2048]{0:T(1024)S(1)} %broadcast_clamp_fusion), kind=kCustom, calls=%fused_computation.7 | custom fusion | bytes 24576 | tf_op jit(solution)/shard_map/gather | solution.py:175
  108.4 3.2 gather_fusion.1
  113.8 13.2 %all-to-all-start.3 = ((s32[128,1,16]{2,1,0:T(1,128)}), s32[128,1,16]{2,1,0:T(1,128)S(1)}, u32[]{:S(2)}, u32[]{:S(2)}) async-start(s32[128,1,16]{2,1,0:T(1,128)} %bitcast.43), calls=%async_computation.3 | async-start | bytes 131072 | tf_op jit(solution)/shard_map/all_to_all | solution.py:182
  128.6 4.4 sort.74
  133.0 4.7 all-to-all-done.3
  137.7 8.5 %all-to-all-start = ((bf16[128,2,256]{2,1,0:T(2,128)(2,1)}), bf16[128,2,256]{2,1,0:T(2,128)(2,1)S(1)}, u32[]{:S(2)}, u32[]{:S(2)}) async-start(bf16[128,2,256]{2,1,0:T(2,128)(2,1)} %reshape.665), calls=%async_computation | async-start | bytes 262144 | tf_op jit(solution)/shard_map/all_to_all | solution.py:154
  149.9 0.9 reshape.669
  150.8 6.7 %all-to-all-done = bf16[128,2,256]{2,1,0:T(2,128)(2,1)S(1)} async-done(((bf16[128,2,256]{2,1,0:T(2,128)(2,1)}), bf16[128,2,256]{2,1,0:T(2,128)(2,1)S(1)}, u32[]{:S(2)}, u32[]{:S(2)}) %all-to-all-start) | async-done | bytes 131104 | tf_op jit(solution)/shard_map/all_to_all | solution.py:154
  157.4 6.5 %all-to-all-start.4 = ((bf16[128,2,512]{2,1,0:T(2,128)(2,1)}), bf16[128,2,512]{2,1,0:T(2,128)(2,1)S(1)}, u32[]{:S(2)}, u32[]{:S(2)}) async-start(bf16[128,2,512]{2,1,0:T(2,128)(2,1)} %reshape.669), calls=%async_computation.4 | async-start | bytes 524288 | tf_op jit(solution)/shard_map/all_to_all | solution.py:191
  164.5 3.2 gather_fusion.3
  168.3 6.3 %while.20 = (s32[]{:T(128)}, bf16[4,16,1024]{2,1,0:T(8,128)(2,1)S(1)}, bf16[4,3,16,1024]{3,2,1,0:T(8,128)(2,1)S(1)}, s32[]{:T(128)}, s32[]{:T(128)}, /*index=5*/s32[]{}, s32[]{}) while((s32[]{:T(128)}, bf16[4,16,1024]{2,1,0:T(8,128)(2,1)S(1)}, bf16[4,3,16,1024]{3,2,1,0:T(8,128)(2,1)S(1)}, s32[]{:T(128)}, s32[]{:T(128)}, /*index=5*/s32[]{}, ...), condition=%wide.region_7.8_spmd, body=%wide.region_5.7_spmd.sunk | while | flops 72367104 | bytes 8531053 | solution.py:83
  175.0 6.2 %gather_fusion.6 = bf16[2048,64]{1,0:T(8,128)(2,1)S(1)} fusion(bf16[64,1024]{0,1:T(8,128)(2,1)S(1)} %copy.84, s32[2048]{0:T(1024)S(1)} %broadcast_clamp_fusion), kind=kCustom, calls=%fused_computation.6 | custom fusion | bytes 532480 | tf_op jit(solution)/shard_map/gather | solution.py:178
  182.7 0.9 reshape.667
  183.6 13.4 %all-to-all-start.2 = ((bf16[128,2,512]{2,1,0:T(2,128)(2,1)}), bf16[128,2,512]{2,1,0:T(2,128)(2,1)S(1)}, u32[]{:S(2)}, u32[]{:S(2)}) async-start(bf16[128,2,512]{2,1,0:T(2,128)(2,1)} %reshape.667), calls=%async_computation.2 | async-start | bytes 524288 | tf_op jit(solution)/shard_map/all_to_all | solution.py:179
  198.3 3.2 gather_fusion.11
  201.9 19.4 %while.21 = (s32[]{:T(128)}, bf16[4,3,16,1024]{3,2,0,1:T(8,128)(2,1)S(1)}, bf16[4,3,16,1024]{3,2,1,0:T(8,128)(2,1)S(1)}, bf16[4,16,1024]{2,1,0:T(8,128)(2,1)S(1)}, s32[]{:T(128)}, /*index=5*/s32[]{:T(128)}, s32[]{}, s32[]{}) while((s32[]{:T(128)}, bf16[4,3,16,1024]{3,2,0,1:T(8,128)(2,1)S(1)}, bf16[4,3,16,1024]{3,2,1,0:T(8,128)(2,1)S(1)}, ...), condition=%wide.region_15.16_spmd, body=%wide.region_12.15_spmd.sunk | while | flops 183842816 | bytes 32009352 | solution.py:97
  203.5 1.0 multiply_reduce_fusion.3
  204.5 1.2 multiply_convert_fusion.2
  208.3 1.0 multiply_reduce_fusion.3
  209.3 1.2 multiply_convert_fusion.2
  213.2 1.0 multiply_reduce_fusion.3
  214.2 1.2 multiply_convert_fusion.2
  218.0 1.0 multiply_reduce_fusion.3
  219.0 1.2 multiply_convert_fusion.2
  221.3 0.8 fusion.57
  222.5 3.2 gather_fusion.12
  227.4 0.8 fusion.80
  228.2 0.9 fusion.70
  229.2 13.0 %all-to-all-start.5 = ((bf16[128,2,256]{2,1,0:T(2,128)(2,1)}), bf16[128,2,256]{2,1,0:T(2,128)(2,1)S(1)}, u32[]{:S(2)}, u32[]{:S(2)}) async-start(bf16[128,2,256]{2,1,0:T(2,128)(2,1)} %reshape.671), calls=%async_computation.5 | async-start | bytes 262144 | tf_op jit(solution)/shard_map/all_to_all | solution.py:209
  245.8 7.5 %all-to-all-done.5 = bf16[128,2,256]{2,1,0:T(2,128)(2,1)S(1)} async-done(((bf16[128,2,256]{2,1,0:T(2,128)(2,1)}), bf16[128,2,256]{2,1,0:T(2,128)(2,1)S(1)}, u32[]{:S(2)}, u32[]{:S(2)}) %all-to-all-start.5) | async-done | bytes 131104 | tf_op jit(solution)/shard_map/all_to_all | solution.py:209
  253.9 3.2 gather_fusion.13
  257.9 238.1 %all-reduce.3.cloned.1.call-done = (f32[192,64]{0,1:T(8,128)}, f32[64,64]{1,0:T(8,128)}, f32[128,64]{0,1:T(8,128)}, f32[64]{0:T(128)}) async-done(((f32[192,64]{0,1:T(8,128)}, f32[64,64]{1,0:T(8,128)}, f32[128,64]{0,1:T(8,128)}, f32[64]{0:T(128)}), (f32[192,64]{0,1:T(8,128)}, f32[64,64]{1,0:T(8,128)}, f32[128,64]{0,1:T(8,128)}, f32[64]{0:T(128)})) %all-reduce.3.cloned.1.call-update) | async-done | bytes 98576 | tf_op jit(solution)/shard_map/psum | solution.py:208
  496.0 1.5 broadcast_multiply_fusion
  497.4 1.1 broadcast_multiply_fusion.6
  498.5 1.4 broadcast_multiply_fusion.2
  499.9 1.4 broadcast_multiply_fusion.1
  (146 shorter events, 38.3 us)
Async XLA Ops:
  7.2 140.3 %copy-start = (bf16[1,128,256]{2,1,0:T(8,128)(2,1)S(1)}, bf16[1,128,256]{2,1,0:T(8,128)(2,1)}, u32[]{:S(2)}) copy-start(bf16[1,128,256]{2,1,0:T(8,128)(2,1)} %param.21) | copy-start | bytes 196612
  7.2 27.9 %copy-start.2 = (s32[1,1024,1]{1,2,0:T(1,128)S(1)}, s32[1,1024,1]{1,2,0:T(1,128)}, u32[]{:S(2)}) copy-start(s32[1,1024,1]{1,2,0:T(1,128)} %param.15) | copy-start | bytes 12292
  18.7 95.1 %all-to-all-start.1 = ((s32[128,1,8]{2,1,0:T(1,128)}), s32[128,1,8]{2,1,0:T(1,128)S(1)}, u32[]{:S(2)}, u32[]{:S(2)}) async-start(s32[128,1,8]{2,1,0:T(1,128)} %bitcast.22), calls=%async_computation.1 | async-start | bytes 131072 | tf_op jit(solution)/shard_map/all_to_all | solution.py:155
  94.1 4.6 copy-start.1
  98.8 9.4 %copy-start.3 = (bf16[1,64,1024]{2,1,0:T(8,128)(2,1)S(1)}, bf16[1,64,1024]{2,1,0:T(8,128)(2,1)}, u32[]{:S(2)}) copy-start(bf16[1,64,1024]{2,1,0:T(8,128)(2,1)} %param.13) | copy-start | bytes 393220
  98.8 48.7 %copy-start.6 = (bf16[128,64]{0,1:T(8,128)(2,1)S(1)}, bf16[128,64]{0,1:T(8,128)(2,1)}, u32[]{:S(2)}) copy-start(bf16[128,64]{0,1:T(8,128)(2,1)} %param.19) | copy-start | bytes 49156
  113.8 23.9 %all-to-all-start.3 = ((s32[128,1,16]{2,1,0:T(1,128)}), s32[128,1,16]{2,1,0:T(1,128)S(1)}, u32[]{:S(2)}, u32[]{:S(2)}) async-start(s32[128,1,16]{2,1,0:T(1,128)} %bitcast.43), calls=%async_computation.3 | async-start | bytes 131072 | tf_op jit(solution)/shard_map/all_to_all | solution.py:182
  127.7 40.3 %copy-start.5 = (bf16[192,64]{0,1:T(8,128)(2,1)S(1)}, bf16[192,64]{0,1:T(8,128)(2,1)}, u32[]{:S(2)}) copy-start(bf16[192,64]{0,1:T(8,128)(2,1)} %param.17) | copy-start | bytes 73732
  127.7 40.3 %copy-start.7 = (f32[64]{0:T(128)S(1)}, f32[64]{0:T(128)}, u32[]{:S(2)}) copy-start(f32[64]{0:T(128)} %param.20) | copy-start | bytes 772
  137.7 19.7 %all-to-all-start = ((bf16[128,2,256]{2,1,0:T(2,128)(2,1)}), bf16[128,2,256]{2,1,0:T(2,128)(2,1)S(1)}, u32[]{:S(2)}, u32[]{:S(2)}) async-start(bf16[128,2,256]{2,1,0:T(2,128)(2,1)} %reshape.665), calls=%async_computation | async-start | bytes 262144 | tf_op jit(solution)/shard_map/all_to_all | solution.py:154
  157.4 26.2 %all-to-all-start.4 = ((bf16[128,2,512]{2,1,0:T(2,128)(2,1)}), bf16[128,2,512]{2,1,0:T(2,128)(2,1)S(1)}, u32[]{:S(2)}, u32[]{:S(2)}) async-start(bf16[128,2,512]{2,1,0:T(2,128)(2,1)} %reshape.669), calls=%async_computation.4 | async-start | bytes 524288 | tf_op jit(solution)/shard_map/all_to_all | solution.py:191
  168.3 6.3 %copy-start.4 = (bf16[64,64]{1,0:T(8,128)(2,1)S(1)}, bf16[64,64]{1,0:T(8,128)(2,1)}, u32[]{:S(2)}) copy-start(bf16[64,64]{1,0:T(8,128)(2,1)} %param.18) | copy-start | bytes 24580
  183.6 45.5 %all-to-all-start.2 = ((bf16[128,2,512]{2,1,0:T(2,128)(2,1)}), bf16[128,2,512]{2,1,0:T(2,128)(2,1)S(1)}, u32[]{:S(2)}, u32[]{:S(2)}) async-start(bf16[128,2,512]{2,1,0:T(2,128)(2,1)} %reshape.667), calls=%async_computation.2 | async-start | bytes 524288 | tf_op jit(solution)/shard_map/all_to_all | solution.py:179
  229.2 24.2 %all-to-all-start.5 = ((bf16[128,2,256]{2,1,0:T(2,128)(2,1)}), bf16[128,2,256]{2,1,0:T(2,128)(2,1)S(1)}, u32[]{:S(2)}, u32[]{:S(2)}) async-start(bf16[128,2,256]{2,1,0:T(2,128)(2,1)} %reshape.671), calls=%async_computation.5 | async-start | bytes 262144 | tf_op jit(solution)/shard_map/all_to_all | solution.py:209
  242.1 253.8 %all-reduce.3.cloned.1.call-start = ((), (), s32[]{:S(2)}) async-start(), calls=%async_computation.6 | async-start | bytes 263168 | tf_op jit(solution)/shard_map/psum | solution.py:208
Sparse Core Ops, SparseCore 0:
  249.6 246.3 all-reduce.2
where the time goes:
time: 509 us; the launch traced here: 508 us
  waiting for transfers between devices  257 us (50%)
  local copies, waits for them, and re-layouts  99.1 us (19%)
  starting transfers between devices  70.9 us (14%)
  other arithmetic  39.9 us (8%)
  matrix products  26.2 us (5%)
  between operations  14.8 us (3%)
    psum x1, waiting for transfers between devices, body(): lax.psum((grad_qkv_weight, grad_gain), ('pts', 'rep'))  238 us
    all_to_all x1, starting transfers between devices, body(): lax.all_to_all(outgoing_pos, 'pts', split_axis=0, concat_axis=0, tiled=True)  16.3 us
    all_to_all x1, starting transfers between devices, body(): lax.all_to_all(pack_blocks(picked, shard_count), 'pts', split_axis=0, con...  13.4 us
    all_to_all x1, starting transfers between devices, body(): lax.all_to_all(outgoing_ids, 'pts', split_axis=0, concat_axis=0, tiled=True)  13.2 us
    all_to_all x1, starting transfers between devices, body(): lax.all_to_all(pack_blocks(grad_rows[:, arrived_flat], shard_count), 'pts...  13 us
    gather x3, local copies, waits for them, and re-layouts, body(): filled = buffer_rank < owner_counts[buffer_owner]  12.8 us
    gather x1, local copies, waits for them, and re-layouts, body(): owner_starts[buffer_owner] + buffer_rank  12.6 us
    gather x2, local copies, waits for them, and re-layouts, body(): rank_sorted = row_range - owner_starts[owner_ids[by_owner]]  11.1 us
  transfers between devices with their start and end apart: 7, of which 4 were waited for; matrix products, arithmetic and copies ran while one was open for 29% of the time, Pallas kernels for 0%

commit v1 on v0

v1 whole, which is shorter than its diff:
```python
import functools

import jax
import jax.numpy as jnp
from jax import lax
from jax.experimental import pallas as pl
from jax.experimental.pallas import tpu as pltpu
from jax.sharding import PartitionSpec as P

HEADS = 4
HEAD_DIM = 16
CHANNELS = 64
NORM_EPS = 1e-05
CHUNK = 256

F32 = jnp.float32
BF16 = jnp.bfloat16
I32 = jnp.int32


def dot(a, b):
    return lax.dot_general(a, b, (((1,), (0,)), ((), ())), preferred_element_type=F32)


def dot_nt(a, b):
    return lax.dot_general(a, b, (((1,), (1,)), ((), ())), preferred_element_type=F32)


def dot_tn(a, b):
    return lax.dot_general(a, b, (((0,), (0,)), ((), ())), preferred_element_type=F32)


def turned(a):
    return a.astype(F32).T


def iota(shape, dim):
    return lax.broadcasted_iota(I32, shape, dim)


def onehot(mask):
    return jnp.where(mask, 1.0, 0.0).astype(BF16)


def on_rows(row, count):
    return onehot(iota((count, row.shape[1]), 0) == row)


def on_columns(column, count):
    return onehot(iota((column.shape[0], count), 1) == column)


def rank_in_group(groups, count):
    length = groups.shape[1]
    member = on_rows(groups, count)
    upto = onehot(iota((128, 128), 0) <= iota((128, 128), 1))
    seen = jnp.zeros((count, 1), F32)
    ranks = []
    for start in range(0, length, 128):
        block = member[:, start : start + 128]
        running = dot(block, upto) + seen
        seen = running[:, 127:128]
        ranks.append(jnp.sum(block.astype(F32) * running, axis=0, keepdims=True) - 1.0)
    return jnp.concatenate(ranks, axis=1).astype(I32)


def send_kernel(pos_ref, owner_ref, cell_ref, feats_ref, out_ref, z_slot_ref, o_slot_ref):
    length = pos_ref.shape[1]
    shards = out_ref.shape[0]
    per_peer = length // shards
    positions = pos_ref[...]
    owners = owner_ref[...]
    shift = length.bit_length() - 1
    target = lax.shift_right_logical(positions, shift)
    local = lax.bitwise_and(positions, length - 1)
    z_slot = target * per_peer + rank_in_group(target, shards)
    o_slot = owners * (2 * per_peer) + rank_in_group(owners, shards)
    z_slot_ref[...] = z_slot
    o_slot_ref[...] = o_slot
    row = iota((CHANNELS, length), 0)
    high = lax.shift_right_logical(local, 5).astype(F32)
    low = lax.bitwise_and(local, 31).astype(F32)
    place = jnp.where(row == 0, high, jnp.where(row == 1, low, 0.0)).astype(BF16)
    cell = (cell_ref[...] + 1).astype(F32)
    odd = lax.bitwise_and(o_slot, 1)
    cells = jnp.where(row - 2 == odd, cell, 0.0).astype(BF16)
    first = jnp.concatenate([feats_ref[...], place], axis=0)
    second = jnp.concatenate([jnp.zeros((CHANNELS, length), BF16), cells], axis=0)
    out = dot_nt(on_rows(z_slot, length), first)
    out = out + dot_nt(on_rows(lax.shift_right_logical(o_slot, 1), length), second)
    out_ref[...] = out.astype(BF16).reshape(out_ref.shape)


def arrived_columns(arrived):
    side = arrived[:, CHANNELS:].astype(F32)
    place = (side[:, 0:1] * 32.0 + side[:, 1:2]).astype(I32)
    return place, side[:, 2:3].astype(I32) - 1, side[:, 3:4].astype(I32) - 1


def gain_column(gain_ref):
    gain = gain_ref[...]
    eye = iota((CHANNELS, CHANNELS), 0) == iota((CHANNELS, CHANNELS), 1)
    return jnp.sum(jnp.where(eye, gain, 0.0), axis=1, keepdims=True)


def layer_norm(floats, gain):
    centred = floats - jnp.mean(floats, axis=0, keepdims=True)
    inverse_std = lax.rsqrt(jnp.mean(centred * centred, axis=0, keepdims=True) + NORM_EPS)
    normed = centred * inverse_std
    return normed, inverse_std, (gain * normed).astype(BF16)


def cluster_counts(first, second):
    return jnp.maximum(
        jnp.sum(first.astype(F32) + second.astype(F32), axis=0, keepdims=True), 1.0
    )


def head_lanes(shape, head):
    return lax.shift_right_logical(iota(shape, 1), 4) == head


def forward_kernel(
    arrived_ref,
    o_slot_ref,
    qkv_t_ref,
    out_w_ref,
    pool_t_ref,
    gain_ref,
    pool_grad_ref,
    out_ref,
    hilbert_ref,
    attended_ref,
    probs_ref,
    query_ref,
    key_ref,
    value_ref,
    rows_ref,
):
    shards = out_ref.shape[0]
    length = arrived_ref.shape[0]
    clusters = pool_grad_ref.shape[1]
    arrived = arrived_ref[...]
    place, first_cell, second_cell = arrived_columns(arrived)
    first = on_columns(first_cell, clusters)
    second = on_columns(second_cell, clusters)
    denom = cluster_counts(first, second)
    grad_mean = (dot(pool_t_ref[...], pool_grad_ref[...]) / denom).astype(BF16)
    blank = jnp.zeros_like(grad_mean)
    back = dot_nt(first, jnp.concatenate([grad_mean, blank], axis=0))
    back = back + dot_nt(second, jnp.concatenate([blank, grad_mean], axis=0))
    per_peer = length // shards
    out_ref[:, per_peer:, :] = back.astype(BF16).reshape(shards, per_peer, 2 * CHANNELS)
    turned_rows = turned(arrived)[:CHANNELS].astype(BF16)
    floats = dot(turned_rows, on_columns(place, length))
    hilbert_ref[...] = floats.astype(BF16)
    _, _, hidden = layer_norm(floats, gain_column(gain_ref))
    qkv = dot_tn(qkv_t_ref[...], hidden).astype(BF16)
    query_ref[...] = (turned(qkv[:CHANNELS]) * HEAD_DIM ** (-0.5)).astype(BF16)
    key_ref[...] = qkv[CHANNELS : 2 * CHANNELS]
    values = turned(qkv[2 * CHANNELS :])
    for head in range(HEADS):
        mask = head_lanes((length, CHANNELS), head)
        value_ref[head] = jnp.where(mask, values, 0.0).astype(BF16)

    def one_chunk(index, carry):
        rows = pl.ds(pl.multiple_of(index * CHUNK, CHUNK), CHUNK)
        queries = query_ref[rows, :].astype(F32)
        total = jnp.zeros((CHUNK, CHANNELS), F32)
        for head in range(HEADS):
            mask = head_lanes((CHUNK, CHANNELS), head)
            mine = jnp.where(mask, queries, 0.0).astype(BF16)
            weights = jnp.exp(dot(mine, key_ref[...]))
            share = 1.0 / jnp.sum(weights, axis=1, keepdims=True)
            probs = (weights * share).astype(BF16)
            probs_ref[head, rows, :] = probs
            total = total + dot(probs, value_ref[head])
        rows_ref[rows, :] = total
        return carry

    lax.fori_loop(0, length // CHUNK, one_chunk, 0)
    attended = rows_ref[...].T
    attended_ref[...] = attended
    mixed = (floats + dot(out_w_ref[...], attended.astype(BF16))).astype(BF16).astype(F32)
    o_slot = o_slot_ref[...]
    odd = lax.bitwise_and(o_slot, 1) == 1
    pair = jnp.concatenate([jnp.where(odd, 0.0, mixed), jnp.where(odd, mixed, 0.0)], axis=0)
    picked = dot_nt(on_rows(lax.shift_right_logical(o_slot, 1), length), pair.astype(BF16))
    out_ref[:, :per_peer, :] = picked.astype(BF16).reshape(shards, per_peer, 2 * CHANNELS)


def backward_kernel(
    returned_ref,
    arrived_ref,
    o_slot_ref,
    qkv_t_ref,
    out_w_ref,
    pool_t_ref,
    gain_ref,
    pool_grad_ref,
    hilbert_ref,
    attended_ref,
    probs_ref,
    out_ref,
    pooled_ref,
    key_rows_ref,
    upstream_ref,
    value_ref,
    query_ref,
    grad_out_ref,
    grad_query_ref,
    grad_key_ref,
    grad_value_ref,
):
    shards = out_ref.shape[0]
    length = arrived_ref.shape[0]
    clusters = pool_grad_ref.shape[1]
    per_peer = length // shards
    place, first_cell, second_cell = arrived_columns(arrived_ref[...])
    blank = jnp.zeros((CHANNELS, length), BF16)
    blank_clusters = jnp.zeros((CHANNELS, clusters), BF16)

    first = on_columns(first_cell, clusters)
    second = on_columns(second_cell, clusters)
    denom = cluster_counts(first, second)
    mixed_rows = turned(returned_ref[:, :per_peer, :].reshape(length, 2 * CHANNELS)).astype(BF16)
    sums = dot(mixed_rows[:CHANNELS], first) + dot(mixed_rows[CHANNELS:], second)
    pooled_mean = (sums / denom).astype(BF16)
    pooled_ref[...] = dot_tn(pool_t_ref[...], pooled_mean).astype(BF16)
    pool_grad = pool_grad_ref[...]
    pool_parts = [
        dot_nt(pooled_mean, jnp.concatenate([blank_clusters, pool_grad[start : start + CHANNELS]], axis=0))
        for start in (0, CHANNELS)
    ]

    gain = gain_column(gain_ref)
    normed, inverse_std, hidden = layer_norm(hilbert_ref[...].astype(F32), gain)
    qkv = dot_tn(qkv_t_ref[...], hidden).astype(BF16)
    query_ref[...] = qkv[:CHANNELS]
    key_rows = turned(qkv[CHANNELS : 2 * CHANNELS])
    for head in range(HEADS):
        mask = head_lanes((length, CHANNELS), head)
        key_rows_ref[head] = jnp.where(mask, key_rows, 0.0).astype(BF16)
    value_ref[:CHANNELS, :] = qkv[2 * CHANNELS :]
    value_ref[CHANNELS:, :] = jnp.ones((CHANNELS, length), BF16)

    o_slot = o_slot_ref[...]
    odd = lax.bitwise_and(o_slot, 1) == 1
    slots = turned(returned_ref[:, per_peer:, :].reshape(length, 2 * CHANNELS)).astype(BF16)
    both = dot(slots, on_rows(lax.shift_right_logical(o_slot, 1), length))
    grad_mixed = jnp.where(odd, both[CHANNELS:], both[:CHANNELS])
    grad_mixed_low = grad_mixed.astype(BF16)
    attended = attended_ref[...]
    attended_low = attended.astype(BF16)
    out_part = dot_nt(grad_mixed_low, jnp.concatenate([blank, attended_low], axis=0))
    grad_attended = dot_tn(out_w_ref[...], grad_mixed_low).astype(BF16)
    grad_out_ref[...] = grad_attended
    scaled = grad_attended.astype(F32) * HEAD_DIM ** (-0.5)
    delta = -jnp.sum((scaled * attended).reshape(HEADS, HEAD_DIM, length), axis=1)
    delta_high = delta.astype(BF16).astype(F32)
    rest = jnp.concatenate(
        [delta_high, delta - delta_high, jnp.zeros((CHANNELS - 2 * HEADS, length), F32)], axis=0
    )
    upstream_ref[...] = jnp.concatenate([scaled, rest], axis=0).T.astype(BF16)
    grad_key_ref[...] = jnp.zeros_like(grad_key_ref)
    grad_value_ref[...] = jnp.zeros_like(grad_value_ref)

    def one_chunk(index, carry):
        rows = pl.ds(pl.multiple_of(index * CHUNK, CHUNK), CHUNK)
        upstream = upstream_ref[rows, :].astype(F32)
        total = jnp.zeros((CHUNK, CHANNELS), F32)
        lane = iota((CHUNK, 2 * CHANNELS), 1)
        for head in range(HEADS):
            own = slice(head * HEAD_DIM, (head + 1) * HEAD_DIM)
            mask = (
                (lax.shift_right_logical(lane, 4) == head)
                | (lane == CHANNELS + head)
                | (lane == CHANNELS + HEADS + head)
            )
            mine = jnp.where(mask, upstream, 0.0).astype(BF16)
            probs = probs_ref[head, rows, :]
            grad_value_ref[own, :] += dot(grad_out_ref[own, rows], probs)
            change = dot(mine, value_ref[...])
            grad_scores = (probs.astype(F32) * change).astype(BF16)
            total = total + dot(grad_scores, key_rows_ref[head])
            grad_key_ref[own, :] += dot(query_ref[own, rows], grad_scores)
        grad_query_ref[rows, :] = total
        return carry

    lax.fori_loop(0, length // CHUNK, one_chunk, 0)
    grad_qkv = jnp.concatenate(
        [grad_query_ref[...].T, grad_key_ref[...], grad_value_ref[...]], axis=0
    ).astype(BF16)
    qkv_parts = [
        dot_nt(hidden, jnp.concatenate([blank, grad_qkv[start : start + CHANNELS]], axis=0))
        for start in (0, CHANNELS, 2 * CHANNELS)
    ]
    grad_hidden = dot(qkv_t_ref[...], grad_qkv)
    grad_gain = jnp.sum(grad_hidden * normed, axis=1, keepdims=True)
    grad_normed = grad_hidden * gain
    grad_norm_in = inverse_std * (
        grad_normed
        - jnp.mean(grad_normed, axis=0, keepdims=True)
        - normed * jnp.mean(grad_normed * normed, axis=0, keepdims=True)
    )
    grad_rows = (grad_mixed + grad_norm_in).astype(BF16)
    eye = iota((CHANNELS, 2 * CHANNELS), 0) + CHANNELS == iota((CHANNELS, 2 * CHANNELS), 1)
    gain_row = jnp.sum(jnp.where(eye, grad_gain, 0.0), axis=0, keepdims=True)
    back = dot_nt(on_columns(place, length), jnp.concatenate([grad_rows, blank], axis=0))
    parts = jnp.concatenate(qkv_parts + [out_part] + pool_parts, axis=0)
    high = parts.astype(BF16).astype(F32)
    gain_high = gain_row.astype(BF16).astype(F32)
    row = iota((8, 2 * CHANNELS), 0)
    gain_rows = jnp.where(row == 0, gain_high, jnp.where(row == 1, gain_row - gain_high, 0.0))
    count = parts.shape[0]
    used = 2 * count + 8
    side = jnp.concatenate(
        [high, parts - high, gain_rows, jnp.zeros((length - used, 2 * CHANNELS), F32)], axis=0
    )
    out_ref[...] = (back + side).astype(BF16).reshape(out_ref.shape)


def total_kernel(arrived_ref, out_ref):
    shards, per_peer, lanes = arrived_ref.shape
    total = jnp.sum(arrived_ref[...].astype(F32), axis=0)
    high = total.astype(BF16).astype(F32)
    low = pltpu.roll(total - high, CHANNELS, 1)
    chosen = jnp.where(iota((per_peer, lanes), 1) >= CHANNELS, high, low)
    out_ref[...] = jnp.broadcast_to(chosen[None], (shards, per_peer, lanes)).astype(BF16)


def feat_grad_kernel(arrived_ref, z_slot_ref, out_ref):
    length = arrived_ref.shape[0]
    rows = turned(arrived_ref[...])[:CHANNELS].astype(BF16)
    out_ref[...] = dot(rows, on_rows(z_slot_ref[...], length)).astype(BF16)


def finish_kernel(factor, own_ref, other_ref, qkv_ref, out_ref, pool_ref, gain_ref):
    both = own_ref[...].astype(F32) + other_ref[...].astype(F32)
    count = 6 * CHANNELS
    halves = both[:count] + both[count : 2 * count]
    halves = (halves[:, CHANNELS:] + halves[:, :CHANNELS]) * factor
    piece = [halves[k * CHANNELS : (k + 1) * CHANNELS] for k in range(6)]
    qkv_ref[...] = jnp.concatenate(piece[:3], axis=1)
    out_ref[...] = piece[3]
    pool_ref[...] = jnp.concatenate(piece[4:], axis=1)
    gain = both[2 * count : 2 * count + 1] + both[2 * count + 1 : 2 * count + 2]
    gain_ref[...] = (gain[:, CHANNELS:] + gain[:, :CHANNELS]) * factor


def shape(dims, dtype):
    return jax.ShapeDtypeStruct(dims, dtype)


def call(kernel, outs, scratch=(), flops=0):
    return pl.pallas_call(
        kernel,
        out_shape=outs,
        scratch_shapes=list(scratch),
        compiler_params=pltpu.CompilerParams(vmem_limit_bytes=48 * 1024 * 1024),
        cost_estimate=pl.CostEstimate(flops=flops, bytes_accessed=1 << 20, transcendentals=0),
    )


def exchange(blocks):
    return lax.all_to_all(blocks, "pts", split_axis=0, concat_axis=0, tiled=True)


def body(
    feats,
    hilbert_of_z,
    pool_owner,
    pool_slot,
    qkv_weight,
    out_weight,
    pool_weight,
    norm_gain,
    pooled_grad,
):
    length = feats.shape[2]
    shards = lax.axis_size("pts")
    per_peer = length // shards
    clusters = pooled_grad.shape[2]
    lanes = 2 * CHANNELS
    qkv_t = qkv_weight.T
    pool_t = pool_weight.T
    gain = norm_gain.reshape(1, CHANNELS)
    upstream_pool = pooled_grad[0]

    outgoing, z_slot, o_slot = call(
        send_kernel,
        (
            shape((shards, per_peer, lanes), BF16),
            shape((1, length), I32),
            shape((1, length), I32),
        ),
        flops=1 << 30,
    )(hilbert_of_z, pool_owner.reshape(1, length), pool_slot, feats[0])
    arrived = exchange(outgoing).reshape(length, lanes)

    both_ways, hilbert_rows, attended, probs = call(
        forward_kernel,
        (
            shape((shards, 2 * per_peer, lanes), BF16),
            shape((CHANNELS, length), BF16),
            shape((CHANNELS, length), F32),
            shape((HEADS, length, length), BF16),
        ),
        scratch=(
            pltpu.VMEM((length, CHANNELS), BF16),
            pltpu.VMEM((CHANNELS, length), BF16),
            pltpu.VMEM((HEADS, length, CHANNELS), BF16),
            pltpu.VMEM((length, CHANNELS), F32),
        ),
        flops=1 << 32,
    )(arrived, o_slot, qkv_t, out_weight, pool_t, gain, upstream_pool)
    returned = exchange(both_ways)

    last, pooled = call(
        backward_kernel,
        (shape((shards, per_peer, lanes), BF16), shape((2 * CHANNELS, clusters), BF16)),
        scratch=(
            pltpu.VMEM((HEADS, length, CHANNELS), BF16),
            pltpu.VMEM((length, lanes), BF16),
            pltpu.VMEM((lanes, length), BF16),
            pltpu.VMEM((CHANNELS, length), BF16),
            pltpu.VMEM((CHANNELS, length), BF16),
            pltpu.VMEM((length, CHANNELS), F32),
            pltpu.VMEM((CHANNELS, length), F32),
            pltpu.VMEM((CHANNELS, length), F32),
        ),
        flops=1 << 33,
    )(
        returned,
        arrived,
        o_slot,
        qkv_t,
        out_weight,
        pool_t,
        gain,
        upstream_pool,
        hilbert_rows,
        attended,
        probs,
    )
    final = exchange(last)

    chunk = call(total_kernel, shape((shards, per_peer, lanes), BF16))(final)
    gathered = exchange(chunk).reshape(length, lanes)
    feat_grad = call(feat_grad_kernel, shape((CHANNELS, length), BF16), flops=1 << 28)(
        final.reshape(length, lanes), z_slot
    )
    other = lax.ppermute(gathered, "rep", [(0, 1), (1, 0)])
    factor = float(lax.axis_size("rep") * shards * length) ** (-0.5)
    qkv_total, out_total, pool_total, gain_total = call(
        functools.partial(finish_kernel, factor),
        (
            shape((CHANNELS, 3 * CHANNELS), F32),
            shape((CHANNELS, CHANNELS), F32),
            shape((CHANNELS, lanes), F32),
            shape((1, CHANNELS), F32),
        ),
    )(gathered, other)
    return (
        pooled[None],
        feat_grad[None],
        qkv_total.T,
        out_total,
        pool_total.T,
        gain_total.reshape(CHANNELS),
    )


def solution(mesh):
    return jax.shard_map(
        body,
        mesh=mesh,
        in_specs=(
            P("rep", None, "pts"),
            P("rep", "pts"),
            P("rep", "pts", None),
            P("rep", "pts"),
            P(),
            P(),
            P(),
            P(),
            P("rep", None, "pts"),
        ),
        out_specs=(P("rep", None, "pts"), P("rep", None, "pts"), P(), P(), P(), P()),
        check_vma=False,
    )
```

time: 509 us -> 134 us (0.26)
  waiting for transfers between devices: 257 us -> 0.01 us
  local copies, waits for them, and re-layouts: 99.1 us -> 6.65 us
  blocking collectives: 0 us -> 90.9 us
  starting transfers between devices: 70.9 us -> 4.89 us
  other arithmetic: 39.9 us -> 0 us
  Pallas kernels: 0 us -> 30 us
  matrix products: 26.2 us -> 0 us
  between operations: 14.8 us -> 0.67 us
    psum x1 -> x0, waiting for transfers between devices: 238 us -> none  [body(): lax.psum((grad_qkv_weight, grad_gain), ('pts', 'rep'))]
    all_to_all x0 -> x4, blocking collectives: none -> 90.9 us  [exchange(): lax.all_to_all(blocks, 'pts', split_axis=0, concat_axis=0, tiled=True)]
    gather x21 -> x0, local copies, waits for them, and re-layouts: 87.1 us -> none  [the longest x3 12.8 us: body(): filled = buffer_rank < owner_counts[buffer_owner]]
    all_to_all x6 -> x0, starting transfers between devices: 70.9 us -> none  [the longest x1 16.3 us: body(): lax.all_to_all(outgoing_pos, 'pts', split_axis=0, concat_axis=0, tiled=True)]
    pallas_call x0 -> x6, Pallas kernels: none -> 30 us  [the longest x1 13.7 us: body(): call(backward_kernel, (shape((shards, per_peer, lanes), BF16), shape((2 *...]
    dot_general x38 -> x0, matrix products: 26.2 us -> none  [the longest x8 6.56 us: probabilities(): jnp.dot(queries.T, key_rows, preferred_element_type=jnp.float32)]
    sort x5 -> x0, other arithmetic: 22.5 us -> none  [the longest x1 5.07 us: body(): sort_order = jnp.argsort(positions)]
    all_to_all x6 -> x0, waiting for transfers between devices: 18.9 us -> none  [the longest x1 7.51 us: body(): lax.all_to_all(pack_blocks(grad_rows[:, arrived_flat], shard_count), 'pts...]
  transfers between devices with their start and end apart: 7 -> 1, of which waited for: 4 -> 0; matrix products, arithmetic and copies ran while one was open for 29% -> 0% of each run, Pallas kernels for 0% -> 1%
where the time goes in v1:
time: 134 us; the launch traced here: 133 us
  blocking collectives  90.9 us (68%)
  Pallas kernels  30 us (22%)
  local copies, waits for them, and re-layouts  6.65 us (5%)
  starting transfers between devices  4.89 us (4%)
    all_to_all x4, blocking collectives, exchange(): lax.all_to_all(blocks, 'pts', split_axis=0, concat_axis=0, tiled=True)  90.9 us
    pallas_call x1, Pallas kernels, body(): call(backward_kernel, (shape((shards, per_peer, lanes), BF16), shape((2 *...  13.7 us
    pallas_call x1, Pallas kernels, body(): call(forward_kernel, (shape((shards, 2 * per_peer, lanes), BF16), shape((...  12 us
    unnamed x22, local copies, waits for them, and re-layouts  6.65 us
    ppermute x1, starting transfers between devices, body(): other = lax.ppermute(gathered, 'rep', [(0, 1), (1, 0)])  4.89 us
  transfers between devices with their start and end apart: 1, of which 0 were waited for; matrix products, arithmetic and copies ran while one was open for 0% of the time, Pallas kernels for 1%

profile of v1, /device:TPU:1, one launch (start us, length us, event | category | flops | bytes accessed | tf_op | source)
XLA Modules:
  0.0 133.2 jit_solution(2562310573043865044)
XLA Ops:
  0.6 0.0 copy-start
  0.6 0.9 copy-done
  1.5 0.0 copy-start.7
  1.5 0.7 copy-done.7
  2.2 0.0 copy-start.8
  2.2 0.7 copy-done.8
  2.9 0.0 copy-start.9
  2.9 0.7 copy-done.9
  3.6 2.0 %shard_map.136 = (bf16[128,8,128]{2,1,0:T(8,128)(2,1)S(1)}, s32[1,1024]{1,0:T(1,128)S(1)}, s32[1,1024]{1,0:T(1,128)S(1)}) custom-call(s32[1,1024]{1,0:T(1,128)S(1)} %copy-done.7, s32[1,1024]{1,0:T(1,128)S(1)} %bitcast.26, s32[1,1024]{1,0:T(1,128)S(1)} %copy-done.9, bf16[64,1024]{1,0:T(8,128)(2,1)S(1)} %bitcast.19), custom_call_target="tpu_custom_call" | custom-call | flops 1073741824 | bytes 1048576 | tf_op jit(solution)/shard_map/pallas_call | solution.py:390
  5.6 29.4 %all_to_all.20 = bf16[128,8,128]{2,1,0:T(8,128)(2,1)S(1)} all-to-all(bf16[128,8,128]{2,1,0:T(8,128)(2,1)S(1)} %get-tuple-element.19), channel_id=1, replica_groups=mesh['pts'=128,'rep'=2] {'pts'}, dimensions={0} | all-to-all | bytes 524288 | tf_op jit(solution)/shard_map/all_to_all | solution.py:366
  35.0 0.0 copy-start.1
  35.0 0.8 copy-done.1
  35.8 0.0 copy-start.3
  35.8 0.8 copy-done.3
  36.6 0.0 copy-start.5
  36.6 0.7 copy-done.5
  37.3 0.0 copy-start.6
  37.3 0.7 copy-done.6
  38.0 0.0 copy-start.10
  38.0 0.7 copy-done.10
  38.7 0.0 copy-start.2
  38.7 0.0 copy-start.4
  38.7 12.0 %shard_map.137 = (bf16[128,16,128]{2,1,0:T(8,128)(2,1)S(1)}, bf16[64,1024]{1,0:T(8,128)(2,1)S(1)}, f32[64,1024]{1,0:T(8,128)S(1)}, bf16[4,1024,1024]{2,1,0:T(8,128)(2,1)}) custom-call(bf16[1024,128]{1,0:T(8,128)(2,1)S(1)} %bitcast.17, s32[1,1024]{1,0:T(1,128)S(1)} %get-tuple-element.20.o_slot_ref, bf16[64,192]{1,0:T(8,128)(2,1)S(1)} %bitcast.22, ...), custom_call_target="tpu_custom_call" | custom-call | flops 4294967296 | bytes 1048576 | tf_op jit(solution)/shard_map/pallas_call | solution.py:401
  50.7 23.5 %all_to_all.21.returned_ref = bf16[128,16,128]{2,1,0:T(8,128)(2,1)S(1)} all-to-all(bf16[128,16,128]{2,1,0:T(8,128)(2,1)S(1)} %get-tuple-element.21), channel_id=1, replica_groups=mesh['pts'=128,'rep'=2] {'pts'}, dimensions={0} | all-to-all | bytes 1048576 | tf_op jit(solution)/shard_map/all_to_all | solution.py:366
  74.2 0.0 copy-done.2
  74.2 0.0 copy-done.4
  74.2 13.7 %shard_map.138 = (bf16[128,8,128]{2,1,0:T(8,128)(2,1)S(1)}, bf16[128,256]{1,0:T(8,128)(2,1)}) custom-call(bf16[128,16,128]{2,1,0:T(8,128)(2,1)S(1)} %all_to_all.21.returned_ref, bf16[1024,128]{1,0:T(8,128)(2,1)S(1)} %bitcast.18, s32[1,1024]{1,0:T(1,128)S(1)} %get-tuple-element.20.o_slot_ref, bf16[64,192]{1,0:T(8,128)(2,1)S(1)} %bitcast.23, ...), custom_call_target="tpu_custom_call" | custom-call | flops 8589934592 | bytes 1048576 | tf_op jit(solution)/shard_map/pallas_call | solution.py:419
  87.9 19.9 %all_to_all.22.arrived_ref = bf16[128,8,128]{2,1,0:T(8,128)(2,1)S(1)} all-to-all(bf16[128,8,128]{2,1,0:T(8,128)(2,1)S(1)} %get-tuple-element.26), channel_id=1, replica_groups=mesh['pts'=128,'rep'=2] {'pts'}, dimensions={0} | all-to-all | bytes 524288 | tf_op jit(solution)/shard_map/all_to_all | solution.py:366
  107.8 0.2 shard_map.140
  108.1 18.1 %all_to_all.23 = bf16[128,8,128]{2,1,0:T(8,128)(2,1)S(1)} all-to-all(bf16[128,8,128]{2,1,0:T(8,128)(2,1)S(1)} %shard_map.140), channel_id=1, replica_groups=mesh['pts'=128,'rep'=2] {'pts'}, dimensions={0} | all-to-all | bytes 524288 | tf_op jit(solution)/shard_map/all_to_all | solution.py:366
  126.2 4.9 %collective-permute-start = (bf16[1024,128]{1,0:T(8,128)(2,1)S(1)}, bf16[1024,128]{1,0:T(8,128)(2,1)S(1)}, u32[]{:S(2)}, u32[]{:S(2)}) collective-permute-start(bf16[1024,128]{1,0:T(8,128)(2,1)S(1)} %bitcast.14), channel_id=1, source_target_pairs={{0,1},{1,0},{2,3},{3,2},{4,5},{5,4},{6,7},{7,6},{8,9},{9,8},{10,11... | collective-permute-start | bytes 786440 | tf_op jit(solution)/shard_map/ppermute | solution.py:453
  131.1 1.2 shard_map.139
  132.3 0.0 collective-permute-done.other_ref
  132.3 0.8 shard_map.141
Async XLA Ops:
  0.6 0.9 copy-start
  1.5 0.7 copy-start.7
  2.2 0.7 copy-start.8
  2.9 0.7 copy-start.9
  35.0 0.8 copy-start.1
  35.8 0.8 copy-start.3
  36.6 0.7 copy-start.5
  37.3 0.7 copy-start.6
  38.0 0.7 copy-start.10
  38.7 35.5 %copy-start.2 = (bf16[1,128,256]{2,1,0:T(8,128)(2,1)S(1)}, bf16[1,128,256]{2,1,0:T(8,128)(2,1)}, u32[]{:S(2)}) copy-start(bf16[1,128,256]{2,1,0:T(8,128)(2,1)} %param.17) | copy-start | bytes 196612
  38.7 35.5 %copy-start.4 = (bf16[192,64]{0,1:T(8,128)(2,1)S(1)}, bf16[192,64]{0,1:T(8,128)(2,1)}, u32[]{:S(2)}) copy-start(bf16[192,64]{0,1:T(8,128)(2,1)} %param.13) | copy-start | bytes 73732
  126.2 6.1 %collective-permute-start = (bf16[1024,128]{1,0:T(8,128)(2,1)S(1)}, bf16[1024,128]{1,0:T(8,128)(2,1)S(1)}, u32[]{:S(2)}, u32[]{:S(2)}) collective-permute-start(bf16[1024,128]{1,0:T(8,128)(2,1)S(1)} %bitcast.14), channel_id=1, source_target_pairs={{0,1},{1,0},{2,3},{3,2},{4,5},{5,4},{6,7},{7,6},{8,9},{9,8},{10,11... | collective-permute-start | bytes 786440 | tf_op jit(solution)/shard_map/ppermute | solution.py:453

commit v2 on v1

--- a/solution.py
+++ b/solution.py
@@ -12,6 +12,7 @@
 CHANNELS = 64
 NORM_EPS = 1e-05
 CHUNK = 256
+PLANE = 16
 
 F32 = jnp.float32
 BF16 = jnp.bfloat16
@@ -64,7 +65,50 @@
     return jnp.concatenate(ranks, axis=1).astype(I32)
 
 
-def send_kernel(pos_ref, owner_ref, cell_ref, feats_ref, out_ref, z_slot_ref, o_slot_ref):
+def send_kernel(
+    pos_hbm,
+    owner_hbm,
+    cell_hbm,
+    feats_hbm,
+    pool_grad_hbm,
+    qkv_t_hbm,
+    out_w_hbm,
+    pool_t_hbm,
+    gain_hbm,
+    out_ref,
+    z_slot_ref,
+    o_slot_ref,
+    pool_grad_ref,
+    qkv_t_ref,
+    out_w_ref,
+    pool_t_ref,
+    gain_ref,
+    pos_ref,
+    owner_ref,
+    cell_ref,
+    feats_ref,
+    sems,
+):
+    loads = [
+        pltpu.make_async_copy(source, target, sems.at[number])
+        for number, (source, target) in enumerate(
+            (
+                (pos_hbm, pos_ref),
+                (owner_hbm, owner_ref),
+                (cell_hbm, cell_ref),
+                (feats_hbm, feats_ref),
+                (pool_grad_hbm, pool_grad_ref),
+                (qkv_t_hbm, qkv_t_ref),
+                (out_w_hbm, out_w_ref),
+                (pool_t_hbm, pool_t_ref),
+                (gain_hbm, gain_ref),
+            )
+        )
+    ]
+    for load in loads:
+        load.start()
+    for load in loads[:3]:
+        load.wait()
     length = pos_ref.shape[1]
     shards = out_ref.shape[0]
     per_peer = length // shards
@@ -84,11 +128,14 @@
     cell = (cell_ref[...] + 1).astype(F32)
     odd = lax.bitwise_and(o_slot, 1)
     cells = jnp.where(row - 2 == odd, cell, 0.0).astype(BF16)
+    loads[3].wait()
     first = jnp.concatenate([feats_ref[...], place], axis=0)
     second = jnp.concatenate([jnp.zeros((CHANNELS, length), BF16), cells], axis=0)
     out = dot_nt(on_rows(z_slot, length), first)
     out = out + dot_nt(on_rows(lax.shift_right_logical(o_slot, 1), length), second)
     out_ref[...] = out.astype(BF16).reshape(out_ref.shape)
+    for load in loads[4:]:
+        load.wait()
 
 
 def arrived_columns(arrived):
@@ -218,7 +265,6 @@
     per_peer = length // shards
     place, first_cell, second_cell = arrived_columns(arrived_ref[...])
     blank = jnp.zeros((CHANNELS, length), BF16)
-    blank_clusters = jnp.zeros((CHANNELS, clusters), BF16)
 
     first = on_columns(first_cell, clusters)
     second = on_columns(second_cell, clusters)
@@ -227,11 +273,7 @@
     sums = dot(mixed_rows[:CHANNELS], first) + dot(mixed_rows[CHANNELS:], second)
     pooled_mean = (sums / denom).astype(BF16)
     pooled_ref[...] = dot_tn(pool_t_ref[...], pooled_mean).astype(BF16)
-    pool_grad = pool_grad_ref[...]
-    pool_parts = [
-        dot_nt(pooled_mean, jnp.concatenate([blank_clusters, pool_grad[start : start + CHANNELS]], axis=0))
-        for start in (0, CHANNELS)
-    ]
+    pool_part = dot_nt(pooled_mean, pool_grad_ref[...])
 
     gain = gain_column(gain_ref)
     normed, inverse_std, hidden = layer_norm(hilbert_ref[...].astype(F32), gain)
@@ -291,12 +333,9 @@
     grad_qkv = jnp.concatenate(
         [grad_query_ref[...].T, grad_key_ref[...], grad_value_ref[...]], axis=0
     ).astype(BF16)
-    qkv_parts = [
-        dot_nt(hidden, jnp.concatenate([blank, grad_qkv[start : start + CHANNELS]], axis=0))
-        for start in (0, CHANNELS, 2 * CHANNELS)
-    ]
+    query_key_part = dot_nt(hidden, grad_qkv[: 2 * CHANNELS])
+    value_part = dot_nt(hidden, jnp.concatenate([blank, grad_qkv[2 * CHANNELS :]], axis=0))
     grad_hidden = dot(qkv_t_ref[...], grad_qkv)
-    grad_gain = jnp.sum(grad_hidden * normed, axis=1, keepdims=True)
     grad_normed = grad_hidden * gain
     grad_norm_in = inverse_std * (
         grad_normed
@@ -304,58 +343,52 @@
         - normed * jnp.mean(grad_normed * normed, axis=0, keepdims=True)
     )
     grad_rows = (grad_mixed + grad_norm_in).astype(BF16)
-    eye = iota((CHANNELS, 2 * CHANNELS), 0) + CHANNELS == iota((CHANNELS, 2 * CHANNELS), 1)
-    gain_row = jnp.sum(jnp.where(eye, grad_gain, 0.0), axis=0, keepdims=True)
     back = dot_nt(on_columns(place, length), jnp.concatenate([grad_rows, blank], axis=0))
-    parts = jnp.concatenate(qkv_parts + [out_part] + pool_parts, axis=0)
-    high = parts.astype(BF16).astype(F32)
-    gain_high = gain_row.astype(BF16).astype(F32)
-    row = iota((8, 2 * CHANNELS), 0)
-    gain_rows = jnp.where(row == 0, gain_high, jnp.where(row == 1, gain_row - gain_high, 0.0))
-    count = parts.shape[0]
-    used = 2 * count + 8
-    side = jnp.concatenate(
-        [high, parts - high, gain_rows, jnp.zeros((length - used, 2 * CHANNELS), F32)], axis=0
-    )
-    out_ref[...] = (back + side).astype(BF16).reshape(out_ref.shape)
+    beside = jnp.concatenate([value_part, out_part], axis=0)
+    below = jnp.concatenate([query_key_part, pool_part], axis=0).astype(BF16)
+    below = below.reshape(PLANE, per_peer, 2 * CHANNELS)
+    span = PLANE * per_peer
+    for start in range(0, shards, PLANE):
+        rows = back[start * per_peer : start * per_peer + span] + beside
+        out_ref[start : start + PLANE, :per_peer, :] = rows.astype(BF16).reshape(below.shape)
+        out_ref[start : start + PLANE, per_peer:, :] = below
 
 
 def total_kernel(arrived_ref, out_ref):
-    shards, per_peer, lanes = arrived_ref.shape
-    total = jnp.sum(arrived_ref[...].astype(F32), axis=0)
-    high = total.astype(BF16).astype(F32)
-    low = pltpu.roll(total - high, CHANNELS, 1)
-    chosen = jnp.where(iota((per_peer, lanes), 1) >= CHANNELS, high, low)
-    out_ref[...] = jnp.broadcast_to(chosen[None], (shards, per_peer, lanes)).astype(BF16)
+    out_ref[...] = jnp.sum(arrived_ref[...].astype(F32), axis=0)
 
 
 def feat_grad_kernel(arrived_ref, z_slot_ref, out_ref):
-    length = arrived_ref.shape[0]
-    rows = turned(arrived_ref[...])[:CHANNELS].astype(BF16)
+    shards, rows_per_peer, lanes = arrived_ref.shape
+    length = shards * rows_per_peer // 2
+    arrived = arrived_ref[:, : rows_per_peer // 2, :].reshape(length, lanes)
+    rows = turned(arrived)[:CHANNELS].astype(BF16)
     out_ref[...] = dot(rows, on_rows(z_slot_ref[...], length)).astype(BF16)
 
 
-def finish_kernel(factor, own_ref, other_ref, qkv_ref, out_ref, pool_ref, gain_ref):
-    both = own_ref[...].astype(F32) + other_ref[...].astype(F32)
-    count = 6 * CHANNELS
-    halves = both[:count] + both[count : 2 * count]
-    halves = (halves[:, CHANNELS:] + halves[:, :CHANNELS]) * factor
-    piece = [halves[k * CHANNELS : (k + 1) * CHANNELS] for k in range(6)]
-    qkv_ref[...] = jnp.concatenate(piece[:3], axis=1)
-    out_ref[...] = piece[3]
-    pool_ref[...] = jnp.concatenate(piece[4:], axis=1)
-    gain = both[2 * count : 2 * count + 1] + both[2 * count + 1 : 2 * count + 2]
-    gain_ref[...] = (gain[:, CHANNELS:] + gain[:, :CHANNELS]) * factor
+def finish_kernel(factor, total_ref, qkv_t_ref, gain_in_ref, qkv_ref, out_ref, pool_ref, gain_ref):
+    chunks, rows, lanes = total_ref.shape
+    half = rows // 2
+    beside = total_ref[:, :half, :].reshape(chunks * half, lanes)[:, CHANNELS:] * factor
+    below = total_ref[:, half:, :].reshape(chunks * half, lanes) * factor
+    qkv = jnp.concatenate([below[:CHANNELS], beside[:CHANNELS]], axis=1)
+    qkv_ref[...] = qkv
+    out_ref[...] = beside[CHANNELS:]
+    pool_ref[...] = below[CHANNELS:]
+    column = jnp.sum(qkv * qkv_t_ref[...].astype(F32), axis=1, keepdims=True)
+    eye = iota((CHANNELS, CHANNELS), 0) == iota((CHANNELS, CHANNELS), 1)
+    gain_ref[...] = jnp.sum(jnp.where(eye, column, 0.0), axis=0, keepdims=True) / gain_in_ref[...]
 
 
 def shape(dims, dtype):
     return jax.ShapeDtypeStruct(dims, dtype)
 
 
-def call(kernel, outs, scratch=(), flops=0):
+def call(kernel, outs, scratch=(), flops=0, **more):
     return pl.pallas_call(
         kernel,
         out_shape=outs,
+        **more,
         scratch_shapes=list(scratch),
         compiler_params=pltpu.CompilerParams(vmem_limit_bytes=48 * 1024 * 1024),
         cost_estimate=pl.CostEstimate(flops=flops, bytes_accessed=1 << 20, transcendentals=0),
@@ -387,15 +420,30 @@
     gain = norm_gain.reshape(1, CHANNELS)
     upstream_pool = pooled_grad[0]
 
-    outgoing, z_slot, o_slot = call(
+    arguments = (
+        hilbert_of_z,
+        pool_owner.reshape(1, length),
+        pool_slot,
+        feats[0],
+        upstream_pool,
+        qkv_t,
+        out_weight,
+        pool_t,
+        gain,
+    )
+    outgoing, z_slot, o_slot, upstream_pool, qkv_t, out_weight, pool_t, gain = call(
         send_kernel,
         (
             shape((shards, per_peer, lanes), BF16),
             shape((1, length), I32),
             shape((1, length), I32),
-        ),
+        )
+        + tuple(shape(one.shape, one.dtype) for one in arguments[4:]),
+        scratch=tuple(pltpu.VMEM(one.shape, one.dtype) for one in arguments[:4])
+        + (pltpu.SemaphoreType.DMA((len(arguments),)),),
         flops=1 << 30,
-    )(hilbert_of_z, pool_owner.reshape(1, length), pool_slot, feats[0])
+        in_specs=[pl.BlockSpec(memory_space=pltpu.HBM)] * len(arguments),
+    )(*arguments)
     arrived = exchange(outgoing).reshape(length, lanes)
 
     both_ways, hilbert_rows, attended, probs = call(
@@ -418,7 +466,7 @@
 
     last, pooled = call(
         backward_kernel,
-        (shape((shards, per_peer, lanes), BF16), shape((2 * CHANNELS, clusters), BF16)),
+        (shape((shards, 2 * per_peer, lanes), BF16), shape((2 * CHANNELS, clusters), BF16)),
         scratch=(
             pltpu.VMEM((HEADS, length, CHANNELS), BF16),
             pltpu.VMEM((length, lanes), BF16),
@@ -445,12 +493,22 @@
     )
     final = exchange(last)
 
-    chunk = call(total_kernel, shape((shards, per_peer, lanes), BF16))(final)
-    gathered = exchange(chunk).reshape(length, lanes)
+    own = call(total_kernel, shape((2 * per_peer, lanes), F32))(final)
+    other = lax.ppermute(own, "rep", [(0, 1), (1, 0)])
     feat_grad = call(feat_grad_kernel, shape((CHANNELS, length), BF16), flops=1 << 28)(
-        final.reshape(length, lanes), z_slot
-    )
-    other = lax.ppermute(gathered, "rep", [(0, 1), (1, 0)])
+        final, z_slot
+    )
+    total = jnp.broadcast_to((own + other)[None], (PLANE, 2 * per_peer, lanes))
+    gathered = lax.all_to_all(
+        total,
+        "pts",
+        split_axis=0,
+        concat_axis=0,
+        tiled=True,
+        axis_index_groups=[
+            list(range(start, start + PLANE)) for start in range(0, shards, PLANE)
+        ],
+    )
     factor = float(lax.axis_size("rep") * shards * length) ** (-0.5)
     qkv_total, out_total, pool_total, gain_total = call(
         functools.partial(finish_kernel, factor),
@@ -460,7 +518,7 @@
             shape((CHANNELS, lanes), F32),
             shape((1, CHANNELS), F32),
         ),
-    )(gathered, other)
+    )(gathered, qkv_t, gain)
     return (
         pooled[None],
         feat_grad[None],

time: 134 us -> 131 us (0.978)
  blocking collectives: 90.9 us -> 76.9 us
  waiting for transfers between devices: 0.01 us -> 6.41 us
  starting transfers between devices: 4.89 us -> 8.51 us
    all_to_all x4 -> x3, blocking collectives: 90.9 us -> 76.9 us  [exchange(): lax.all_to_all(blocks, 'pts', split_axis=0, concat_axis=0, tiled=True)]
    all_to_all x0 -> x1, waiting for transfers between devices: none -> 5.58 us  [body(): lax.all_to_all(total, 'pts', split_axis=0, concat_axis=0, tiled=True, axi...]
    all_to_all x0 -> x1, starting transfers between devices: none -> 3.51 us  [body(): lax.all_to_all(total, 'pts', split_axis=0, concat_axis=0, tiled=True, axi...]
    unnamed x22 -> x18, local copies, waits for them, and re-layouts: 6.65 us -> 6.64 us
  transfers between devices with their start and end apart: 1 -> 2, of which waited for: 0 -> 2; matrix products, arithmetic and copies ran while one was open for 0% -> 0% of each run, Pallas kernels for 1% -> 1%
where the time goes in v2:
time: 131 us; the launch traced here: 130 us
  blocking collectives  76.9 us (59%)
  Pallas kernels  30.3 us (23%)
  starting transfers between devices  8.51 us (6%)
  local copies, waits for them, and re-layouts  7.31 us (6%)
  waiting for transfers between devices  6.41 us (5%)
    all_to_all x3, blocking collectives, exchange(): lax.all_to_all(blocks, 'pts', split_axis=0, concat_axis=0, tiled=True)  76.9 us
    pallas_call x1, Pallas kernels, body(): call(backward_kernel, (shape((shards, 2 * per_peer, lanes), BF16), shape(...  13.7 us
    pallas_call x1, Pallas kernels, body(): call(forward_kernel, (shape((shards, 2 * per_peer, lanes), BF16), shape((...  12 us
    unnamed x18, local copies, waits for them, and re-layouts  6.64 us
    all_to_all x1, waiting for transfers between devices, body(): lax.all_to_all(total, 'pts', split_axis=0, concat_axis=0, tiled=True, axi...  5.58 us
    ppermute x1, starting transfers between devices, body(): other = lax.ppermute(own, 'rep', [(0, 1), (1, 0)])  5 us
    all_to_all x1, starting transfers between devices, body(): lax.all_to_all(total, 'pts', split_axis=0, concat_axis=0, tiled=True, axi...  3.51 us
  transfers between devices with their start and end apart: 2, of which 2 were waited for; matrix products, arithmetic and copies ran while one was open for 0% of the time, Pallas kernels for 1%

profile of v2, /device:TPU:1, one launch (start us, length us, event | category | flops | bytes accessed | tf_op | source)
XLA Modules:
  0.0 130.1 jit_solution(3050586794275101715)
XLA Ops:
  0.6 0.0 copy-start
  0.6 0.9 copy-done
  1.5 0.0 copy-start.1
  1.5 0.8 copy-done.1
  2.4 0.0 copy-start.2
  2.4 0.8 copy-done.2
  3.1 0.0 copy-start.3
  3.1 0.7 copy-done.3
  3.9 0.0 copy-start.4
  3.9 0.7 copy-done.4
  4.6 0.0 copy-start.5
  4.6 0.7 copy-done.5
  5.3 0.0 copy-start.6
  5.3 0.7 copy-done.6
  5.9 0.0 copy-start.7
  6.0 0.7 copy-done.7
  6.6 0.0 copy-start.8
  6.6 0.7 copy-done.8
  7.3 2.4 %shard_map.136 = (bf16[128,8,128]{2,1,0:T(8,128)(2,1)S(1)}, s32[1,1024]{1,0:T(1,128)S(1)}, s32[1,1024]{1,0:T(1,128)S(1)}, bf16[128,256]{1,0:T(8,128)(2,1)S(1)}, ...) custom-call(s32[1,1024]{1,0:T(1,128)S(1)} %copy-done.5, ...), custom_call_target="tpu_custom_call" | custom-call | flops 1073741824 | bytes 1048576 | tf_op jit(solution)/shard_map/pallas_call | solution.py:434
  9.7 29.4 %all_to_all.20 = bf16[128,8,128]{2,1,0:T(8,128)(2,1)S(1)} all-to-all(bf16[128,8,128]{2,1,0:T(8,128)(2,1)S(1)} %get-tuple-element.24), channel_id=1, replica_groups=mesh['pts'=128,'rep'=2] {'pts'}, dimensions={0} | all-to-all | bytes 524288 | tf_op jit(solution)/shard_map/all_to_all | solution.py:399
  39.1 12.0 %shard_map.137 = (bf16[128,16,128]{2,1,0:T(8,128)(2,1)S(1)}, bf16[64,1024]{1,0:T(8,128)(2,1)S(1)}, f32[64,1024]{1,0:T(8,128)S(1)}, bf16[4,1024,1024]{2,1,0:T(8,128)(2,1)}) custom-call(bf16[1024,128]{1,0:T(8,128)(2,1)S(1)} %bitcast.12, s32[1,1024]{1,0:T(1,128)S(1)} %get-tuple-element.25.o_slot_ref, bf16[64,192]{1,0:T(8,128)(2,1)S(1)} %get-tuple-element.26.qkv_t_ref, ...), custom_call_target="tpu_custom_call" | custom-call | flops 4294967296 | bytes 1048576 | tf_op jit(solution)/shard_map/pallas_call | solution.py:449
  51.2 23.5 %all_to_all.21.returned_ref = bf16[128,16,128]{2,1,0:T(8,128)(2,1)S(1)} all-to-all(bf16[128,16,128]{2,1,0:T(8,128)(2,1)S(1)} %get-tuple-element.31), channel_id=1, replica_groups=mesh['pts'=128,'rep'=2] {'pts'}, dimensions={0} | all-to-all | bytes 1048576 | tf_op jit(solution)/shard_map/all_to_all | solution.py:399
  74.6 13.7 %shard_map.138 = (bf16[128,16,128]{2,1,0:T(8,128)(2,1)S(1)}, bf16[128,256]{1,0:T(8,128)(2,1)}) custom-call(bf16[128,16,128]{2,1,0:T(8,128)(2,1)S(1)} %all_to_all.21.returned_ref, bf16[1024,128]{1,0:T(8,128)(2,1)S(1)} %bitcast.13, s32[1,1024]{1,0:T(1,128)S(1)} %get-tuple-element.25.o_slot_ref, bf16[64,192]{1,0:T(8,128)(2,1)S(1)} %get-tuple-element.26.qkv_t_ref, ...), custom_call_target="tpu_custom_call" | custom-call | flops 8589934592 | bytes 1048576 | tf_op jit(solution)/shard_map/pallas_call | solution.py:467
  88.3 24.0 %all_to_all.22.arrived_ref = bf16[128,16,128]{2,1,0:T(8,128)(2,1)S(1)} all-to-all(bf16[128,16,128]{2,1,0:T(8,128)(2,1)S(1)} %get-tuple-element.36), channel_id=1, replica_groups=mesh['pts'=128,'rep'=2] {'pts'}, dimensions={0} | all-to-all | bytes 1048576 | tf_op jit(solution)/shard_map/all_to_all | solution.py:399
  112.3 0.2 shard_map.140
  112.5 5.0 %collective-permute-start = (f32[16,128]{1,0:T(8,128)S(1)}, f32[16,128]{1,0:T(8,128)S(1)}, u32[]{:S(2)}, u32[]{:S(2)}) collective-permute-start(f32[16,128]{1,0:T(8,128)S(1)} %shard_map.140), channel_id=1, source_target_pairs={{0,1},{1,0},{2,3},{3,2},{4,5},{5,4},{6,7},{7,6},{8,9},{9,8},{10,11... | collective-permute-start | bytes 24584 | tf_op jit(solution)/shard_map/ppermute | solution.py:497
  117.5 0.8 collective-permute-done
  118.3 0.7 broadcast_in_dim.14
  119.0 3.5 %all-to-all-start.3 = ((f32[16,16,128]{2,1,0:T(8,128)}), f32[16,16,128]{2,1,0:T(8,128)S(1)}, u32[]{:S(2)}, u32[]{:S(2)}) async-start(f32[16,16,128]{2,1,0:T(8,128)} %broadcast_in_dim.14), calls=%async_computation.3 | async-start | bytes 262144 | tf_op jit(solution)/shard_map/all_to_all | solution.py:502
  122.5 1.2 shard_map.139
  123.7 5.6 %all-to-all-done.3.total_ref = f32[16,16,128]{2,1,0:T(8,128)S(1)} async-done(((f32[16,16,128]{2,1,0:T(8,128)}), f32[16,16,128]{2,1,0:T(8,128)S(1)}, u32[]{:S(2)}, u32[]{:S(2)}) %all-to-all-start.3) | async-done | bytes 131104 | tf_op jit(solution)/shard_map/all_to_all | solution.py:502
  129.3 0.8 shard_map.141
  (1 shorter events, 0.0 us)
Async XLA Ops:
  0.6 0.9 copy-start
  1.5 0.8 copy-start.1
  2.4 0.8 copy-start.2
  3.1 0.7 copy-start.3
  3.9 0.7 copy-start.4
  4.6 0.7 copy-start.5
  5.3 0.7 copy-start.6
  5.9 0.7 copy-start.7
  6.6 0.7 copy-start.8
  112.5 5.8 %collective-permute-start = (f32[16,128]{1,0:T(8,128)S(1)}, f32[16,128]{1,0:T(8,128)S(1)}, u32[]{:S(2)}, u32[]{:S(2)}) collective-permute-start(f32[16,128]{1,0:T(8,128)S(1)} %shard_map.140), channel_id=1, source_target_pairs={{0,1},{1,0},{2,3},{3,2},{4,5},{5,4},{6,7},{7,6},{8,9},{9,8},{10,11... | collective-permute-start | bytes 24584 | tf_op jit(solution)/shard_map/ppermute | solution.py:497
  119.0 10.3 %all-to-all-start.3 = ((f32[16,16,128]{2,1,0:T(8,128)}), f32[16,16,128]{2,1,0:T(8,128)S(1)}, u32[]{:S(2)}, u32[]{:S(2)}) async-start(f32[16,16,128]{2,1,0:T(8,128)} %broadcast_in_dim.14), calls=%async_computation.3 | async-start | bytes 262144 | tf_op jit(solution)/shard_map/all_to_all | solution.py:502

commit v3 on v2

--- a/solution.py
+++ b/solution.py
@@ -12,7 +12,7 @@
 CHANNELS = 64
 NORM_EPS = 1e-05
 CHUNK = 256
-PLANE = 16
+GROUP = 64
 
 F32 = jnp.float32
 BF16 = jnp.bfloat16
@@ -265,6 +265,7 @@
     per_peer = length // shards
     place, first_cell, second_cell = arrived_columns(arrived_ref[...])
     blank = jnp.zeros((CHANNELS, length), BF16)
+    blank_clusters = jnp.zeros((CHANNELS, clusters), BF16)
 
     first = on_columns(first_cell, clusters)
     second = on_columns(second_cell, clusters)
@@ -273,7 +274,10 @@
     sums = dot(mixed_rows[:CHANNELS], first) + dot(mixed_rows[CHANNELS:], second)
     pooled_mean = (sums / denom).astype(BF16)
     pooled_ref[...] = dot_tn(pool_t_ref[...], pooled_mean).astype(BF16)
-    pool_part = dot_nt(pooled_mean, pool_grad_ref[...])
+    pool_parts = [
+        dot_nt(pooled_mean, jnp.concatenate([blank_clusters, half], axis=0))
+        for half in (pool_grad_ref[:CHANNELS, :], pool_grad_ref[CHANNELS:, :])
+    ]
 
     gain = gain_column(gain_ref)
     normed, inverse_std, hidden = layer_norm(hilbert_ref[...].astype(F32), gain)
@@ -333,8 +337,10 @@
     grad_qkv = jnp.concatenate(
         [grad_query_ref[...].T, grad_key_ref[...], grad_value_ref[...]], axis=0
     ).astype(BF16)
-    query_key_part = dot_nt(hidden, grad_qkv[: 2 * CHANNELS])
-    value_part = dot_nt(hidden, jnp.concatenate([blank, grad_qkv[2 * CHANNELS :]], axis=0))
+    qkv_parts = [
+        dot_nt(hidden, jnp.concatenate([blank, grad_qkv[start : start + CHANNELS]], axis=0))
+        for start in (0, CHANNELS, 2 * CHANNELS)
+    ]
     grad_hidden = dot(qkv_t_ref[...], grad_qkv)
     grad_normed = grad_hidden * gain
     grad_norm_in = inverse_std * (
@@ -344,37 +350,41 @@
     )
     grad_rows = (grad_mixed + grad_norm_in).astype(BF16)
     back = dot_nt(on_columns(place, length), jnp.concatenate([grad_rows, blank], axis=0))
-    beside = jnp.concatenate([value_part, out_part], axis=0)
-    below = jnp.concatenate([query_key_part, pool_part], axis=0).astype(BF16)
-    below = below.reshape(PLANE, per_peer, 2 * CHANNELS)
-    span = PLANE * per_peer
-    for start in range(0, shards, PLANE):
-        rows = back[start * per_peer : start * per_peer + span] + beside
-        out_ref[start : start + PLANE, :per_peer, :] = rows.astype(BF16).reshape(below.shape)
-        out_ref[start : start + PLANE, per_peer:, :] = below
+    parts = qkv_parts + [out_part] + pool_parts
+    unused = jnp.zeros((GROUP * per_peer - len(parts) * CHANNELS, 2 * CHANNELS), F32)
+    side = jnp.concatenate(parts + [unused], axis=0)
+    span = GROUP * per_peer
+    for start in range(0, shards, GROUP):
+        rows = back[start * per_peer : start * per_peer + span] + side
+        out_ref[start : start + GROUP] = rows.astype(BF16).reshape(GROUP, per_peer, 2 * CHANNELS)
 
 
 def total_kernel(arrived_ref, out_ref):
     out_ref[...] = jnp.sum(arrived_ref[...].astype(F32), axis=0)
 
 
+def spread_kernel(own_ref, other_ref, out_ref):
+    total = own_ref[...] + other_ref[...]
+    high = total.astype(BF16).astype(F32)
+    low = pltpu.roll(total - high, CHANNELS, 1)
+    chosen = jnp.where(iota(total.shape, 1) >= CHANNELS, high, low)
+    out_ref[...] = jnp.broadcast_to(chosen[None], out_ref.shape).astype(BF16)
+
+
 def feat_grad_kernel(arrived_ref, z_slot_ref, out_ref):
-    shards, rows_per_peer, lanes = arrived_ref.shape
-    length = shards * rows_per_peer // 2
-    arrived = arrived_ref[:, : rows_per_peer // 2, :].reshape(length, lanes)
-    rows = turned(arrived)[:CHANNELS].astype(BF16)
+    length = arrived_ref.shape[0]
+    rows = turned(arrived_ref[...])[:CHANNELS].astype(BF16)
     out_ref[...] = dot(rows, on_rows(z_slot_ref[...], length)).astype(BF16)
 
 
 def finish_kernel(factor, total_ref, qkv_t_ref, gain_in_ref, qkv_ref, out_ref, pool_ref, gain_ref):
-    chunks, rows, lanes = total_ref.shape
-    half = rows // 2
-    beside = total_ref[:, :half, :].reshape(chunks * half, lanes)[:, CHANNELS:] * factor
-    below = total_ref[:, half:, :].reshape(chunks * half, lanes) * factor
-    qkv = jnp.concatenate([below[:CHANNELS], beside[:CHANNELS]], axis=1)
+    both = total_ref[...].astype(F32)
+    both = (both[:, CHANNELS:] + both[:, :CHANNELS]) * factor
+    piece = [both[k * CHANNELS : (k + 1) * CHANNELS] for k in range(6)]
+    qkv = jnp.concatenate(piece[:3], axis=1)
     qkv_ref[...] = qkv
-    out_ref[...] = beside[CHANNELS:]
-    pool_ref[...] = below[CHANNELS:]
+    out_ref[...] = piece[3]
+    pool_ref[...] = jnp.concatenate(piece[4:], axis=1)
     column = jnp.sum(qkv * qkv_t_ref[...].astype(F32), axis=1, keepdims=True)
     eye = iota((CHANNELS, CHANNELS), 0) == iota((CHANNELS, CHANNELS), 1)
     gain_ref[...] = jnp.sum(jnp.where(eye, column, 0.0), axis=0, keepdims=True) / gain_in_ref[...]
@@ -420,7 +430,9 @@
     gain = norm_gain.reshape(1, CHANNELS)
     upstream_pool = pooled_grad[0]
 
-    arguments = (
+    arguments = tuple(
+        pltpu.with_memory_space_constraint(one, pltpu.HBM)
+        for one in (
         hilbert_of_z,
         pool_owner.reshape(1, length),
         pool_slot,
@@ -430,6 +442,7 @@
         out_weight,
         pool_t,
         gain,
+        )
     )
     outgoing, z_slot, o_slot, upstream_pool, qkv_t, out_weight, pool_t, gain = call(
         send_kernel,
@@ -466,7 +479,7 @@
 
     last, pooled = call(
         backward_kernel,
-        (shape((shards, 2 * per_peer, lanes), BF16), shape((2 * CHANNELS, clusters), BF16)),
+        (shape((shards, per_peer, lanes), BF16), shape((2 * CHANNELS, clusters), BF16)),
         scratch=(
             pltpu.VMEM((HEADS, length, CHANNELS), BF16),
             pltpu.VMEM((length, lanes), BF16),
@@ -493,12 +506,12 @@
     )
     final = exchange(last)
 
-    own = call(total_kernel, shape((2 * per_peer, lanes), F32))(final)
+    own = call(total_kernel, shape((per_peer, lanes), F32))(final)
     other = lax.ppermute(own, "rep", [(0, 1), (1, 0)])
     feat_grad = call(feat_grad_kernel, shape((CHANNELS, length), BF16), flops=1 << 28)(
-        final, z_slot
-    )
-    total = jnp.broadcast_to((own + other)[None], (PLANE, 2 * per_peer, lanes))
+        final.reshape(length, lanes), z_slot
+    )
+    total = call(spread_kernel, shape((GROUP, per_peer, lanes), BF16))(own, other)
     gathered = lax.all_to_all(
         total,
         "pts",
@@ -506,9 +519,9 @@
         concat_axis=0,
         tiled=True,
         axis_index_groups=[
-            list(range(start, start + PLANE)) for start in range(0, shards, PLANE)
+            list(range(start, start + GROUP)) for start in range(0, shards, GROUP)
         ],
-    )
+    ).reshape(GROUP * per_peer, lanes)
     factor = float(lax.axis_size("rep") * shards * length) ** (-0.5)
     qkv_total, out_total, pool_total, gain_total = call(
         functools.partial(finish_kernel, factor),

time: 131 us -> 123 us (0.939)
  local copies, waits for them, and re-layouts: 7.31 us -> 0 us
  blocking collectives: 76.9 us -> 72.8 us
  waiting for transfers between devices: 6.41 us -> 9.47 us
    unnamed x18 -> x0, local copies, waits for them, and re-layouts: 6.64 us -> none
    all_to_all x3, blocking collectives: 76.9 us -> 72.8 us  [exchange(): lax.all_to_all(blocks, 'pts', split_axis=0, concat_axis=0, tiled=True)]
    all_to_all x1, waiting for transfers between devices: 5.58 us -> 8.64 us  [body(): lax.all_to_all(total, 'pts', split_axis=0, concat_axis=0, tiled=True, axi...]
    pallas_call x2 -> x3, Pallas kernels: 13.8 us -> 14.6 us  [the longest x1 13.7 us: body(): call(backward_kernel, (shape((shards, per_peer, lanes), BF16), shape((2 *...]
where the time goes in v3:
time: 123 us
  blocking collectives  72.8 us (59%)
  Pallas kernels  31.5 us (26%)
  waiting for transfers between devices  9.47 us (8%)
  starting transfers between devices  8.41 us (7%)
    all_to_all x3, blocking collectives, exchange(): lax.all_to_all(blocks, 'pts', split_axis=0, concat_axis=0, tiled=True)  72.8 us
    pallas_call x1, Pallas kernels, body(): call(backward_kernel, (shape((shards, per_peer, lanes), BF16), shape((2 *...  13.7 us
    pallas_call x1, Pallas kernels, body(): call(forward_kernel, (shape((shards, 2 * per_peer, lanes), BF16), shape((...  12 us
    all_to_all x1, waiting for transfers between devices, body(): lax.all_to_all(total, 'pts', split_axis=0, concat_axis=0, tiled=True, axi...  8.64 us
    all_to_all x1, starting transfers between devices, body(): lax.all_to_all(total, 'pts', split_axis=0, concat_axis=0, tiled=True, axi...  4.62 us
    ppermute x1, starting transfers between devices, body(): other = lax.ppermute(own, 'rep', [(0, 1), (1, 0)])  3.8 us
    pallas_call x1, Pallas kernels, body(): call(send_kernel, (shape((shards, per_peer, lanes), BF16), shape((1, leng...  2.83 us
  transfers between devices with their start and end apart: 2, of which 2 were waited for; matrix products, arithmetic and copies ran while one was open for 0% of the time, Pallas kernels for 1%

profile of v3, /device:TPU:1, one launch (start us, length us, event | category | flops | bytes accessed | tf_op | source)
XLA Modules:
  0.0 122.9 jit_solution(2308968376729435439)
XLA Ops:
  0.6 2.8 %shard_map.136 = (bf16[128,8,128]{2,1,0:T(8,128)(2,1)S(1)}, s32[1,1024]{1,0:T(1,128)S(1)}, s32[1,1024]{1,0:T(1,128)S(1)}, bf16[128,256]{1,0:T(8,128)(2,1)S(1)}, ...) custom-call(s32[1,1024]{1,0:T(1,128)} %pos_hbm.1, ...), custom_call_target="tpu_custom_call" | custom-call | flops 1073741824 | bytes 1048576 | tf_op jit(solution)/shard_map/pallas_call | solution.py:447
  3.5 29.4 %all_to_all.20 = bf16[128,8,128]{2,1,0:T(8,128)(2,1)S(1)} all-to-all(bf16[128,8,128]{2,1,0:T(8,128)(2,1)S(1)} %get-tuple-element.24), channel_id=1, replica_groups=mesh['pts'=128,'rep'=2] {'pts'}, dimensions={0} | all-to-all | bytes 524288 | tf_op jit(solution)/shard_map/all_to_all | solution.py:409
  32.9 12.0 %shard_map.137 = (bf16[128,16,128]{2,1,0:T(8,128)(2,1)S(1)}, bf16[64,1024]{1,0:T(8,128)(2,1)S(1)}, f32[64,1024]{1,0:T(8,128)S(1)}, bf16[4,1024,1024]{2,1,0:T(8,128)(2,1)}) custom-call(bf16[1024,128]{1,0:T(8,128)(2,1)S(1)} %bitcast.16, s32[1,1024]{1,0:T(1,128)S(1)} %get-tuple-element.25.o_slot_ref, bf16[64,192]{1,0:T(8,128)(2,1)S(1)} %get-tuple-element.26.qkv_t_ref, ...), custom_call_target="tpu_custom_call" | custom-call | flops 4294967296 | bytes 1048576 | tf_op jit(solution)/shard_map/pallas_call | solution.py:462
  44.9 23.5 %all_to_all.21.returned_ref = bf16[128,16,128]{2,1,0:T(8,128)(2,1)S(1)} all-to-all(bf16[128,16,128]{2,1,0:T(8,128)(2,1)S(1)} %get-tuple-element.31), channel_id=1, replica_groups=mesh['pts'=128,'rep'=2] {'pts'}, dimensions={0} | all-to-all | bytes 1048576 | tf_op jit(solution)/shard_map/all_to_all | solution.py:409
  68.4 13.7 %shard_map.138 = (bf16[128,8,128]{2,1,0:T(8,128)(2,1)S(1)}, bf16[128,256]{1,0:T(8,128)(2,1)}) custom-call(bf16[128,16,128]{2,1,0:T(8,128)(2,1)S(1)} %all_to_all.21.returned_ref, bf16[1024,128]{1,0:T(8,128)(2,1)S(1)} %bitcast.17, s32[1,1024]{1,0:T(1,128)S(1)} %get-tuple-element.25.o_slot_ref, bf16[64,192]{1,0:T(8,128)(2,1)S(1)} %get-tuple-element.26.qkv_t_ref, ...), custom_call_target="tpu_custom_call" | custom-call | flops 8589934592 | bytes 1048576 | tf_op jit(solution)/shard_map/pallas_call | solution.py:480
  82.1 19.9 %all_to_all.22.arrived_ref = bf16[128,8,128]{2,1,0:T(8,128)(2,1)S(1)} all-to-all(bf16[128,8,128]{2,1,0:T(8,128)(2,1)S(1)} %get-tuple-element.36), channel_id=1, replica_groups=mesh['pts'=128,'rep'=2] {'pts'}, dimensions={0} | all-to-all | bytes 524288 | tf_op jit(solution)/shard_map/all_to_all | solution.py:409
  102.0 0.1 shard_map.140.own_ref
  102.1 3.8 %collective-permute-start = (f32[8,128]{1,0:T(8,128)S(1)}, f32[8,128]{1,0:T(8,128)S(1)}, u32[]{:S(2)}, u32[]{:S(2)}) collective-permute-start(f32[8,128]{1,0:T(8,128)S(1)} %shard_map.140.own_ref), channel_id=1, source_target_pairs={{0,1},{1,0},{2,3},{3,2},{4,5},{5,4},{6,7},{7,6},{8,9},{9,8},{10,11... | collective-permute-start | bytes 12296 | tf_op jit(solution)/shard_map/ppermute | solution.py:510
  105.9 0.8 collective-permute-done.other_ref
  106.8 0.7 shard_map.141
  107.5 4.6 %all-to-all-start.3 = ((bf16[64,8,128]{2,1,0:T(8,128)(2,1)}), bf16[64,8,128]{2,1,0:T(8,128)(2,1)S(1)}, u32[]{:S(2)}, u32[]{:S(2)}) async-start(bf16[64,8,128]{2,1,0:T(8,128)(2,1)} %shard_map.141), calls=%async_computation.3 | async-start | bytes 262144 | tf_op jit(solution)/shard_map/all_to_all | solution.py:515
  112.1 1.2 %shard_map.139 = bf16[64,1024]{1,0:T(8,128)(2,1)} custom-call(bf16[1024,128]{1,0:T(8,128)(2,1)S(1)} %bitcast.14, s32[1,1024]{1,0:T(1,128)S(1)} %get-tuple-element.37.z_slot_ref), custom_call_target="tpu_custom_call" | custom-call | flops 268435456 | bytes 1048576 | tf_op jit(solution)/shard_map/pallas_call | solution.py:511
  113.4 8.6 %all-to-all-done.3 = bf16[64,8,128]{2,1,0:T(8,128)(2,1)S(1)} async-done(((bf16[64,8,128]{2,1,0:T(8,128)(2,1)}), bf16[64,8,128]{2,1,0:T(8,128)(2,1)S(1)}, u32[]{:S(2)}, u32[]{:S(2)}) %all-to-all-start.3) | async-done | bytes 131104 | tf_op jit(solution)/shard_map/all_to_all | solution.py:515
  122.0 0.9 shard_map.142
Async XLA Ops:
  102.1 4.6 %collective-permute-start = (f32[8,128]{1,0:T(8,128)S(1)}, f32[8,128]{1,0:T(8,128)S(1)}, u32[]{:S(2)}, u32[]{:S(2)}) collective-permute-start(f32[8,128]{1,0:T(8,128)S(1)} %shard_map.140.own_ref), channel_id=1, source_target_pairs={{0,1},{1,0},{2,3},{3,2},{4,5},{5,4},{6,7},{7,6},{8,9},{9,8},{10,11... | collective-permute-start | bytes 12296 | tf_op jit(solution)/shard_map/ppermute | solution.py:510
  107.5 14.5 %all-to-all-start.3 = ((bf16[64,8,128]{2,1,0:T(8,128)(2,1)}), bf16[64,8,128]{2,1,0:T(8,128)(2,1)S(1)}, u32[]{:S(2)}, u32[]{:S(2)}) async-start(bf16[64,8,128]{2,1,0:T(8,128)(2,1)} %shard_map.141), calls=%async_computation.3 | async-start | bytes 262144 | tf_op jit(solution)/shard_map/all_to_all | solution.py:515

commit v4 on v3

--- a/solution.py
+++ b/solution.py
@@ -210,22 +210,33 @@
         mask = head_lanes((length, CHANNELS), head)
         value_ref[head] = jnp.where(mask, values, 0.0).astype(BF16)
 
-    def one_chunk(index, carry):
-        rows = pl.ds(pl.multiple_of(index * CHUNK, CHUNK), CHUNK)
-        queries = query_ref[rows, :].astype(F32)
-        total = jnp.zeros((CHUNK, CHANNELS), F32)
-        for head in range(HEADS):
-            mask = head_lanes((CHUNK, CHANNELS), head)
-            mine = jnp.where(mask, queries, 0.0).astype(BF16)
-            weights = jnp.exp(dot(mine, key_ref[...]))
-            share = 1.0 / jnp.sum(weights, axis=1, keepdims=True)
-            probs = (weights * share).astype(BF16)
-            probs_ref[head, rows, :] = probs
-            total = total + dot(probs, value_ref[head])
-        rows_ref[rows, :] = total
-        return carry
-
-    lax.fori_loop(0, length // CHUNK, one_chunk, 0)
+    units = [(start, head) for start in range(0, length, CHUNK) for head in range(HEADS)]
+
+    def scores(unit):
+        start, head = unit
+        queries = query_ref[start : start + CHUNK, :].astype(F32)
+        mask = head_lanes((CHUNK, CHANNELS), head)
+        return dot(jnp.where(mask, queries, 0.0).astype(BF16), key_ref[...])
+
+    def mix(unit):
+        start, head = unit
+        return dot(probs_ref[head, start : start + CHUNK, :], value_ref[head])
+
+    totals = []
+    ready = scores(units[0])
+    for number, (start, head) in enumerate(units):
+        now = ready
+        if number + 1 < len(units):
+            ready = scores(units[number + 1])
+        if number > 0:
+            totals.append(mix(units[number - 1]))
+        weights = jnp.exp(now)
+        share = 1.0 / jnp.sum(weights, axis=1, keepdims=True)
+        probs_ref[head, start : start + CHUNK, :] = (weights * share).astype(BF16)
+    totals.append(mix(units[-1]))
+    for number in range(0, len(units), HEADS):
+        start = units[number][0]
+        rows_ref[start : start + CHUNK, :] = sum(totals[number : number + HEADS])
     attended = rows_ref[...].T
     attended_ref[...] = attended
     mixed = (floats + dot(out_w_ref[...], attended.astype(BF16))).astype(BF16).astype(F32)
@@ -311,29 +322,35 @@
     grad_key_ref[...] = jnp.zeros_like(grad_key_ref)
     grad_value_ref[...] = jnp.zeros_like(grad_value_ref)
 
-    def one_chunk(index, carry):
-        rows = pl.ds(pl.multiple_of(index * CHUNK, CHUNK), CHUNK)
-        upstream = upstream_ref[rows, :].astype(F32)
-        total = jnp.zeros((CHUNK, CHANNELS), F32)
-        lane = iota((CHUNK, 2 * CHANNELS), 1)
-        for head in range(HEADS):
-            own = slice(head * HEAD_DIM, (head + 1) * HEAD_DIM)
-            mask = (
-                (lax.shift_right_logical(lane, 4) == head)
-                | (lane == CHANNELS + head)
-                | (lane == CHANNELS + HEADS + head)
-            )
-            mine = jnp.where(mask, upstream, 0.0).astype(BF16)
-            probs = probs_ref[head, rows, :]
-            grad_value_ref[own, :] += dot(grad_out_ref[own, rows], probs)
-            change = dot(mine, value_ref[...])
-            grad_scores = (probs.astype(F32) * change).astype(BF16)
-            total = total + dot(grad_scores, key_rows_ref[head])
-            grad_key_ref[own, :] += dot(query_ref[own, rows], grad_scores)
-        grad_query_ref[rows, :] = total
-        return carry
-
-    lax.fori_loop(0, length // CHUNK, one_chunk, 0)
+    units = [(start, head) for start in range(0, length, CHUNK) for head in range(HEADS)]
+    lane = iota((CHUNK, 2 * CHANNELS), 1)
+
+    def change(unit):
+        start, head = unit
+        mask = (
+            (lax.shift_right_logical(lane, 4) == head)
+            | (lane == CHANNELS + head)
+            | (lane == CHANNELS + HEADS + head)
+        )
+        upstream = upstream_ref[start : start + CHUNK, :].astype(F32)
+        return dot(jnp.where(mask, upstream, 0.0).astype(BF16), value_ref[...])
+
+    totals = []
+    ready = change(units[0])
+    for number, (start, head) in enumerate(units):
+        own = slice(head * HEAD_DIM, (head + 1) * HEAD_DIM)
+        rows = slice(start, start + CHUNK)
+        now = ready
+        if number + 1 < len(units):
+            ready = change(units[number + 1])
+        probs = probs_ref[head, rows, :]
+        grad_value_ref[own, :] += dot(grad_out_ref[own, rows], probs)
+        grad_scores = (probs.astype(F32) * now).astype(BF16)
+        totals.append(dot(grad_scores, key_rows_ref[head]))
+        grad_key_ref[own, :] += dot(query_ref[own, rows], grad_scores)
+    for number in range(0, len(units), HEADS):
+        start = units[number][0]
+        grad_query_ref[start : start + CHUNK, :] = sum(totals[number : number + HEADS])
     grad_qkv = jnp.concatenate(
         [grad_query_ref[...].T, grad_key_ref[...], grad_value_ref[...]], axis=0
     ).astype(BF16)
@@ -400,7 +417,7 @@
         out_shape=outs,
         **more,
         scratch_shapes=list(scratch),
-        compiler_params=pltpu.CompilerParams(vmem_limit_bytes=48 * 1024 * 1024),
+        compiler_params=pltpu.CompilerParams(vmem_limit_bytes=28 * 1024 * 1024),
         cost_estimate=pl.CostEstimate(flops=flops, bytes_accessed=1 << 20, transcendentals=0),
     )
 

time: 123 us -> 115 us (0.935)
  Pallas kernels: 31.5 us -> 23.3 us
    pallas_call x1, Pallas kernels: 13.7 us -> 9.53 us  [body(): call(backward_kernel, (shape((shards, per_peer, lanes), BF16), shape((2 *...]
    pallas_call x1, Pallas kernels: 12 us -> 8.02 us  [body(): call(forward_kernel, (shape((shards, 2 * per_peer, lanes), BF16), shape((...]
where the time goes in v4:
time: 115 us
  blocking collectives  73 us (63%)
  Pallas kernels  23.3 us (20%)
  waiting for transfers between devices  9.47 us (8%)
  starting transfers between devices  8.61 us (7%)
    all_to_all x3, blocking collectives, exchange(): lax.all_to_all(blocks, 'pts', split_axis=0, concat_axis=0, tiled=True)  73 us
    pallas_call x1, Pallas kernels, body(): call(backward_kernel, (shape((shards, per_peer, lanes), BF16), shape((2 *...  9.53 us
    all_to_all x1, waiting for transfers between devices, body(): lax.all_to_all(total, 'pts', split_axis=0, concat_axis=0, tiled=True, axi...  8.64 us
    pallas_call x1, Pallas kernels, body(): call(forward_kernel, (shape((shards, 2 * per_peer, lanes), BF16), shape((...  8.02 us
    all_to_all x1, starting transfers between devices, body(): lax.all_to_all(total, 'pts', split_axis=0, concat_axis=0, tiled=True, axi...  4.62 us
    ppermute x1, starting transfers between devices, body(): other = lax.ppermute(own, 'rep', [(0, 1), (1, 0)])  3.99 us
    pallas_call x1, Pallas kernels, body(): call(send_kernel, (shape((shards, per_peer, lanes), BF16), shape((1, leng...  2.83 us
  transfers between devices with their start and end apart: 2, of which 2 were waited for; matrix products, arithmetic and copies ran while one was open for 0% of the time, Pallas kernels for 1%

profile of v4, /device:TPU:1, one launch (start us, length us, event | category | flops | bytes accessed | tf_op | source)
XLA Modules:
  0.0 115.0 jit_solution(7531224044518728755)
XLA Ops:
  0.6 2.8 %shard_map.136 = (bf16[128,8,128]{2,1,0:T(8,128)(2,1)S(1)}, s32[1,1024]{1,0:T(1,128)S(1)}, s32[1,1024]{1,0:T(1,128)S(1)}, bf16[128,256]{1,0:T(8,128)(2,1)S(1)}, ...) custom-call(s32[1,1024]{1,0:T(1,128)} %pos_hbm.1, ...), custom_call_target="tpu_custom_call" | custom-call | flops 1073741824 | bytes 1048576 | tf_op jit(solution)/shard_map/pallas_call | solution.py:464
  3.5 29.4 %all_to_all.20 = bf16[128,8,128]{2,1,0:T(8,128)(2,1)S(1)} all-to-all(bf16[128,8,128]{2,1,0:T(8,128)(2,1)S(1)} %get-tuple-element.24), channel_id=1, replica_groups=mesh['pts'=128,'rep'=2] {'pts'}, dimensions={0} | all-to-all | bytes 524288 | tf_op jit(solution)/shard_map/all_to_all | solution.py:426
  32.9 8.0 %shard_map.137 = (bf16[128,16,128]{2,1,0:T(8,128)(2,1)S(1)}, bf16[64,1024]{1,0:T(8,128)(2,1)S(1)}, f32[64,1024]{1,0:T(8,128)S(1)}, bf16[4,1024,1024]{2,1,0:T(8,128)(2,1)S(1)}) custom-call(bf16[1024,128]{1,0:T(8,128)(2,1)S(1)} %bitcast.16, s32[1,1024]{1,0:T(1,128)S(1)} %get-tuple-element.25.o_slot_ref, bf16[64,192]{1,0:T(8,128)(2,1)S(1)} %get-tuple-element.26.qkv_t_ref, ...), custom_call_target="tpu_custom_call" | custom-call | flops 4294967296 | bytes 1048576 | tf_op jit(solution)/shard_map/pallas_call | solution.py:479
  40.9 23.7 %all_to_all.21.returned_ref = bf16[128,16,128]{2,1,0:T(8,128)(2,1)S(1)} all-to-all(bf16[128,16,128]{2,1,0:T(8,128)(2,1)S(1)} %get-tuple-element.31), channel_id=1, replica_groups=mesh['pts'=128,'rep'=2] {'pts'}, dimensions={0} | all-to-all | bytes 1048576 | tf_op jit(solution)/shard_map/all_to_all | solution.py:426
  64.6 9.5 %shard_map.138 = (bf16[128,8,128]{2,1,0:T(8,128)(2,1)S(1)}, bf16[128,256]{1,0:T(8,128)(2,1)}) custom-call(bf16[128,16,128]{2,1,0:T(8,128)(2,1)S(1)} %all_to_all.21.returned_ref, bf16[1024,128]{1,0:T(8,128)(2,1)S(1)} %bitcast.17, s32[1,1024]{1,0:T(1,128)S(1)} %get-tuple-element.25.o_slot_ref, bf16[64,192]{1,0:T(8,128)(2,1)S(1)} %get-tuple-element.26.qkv_t_ref, ...), custom_call_target="tpu_custom_call" | custom-call | flops 8589934592 | bytes 1048576 | tf_op jit(solution)/shard_map/pallas_call | solution.py:497
  74.1 19.9 %all_to_all.22.arrived_ref = bf16[128,8,128]{2,1,0:T(8,128)(2,1)S(1)} all-to-all(bf16[128,8,128]{2,1,0:T(8,128)(2,1)S(1)} %get-tuple-element.36), channel_id=1, replica_groups=mesh['pts'=128,'rep'=2] {'pts'}, dimensions={0} | all-to-all | bytes 524288 | tf_op jit(solution)/shard_map/all_to_all | solution.py:426
  94.0 0.1 shard_map.140.own_ref
  94.1 4.0 %collective-permute-start = (f32[8,128]{1,0:T(8,128)S(1)}, f32[8,128]{1,0:T(8,128)S(1)}, u32[]{:S(2)}, u32[]{:S(2)}) collective-permute-start(f32[8,128]{1,0:T(8,128)S(1)} %shard_map.140.own_ref), channel_id=1, source_target_pairs={{0,1},{1,0},{2,3},{3,2},{4,5},{5,4},{6,7},{7,6},{8,9},{9,8},{10,11... | collective-permute-start | bytes 12296 | tf_op jit(solution)/shard_map/ppermute | solution.py:527
  98.1 0.8 collective-permute-done.other_ref
  99.0 0.7 shard_map.141
  99.7 4.6 %all-to-all-start.3 = ((bf16[64,8,128]{2,1,0:T(8,128)(2,1)}), bf16[64,8,128]{2,1,0:T(8,128)(2,1)S(1)}, u32[]{:S(2)}, u32[]{:S(2)}) async-start(bf16[64,8,128]{2,1,0:T(8,128)(2,1)} %shard_map.141), calls=%async_computation.3 | async-start | bytes 262144 | tf_op jit(solution)/shard_map/all_to_all | solution.py:532
  104.3 1.2 %shard_map.139 = bf16[64,1024]{1,0:T(8,128)(2,1)} custom-call(bf16[1024,128]{1,0:T(8,128)(2,1)S(1)} %bitcast.14, s32[1,1024]{1,0:T(1,128)S(1)} %get-tuple-element.37.z_slot_ref), custom_call_target="tpu_custom_call" | custom-call | flops 268435456 | bytes 1048576 | tf_op jit(solution)/shard_map/pallas_call | solution.py:528
  105.5 8.6 %all-to-all-done.3 = bf16[64,8,128]{2,1,0:T(8,128)(2,1)S(1)} async-done(((bf16[64,8,128]{2,1,0:T(8,128)(2,1)}), bf16[64,8,128]{2,1,0:T(8,128)(2,1)S(1)}, u32[]{:S(2)}, u32[]{:S(2)}) %all-to-all-start.3) | async-done | bytes 131104 | tf_op jit(solution)/shard_map/all_to_all | solution.py:532
  114.2 0.9 shard_map.142
Async XLA Ops:
  94.1 4.8 %collective-permute-start = (f32[8,128]{1,0:T(8,128)S(1)}, f32[8,128]{1,0:T(8,128)S(1)}, u32[]{:S(2)}, u32[]{:S(2)}) collective-permute-start(f32[8,128]{1,0:T(8,128)S(1)} %shard_map.140.own_ref), channel_id=1, source_target_pairs={{0,1},{1,0},{2,3},{3,2},{4,5},{5,4},{6,7},{7,6},{8,9},{9,8},{10,11... | collective-permute-start | bytes 12296 | tf_op jit(solution)/shard_map/ppermute | solution.py:527
  99.7 14.5 %all-to-all-start.3 = ((bf16[64,8,128]{2,1,0:T(8,128)(2,1)}), bf16[64,8,128]{2,1,0:T(8,128)(2,1)S(1)}, u32[]{:S(2)}, u32[]{:S(2)}) async-start(bf16[64,8,128]{2,1,0:T(8,128)(2,1)} %shard_map.141), calls=%async_computation.3 | async-start | bytes 262144 | tf_op jit(solution)/shard_map/all_to_all | solution.py:532

commit v5 on v4

--- a/solution.py
+++ b/solution.py
@@ -13,6 +13,8 @@
 NORM_EPS = 1e-05
 CHUNK = 256
 GROUP = 64
+PLANE = 16
+LAYERS = 8
 
 F32 = jnp.float32
 BF16 = jnp.bfloat16
@@ -63,6 +65,12 @@
         seen = running[:, 127:128]
         ranks.append(jnp.sum(block.astype(F32) * running, axis=0, keepdims=True) - 1.0)
     return jnp.concatenate(ranks, axis=1).astype(I32)
+
+
+def exchange_place(shard):
+    plane_place = lax.bitwise_and(shard, PLANE - 1)
+    layer = lax.shift_right_logical(shard, PLANE.bit_length() - 1)
+    return plane_place * LAYERS + layer
 
 
 def send_kernel(
@@ -113,9 +121,9 @@
     shards = out_ref.shape[0]
     per_peer = length // shards
     positions = pos_ref[...]
-    owners = owner_ref[...]
+    owners = exchange_place(owner_ref[...])
     shift = length.bit_length() - 1
-    target = lax.shift_right_logical(positions, shift)
+    target = exchange_place(lax.shift_right_logical(positions, shift))
     local = lax.bitwise_and(positions, length - 1)
     z_slot = target * per_peer + rank_in_group(target, shards)
     o_slot = owners * (2 * per_peer) + rank_in_group(owners, shards)
@@ -167,14 +175,20 @@
     return lax.shift_right_logical(iota(shape, 1), 4) == head
 
 
+def points_kernel(o_slot_ref, pool_t_ref, pool_grad_ref, slot_map_ref, cluster_grad_ref):
+    rows = lax.shift_right_logical(o_slot_ref[...], 1)
+    slot_map_ref[...] = on_rows(rows, slot_map_ref.shape[0])
+    cluster_grad_ref[...] = dot(pool_t_ref[...], pool_grad_ref[...])
+
+
 def forward_kernel(
     arrived_ref,
     o_slot_ref,
+    slot_map_ref,
     qkv_t_ref,
     out_w_ref,
-    pool_t_ref,
     gain_ref,
-    pool_grad_ref,
+    cluster_grad_ref,
     out_ref,
     hilbert_ref,
     attended_ref,
@@ -186,13 +200,13 @@
 ):
     shards = out_ref.shape[0]
     length = arrived_ref.shape[0]
-    clusters = pool_grad_ref.shape[1]
+    clusters = cluster_grad_ref.shape[1]
     arrived = arrived_ref[...]
     place, first_cell, second_cell = arrived_columns(arrived)
     first = on_columns(first_cell, clusters)
     second = on_columns(second_cell, clusters)
     denom = cluster_counts(first, second)
-    grad_mean = (dot(pool_t_ref[...], pool_grad_ref[...]) / denom).astype(BF16)
+    grad_mean = (cluster_grad_ref[...] / denom).astype(BF16)
     blank = jnp.zeros_like(grad_mean)
     back = dot_nt(first, jnp.concatenate([grad_mean, blank], axis=0))
     back = back + dot_nt(second, jnp.concatenate([blank, grad_mean], axis=0))
@@ -243,55 +257,41 @@
     o_slot = o_slot_ref[...]
     odd = lax.bitwise_and(o_slot, 1) == 1
     pair = jnp.concatenate([jnp.where(odd, 0.0, mixed), jnp.where(odd, mixed, 0.0)], axis=0)
-    picked = dot_nt(on_rows(lax.shift_right_logical(o_slot, 1), length), pair.astype(BF16))
+    picked = dot_nt(slot_map_ref[...], pair.astype(BF16))
     out_ref[:, :per_peer, :] = picked.astype(BF16).reshape(shards, per_peer, 2 * CHANNELS)
 
 
-def backward_kernel(
-    returned_ref,
+def ahead_kernel(
     arrived_ref,
-    o_slot_ref,
+    hilbert_ref,
     qkv_t_ref,
-    out_w_ref,
-    pool_t_ref,
     gain_ref,
-    pool_grad_ref,
-    hilbert_ref,
-    attended_ref,
-    probs_ref,
-    out_ref,
-    pooled_ref,
+    place_ref,
+    first_ref,
+    second_ref,
+    denom_ref,
+    hidden_ref,
+    normed_ref,
+    inverse_std_ref,
+    query_ref,
     key_rows_ref,
-    upstream_ref,
     value_ref,
-    query_ref,
-    grad_out_ref,
-    grad_query_ref,
-    grad_key_ref,
-    grad_value_ref,
 ):
-    shards = out_ref.shape[0]
     length = arrived_ref.shape[0]
-    clusters = pool_grad_ref.shape[1]
-    per_peer = length // shards
+    clusters = first_ref.shape[1]
     place, first_cell, second_cell = arrived_columns(arrived_ref[...])
-    blank = jnp.zeros((CHANNELS, length), BF16)
-    blank_clusters = jnp.zeros((CHANNELS, clusters), BF16)
-
+    place_ref[...] = on_columns(place, length)
     first = on_columns(first_cell, clusters)
     second = on_columns(second_cell, clusters)
-    denom = cluster_counts(first, second)
-    mixed_rows = turned(returned_ref[:, :per_peer, :].reshape(length, 2 * CHANNELS)).astype(BF16)
-    sums = dot(mixed_rows[:CHANNELS], first) + dot(mixed_rows[CHANNELS:], second)
-    pooled_mean = (sums / denom).astype(BF16)
-    pooled_ref[...] = dot_tn(pool_t_ref[...], pooled_mean).astype(BF16)
-    pool_parts = [
-        dot_nt(pooled_mean, jnp.concatenate([blank_clusters, half], axis=0))
-        for half in (pool_grad_ref[:CHANNELS, :], pool_grad_ref[CHANNELS:, :])
-    ]
-
-    gain = gain_column(gain_ref)
-    normed, inverse_std, hidden = layer_norm(hilbert_ref[...].astype(F32), gain)
+    first_ref[...] = first
+    second_ref[...] = second
+    denom_ref[...] = cluster_counts(first, second)
+    normed, inverse_std, hidden = layer_norm(
+        hilbert_ref[...].astype(F32), gain_column(gain_ref)
+    )
+    hidden_ref[...] = hidden
+    normed_ref[...] = normed
+    inverse_std_ref[...] = inverse_std
     qkv = dot_tn(qkv_t_ref[...], hidden).astype(BF16)
     query_ref[...] = qkv[:CHANNELS]
     key_rows = turned(qkv[CHANNELS : 2 * CHANNELS])
@@ -301,10 +301,56 @@
     value_ref[:CHANNELS, :] = qkv[2 * CHANNELS :]
     value_ref[CHANNELS:, :] = jnp.ones((CHANNELS, length), BF16)
 
+
+def backward_kernel(
+    returned_ref,
+    o_slot_ref,
+    slot_map_ref,
+    qkv_t_ref,
+    out_w_ref,
+    pool_t_ref,
+    gain_ref,
+    pool_grad_ref,
+    attended_ref,
+    probs_ref,
+    place_ref,
+    first_ref,
+    second_ref,
+    denom_ref,
+    hidden_ref,
+    normed_ref,
+    inverse_std_ref,
+    query_ref,
+    key_rows_ref,
+    value_ref,
+    out_ref,
+    pooled_ref,
+    upstream_ref,
+    grad_out_ref,
+    grad_query_ref,
+    grad_key_ref,
+    grad_value_ref,
+):
+    shards = out_ref.shape[0]
+    length = o_slot_ref.shape[1]
+    clusters = pool_grad_ref.shape[1]
+    per_peer = length // shards
+    blank = jnp.zeros((CHANNELS, length), BF16)
+    blank_clusters = jnp.zeros((CHANNELS, clusters), BF16)
+
+    mixed_rows = turned(returned_ref[:, :per_peer, :].reshape(length, 2 * CHANNELS)).astype(BF16)
+    sums = dot(mixed_rows[:CHANNELS], first_ref[...]) + dot(mixed_rows[CHANNELS:], second_ref[...])
+    pooled_mean = (sums / denom_ref[...]).astype(BF16)
+    pooled_ref[...] = dot_tn(pool_t_ref[...], pooled_mean).astype(BF16)
+    pool_parts = [
+        dot_nt(pooled_mean, jnp.concatenate([blank_clusters, half], axis=0))
+        for half in (pool_grad_ref[:CHANNELS, :], pool_grad_ref[CHANNELS:, :])
+    ]
+
     o_slot = o_slot_ref[...]
     odd = lax.bitwise_and(o_slot, 1) == 1
     slots = turned(returned_ref[:, per_peer:, :].reshape(length, 2 * CHANNELS)).astype(BF16)
-    both = dot(slots, on_rows(lax.shift_right_logical(o_slot, 1), length))
+    both = dot(slots, slot_map_ref[...])
     grad_mixed = jnp.where(odd, both[CHANNELS:], both[:CHANNELS])
     grad_mixed_low = grad_mixed.astype(BF16)
     attended = attended_ref[...]
@@ -354,19 +400,22 @@
     grad_qkv = jnp.concatenate(
         [grad_query_ref[...].T, grad_key_ref[...], grad_value_ref[...]], axis=0
     ).astype(BF16)
+    hidden = hidden_ref[...]
+    normed = normed_ref[...]
+    inverse_std = inverse_std_ref[...]
     qkv_parts = [
         dot_nt(hidden, jnp.concatenate([blank, grad_qkv[start : start + CHANNELS]], axis=0))
         for start in (0, CHANNELS, 2 * CHANNELS)
     ]
     grad_hidden = dot(qkv_t_ref[...], grad_qkv)
-    grad_normed = grad_hidden * gain
+    grad_normed = grad_hidden * gain_column(gain_ref)
     grad_norm_in = inverse_std * (
         grad_normed
         - jnp.mean(grad_normed, axis=0, keepdims=True)
         - normed * jnp.mean(grad_normed * normed, axis=0, keepdims=True)
     )
     grad_rows = (grad_mixed + grad_norm_in).astype(BF16)
-    back = dot_nt(on_columns(place, length), jnp.concatenate([grad_rows, blank], axis=0))
+    back = dot_nt(place_ref[...], jnp.concatenate([grad_rows, blank], axis=0))
     parts = qkv_parts + [out_part] + pool_parts
     unused = jnp.zeros((GROUP * per_peer - len(parts) * CHANNELS, 2 * CHANNELS), F32)
     side = jnp.concatenate(parts + [unused], axis=0)
@@ -377,11 +426,7 @@
 
 
 def total_kernel(arrived_ref, out_ref):
-    out_ref[...] = jnp.sum(arrived_ref[...].astype(F32), axis=0)
-
-
-def spread_kernel(own_ref, other_ref, out_ref):
-    total = own_ref[...] + other_ref[...]
+    total = jnp.sum(arrived_ref[...].astype(F32), axis=0)
     high = total.astype(BF16).astype(F32)
     low = pltpu.roll(total - high, CHANNELS, 1)
     chosen = jnp.where(iota(total.shape, 1) >= CHANNELS, high, low)
@@ -394,8 +439,18 @@
     out_ref[...] = dot(rows, on_rows(z_slot_ref[...], length)).astype(BF16)
 
 
-def finish_kernel(factor, total_ref, qkv_t_ref, gain_in_ref, qkv_ref, out_ref, pool_ref, gain_ref):
-    both = total_ref[...].astype(F32)
+def finish_kernel(
+    factor,
+    own_ref,
+    other_ref,
+    qkv_t_ref,
+    gain_in_ref,
+    qkv_ref,
+    out_ref,
+    pool_ref,
+    gain_ref,
+):
+    both = own_ref[...].astype(F32) + other_ref[...].astype(F32)
     both = (both[:, CHANNELS:] + both[:, :CHANNELS]) * factor
     piece = [both[k * CHANNELS : (k + 1) * CHANNELS] for k in range(6)]
     qkv = jnp.concatenate(piece[:3], axis=1)
@@ -422,8 +477,16 @@
     )
 
 
-def exchange(blocks):
-    return lax.all_to_all(blocks, "pts", split_axis=0, concat_axis=0, tiled=True)
+def exchange(blocks, size):
+    order = [layer * PLANE + place for place in range(PLANE) for layer in range(LAYERS)]
+    return lax.all_to_all(
+        blocks,
+        "pts",
+        split_axis=0,
+        concat_axis=0,
+        tiled=True,
+        axis_index_groups=[order[start : start + size] for start in range(0, len(order), size)],
+    )
 
 
 def body(
@@ -474,7 +537,12 @@
         flops=1 << 30,
         in_specs=[pl.BlockSpec(memory_space=pltpu.HBM)] * len(arguments),
     )(*arguments)
-    arrived = exchange(outgoing).reshape(length, lanes)
+    arrived = exchange(outgoing, shards).reshape(length, lanes)
+    slot_map, cluster_grad = call(
+        points_kernel,
+        (shape((length, length), BF16), shape((CHANNELS, clusters), F32)),
+        flops=1 << 31,
+    )(o_slot, pool_t, upstream_pool)
 
     both_ways, hilbert_rows, attended, probs = call(
         forward_kernel,
@@ -491,17 +559,30 @@
             pltpu.VMEM((length, CHANNELS), F32),
         ),
         flops=1 << 32,
-    )(arrived, o_slot, qkv_t, out_weight, pool_t, gain, upstream_pool)
-    returned = exchange(both_ways)
+    )(arrived, o_slot, slot_map, qkv_t, out_weight, gain, cluster_grad)
+    returned = exchange(both_ways, shards)
+    ahead = call(
+        ahead_kernel,
+        (
+            shape((length, length), BF16),
+            shape((length, clusters), BF16),
+            shape((length, clusters), BF16),
+            shape((1, clusters), F32),
+            shape((CHANNELS, length), BF16),
+            shape((CHANNELS, length), F32),
+            shape((1, length), F32),
+            shape((CHANNELS, length), BF16),
+            shape((HEADS, length, CHANNELS), BF16),
+            shape((lanes, length), BF16),
+        ),
+        flops=1 << 31,
+    )(arrived, hilbert_rows, qkv_t, gain)
 
     last, pooled = call(
         backward_kernel,
         (shape((shards, per_peer, lanes), BF16), shape((2 * CHANNELS, clusters), BF16)),
         scratch=(
-            pltpu.VMEM((HEADS, length, CHANNELS), BF16),
             pltpu.VMEM((length, lanes), BF16),
-            pltpu.VMEM((lanes, length), BF16),
-            pltpu.VMEM((CHANNELS, length), BF16),
             pltpu.VMEM((CHANNELS, length), BF16),
             pltpu.VMEM((length, CHANNELS), F32),
             pltpu.VMEM((CHANNELS, length), F32),
@@ -510,35 +591,25 @@
         flops=1 << 33,
     )(
         returned,
-        arrived,
         o_slot,
+        slot_map,
         qkv_t,
         out_weight,
         pool_t,
         gain,
         upstream_pool,
-        hilbert_rows,
         attended,
         probs,
-    )
-    final = exchange(last)
-
-    own = call(total_kernel, shape((per_peer, lanes), F32))(final)
-    other = lax.ppermute(own, "rep", [(0, 1), (1, 0)])
-    feat_grad = call(feat_grad_kernel, shape((CHANNELS, length), BF16), flops=1 << 28)(
+        *ahead,
+    )
+    final = exchange(last, shards)
+
+    total = call(total_kernel, shape((GROUP, per_peer, lanes), BF16))(final)
+    gathered = exchange(total, GROUP).reshape(GROUP * per_peer, lanes)
+    feat_grad = call(feat_grad_kernel, shape((CHANNELS, length), BF16), flops=1 << 30)(
         final.reshape(length, lanes), z_slot
     )
-    total = call(spread_kernel, shape((GROUP, per_peer, lanes), BF16))(own, other)
-    gathered = lax.all_to_all(
-        total,
-        "pts",
-        split_axis=0,
-        concat_axis=0,
-        tiled=True,
-        axis_index_groups=[
-            list(range(start, start + GROUP)) for start in range(0, shards, GROUP)
-        ],
-    ).reshape(GROUP * per_peer, lanes)
+    other = lax.ppermute(gathered, "rep", [(0, 1), (1, 0)])
     factor = float(lax.axis_size("rep") * shards * length) ** (-0.5)
     qkv_total, out_total, pool_total, gain_total = call(
         functools.partial(finish_kernel, factor),
@@ -548,7 +619,7 @@
             shape((CHANNELS, lanes), F32),
             shape((1, CHANNELS), F32),
         ),
-    )(gathered, qkv_t, gain)
+    )(gathered, other, qkv_t, gain)
     return (
         pooled[None],
         feat_grad[None],

time: 115 us -> 135 us (1.17)
  blocking collectives: 73 us -> 32.8 us
  local copies, waits for them, and re-layouts: 0 us -> 23.2 us
  starting transfers between devices: 8.61 us -> 28.2 us
  waiting for transfers between devices: 9.47 us -> 23 us
  Pallas kernels: 23.3 us -> 26.7 us
    all_to_all x3 -> x2, blocking collectives: 73 us -> 32.8 us  [exchange(): lax.all_to_all(blocks, 'pts', split_axis=0, concat_axis=0, tiled=True, ax...]
    unnamed x0 -> x44, local copies, waits for them, and re-layouts: none -> 23.2 us
    all_to_all x1 -> x2, starting transfers between devices: 4.62 us -> 23.4 us  [exchange(): lax.all_to_all(blocks, 'pts', split_axis=0, concat_axis=0, tiled=True, ax...]
    all_to_all x1 -> x2, waiting for transfers between devices: 8.64 us -> 23 us  [exchange(): lax.all_to_all(blocks, 'pts', split_axis=0, concat_axis=0, tiled=True, ax...]
    pallas_call x3 -> x4, Pallas kernels: 2.11 us -> 3.83 us  [the longest x1 1.33 us: body(): call(ahead_kernel, (shape((length, length), BF16), shape((length, cluster...]
  transfers between devices with their start and end apart: 2 -> 3, of which waited for: 2 -> 2; matrix products, arithmetic and copies ran while one was open for 0% -> 0% of each run, Pallas kernels for 1% -> 3%
where the time goes in v5:
time: 135 us
  blocking collectives  32.8 us (24%)
  starting transfers between devices  28.2 us (21%)
  Pallas kernels  26.7 us (20%)
  local copies, waits for them, and re-layouts  23.2 us (17%)
  waiting for transfers between devices  23 us (17%)
    all_to_all x2, blocking collectives, exchange(): lax.all_to_all(blocks, 'pts', split_axis=0, concat_axis=0, tiled=True, ax...  32.8 us
    all_to_all x2, starting transfers between devices, exchange(): lax.all_to_all(blocks, 'pts', split_axis=0, concat_axis=0, tiled=True, ax...  23.4 us
    unnamed x44, local copies, waits for them, and re-layouts  23.2 us
    all_to_all x2, waiting for transfers between devices, exchange(): lax.all_to_all(blocks, 'pts', split_axis=0, concat_axis=0, tiled=True, ax...  23 us
    pallas_call x1, Pallas kernels, body(): call(backward_kernel, (shape((shards, per_peer, lanes), BF16), shape((2 *...  9.67 us
    pallas_call x1, Pallas kernels, body(): call(forward_kernel, (shape((shards, 2 * per_peer, lanes), BF16), shape((...  8.82 us
    ppermute x1, starting transfers between devices, body(): other = lax.ppermute(gathered, 'rep', [(0, 1), (1, 0)])  4.76 us
    pallas_call x1, Pallas kernels, body(): call(send_kernel, (shape((shards, per_peer, lanes), BF16), shape((1, leng...  3.53 us
  transfers between devices with their start and end apart: 3, of which 2 were waited for; matrix products, arithmetic and copies ran while one was open for 0% of the time, Pallas kernels for 3%

profile of v5, /device:TPU:1, one launch (start us, length us, event | category | flops | bytes accessed | tf_op | source)
XLA Modules:
  0.0 134.5 jit_solution(596782045544189402)
XLA Ops:
  0.6 3.5 %shard_map.136 = (bf16[128,8,128]{2,1,0:T(8,128)(2,1)}, s32[1,1024]{1,0:T(1,128)S(1)}, s32[1,1024]{1,0:T(1,128)S(1)}, bf16[128,256]{1,0:T(8,128)(2,1)S(1)}, bf16...) custom-call(s32[1,1024]{1,0:T(1,128)} %pos_hbm.1, ...), custom_call_target="tpu_custom_call" | custom-call | flops 1073741824 | bytes 1048576 | tf_op jit(solution)/shard_map/pallas_call | solution.py:527
  4.2 16.5 %all-to-all-start = ((bf16[128,8,128]{2,1,0:T(8,128)(2,1)}), bf16[128,8,128]{2,1,0:T(8,128)(2,1)S(1)}, u32[]{:S(2)}, u32[]{:S(2)}) async-start(bf16[128,8,128]{2,1,0:T(8,128)(2,1)} %get-tuple-element.36), calls=%async_computation | async-start | bytes 524288 | tf_op jit(solution)/shard_map/all_to_all | solution.py:482
  20.7 1.0 shard_map.137
  21.7 0.0 copy-start.2
  21.7 12.3 %all-to-all-done = bf16[128,8,128]{2,1,0:T(8,128)(2,1)S(1)} async-done(((bf16[128,8,128]{2,1,0:T(8,128)(2,1)}), bf16[128,8,128]{2,1,0:T(8,128)(2,1)S(1)}, u32[]{:S(2)}, u32[]{:S(2)}) %all-to-all-start) | async-done | bytes 262176 | tf_op jit(solution)/shard_map/all_to_all | solution.py:482
  34.1 8.8 %shard_map.138 = (bf16[128,16,128]{2,1,0:T(8,128)(2,1)}, bf16[64,1024]{1,0:T(8,128)(2,1)S(1)}, f32[64,1024]{1,0:T(8,128)S(1)}, bf16[4,1024,1024]{2,1,0:T(8,128)(2,1)S(1)}) custom-call(bf16[1024,128]{1,0:T(8,128)(2,1)S(1)} %bitcast.17, s32[1,1024]{1,0:T(1,128)S(1)} %get-tuple-element.37.o_slot_ref, bf16[1024,1024]{1,0:T(8,128)(2,1)S(1)} %get-tuple-element.40.slot_map_ref, ...), custom_call_target="tpu_custom_call" | custom-call | flops 4294967296 | bytes 1048576 | tf_op jit(solution)/shard_map/pallas_call | solution.py:547
  42.9 0.0 copy-done.2
  42.9 0.0 copy-start
  42.9 3.3 %copy-done = bf16[4,1024,1024]{2,1,0:T(8,128)(2,1)} copy-done((bf16[4,1024,1024]{2,1,0:T(8,128)(2,1)}, bf16[4,1024,1024]{2,1,0:T(8,128)(2,1)S(1)}, u32[]{:S(2)}) %copy-start) | copy-done | bytes 8388632
  46.2 0.0 copy-start.16
  46.2 0.7 copy-done.16
  46.8 0.0 copy-start.18
  46.8 0.7 copy-done.18
  47.5 6.9 %all-to-all-start.1 = ((bf16[128,16,128]{2,1,0:T(8,128)(2,1)}), bf16[128,16,128]{2,1,0:T(8,128)(2,1)S(1)}, u32[]{:S(2)}, u32[]{:S(2)}) async-start(bf16[128,16,128]{2,1,0:T(8,128)(2,1)} %get-tuple-element.45), calls=%async_computation.1 | async-start | bytes 1048576 | tf_op jit(solution)/shard_map/all_to_all | solution.py:482
  54.4 0.0 copy-start.17
  54.4 0.9 copy-done.17
  55.3 1.3 shard_map.139
  56.7 0.0 copy-start.4
  56.7 1.0 copy-done.4
  57.7 0.0 copy-start.6
  57.7 0.8 copy-done.6
  58.5 0.0 copy-start.8
  58.5 0.7 copy-done.8
  59.2 0.0 copy-start.10
  59.2 0.7 copy-done.10
  59.9 0.0 copy-start.12
  59.9 0.7 copy-done.12
  60.6 0.6 copy-done.14
  61.2 0.6 copy-done.20
  61.8 10.7 %all-to-all-done.1.returned_ref = bf16[128,16,128]{2,1,0:T(8,128)(2,1)S(1)} async-done(((bf16[128,16,128]{2,1,0:T(8,128)(2,1)}), bf16[128,16,128]{2,1,0:T(8,128)(2,1)S(1)}, u32[]{:S(2)}, u32[]{:S(2)}) %all-to-all-start.1) | async-done | bytes 524320 | tf_op jit(solution)/shard_map/all_to_all | solution.py:482
  72.4 3.4 %copy-done.1 = bf16[4,1024,1024]{2,1,0:T(8,128)(2,1)S(1)} copy-done((bf16[4,1024,1024]{2,1,0:T(8,128)(2,1)S(1)}, bf16[4,1024,1024]{2,1,0:T(8,128)(2,1)}, u32[]{:S(2)}) %copy-start.1) | copy-done | bytes 8388632
  75.8 1.6 %copy-done.3 = bf16[1024,1024]{1,0:T(8,128)(2,1)S(1)} copy-done((bf16[1024,1024]{1,0:T(8,128)(2,1)S(1)}, bf16[1024,1024]{1,0:T(8,128)(2,1)}, u32[]{:S(2)}) %copy-start.3) | copy-done | bytes 2097176
  77.4 1.2 copy-done.5
  78.6 1.0 copy-done.7
  79.7 0.9 copy-done.9
  80.6 0.9 copy-done.11
  81.6 0.9 copy-done.13
  82.5 0.9 copy-done.15
  83.4 0.9 copy-done.19
  84.3 0.7 copy-done.21
  85.0 9.7 %shard_map.140 = (bf16[128,8,128]{2,1,0:T(8,128)(2,1)S(1)}, bf16[128,256]{1,0:T(8,128)(2,1)}) custom-call(bf16[128,16,128]{2,1,0:T(8,128)(2,1)S(1)} %all-to-all-done.1.returned_ref, s32[1,1024]{1,0:T(1,128)S(1)} %get-tuple-element.37.o_slot_ref, bf16[1024,1024]{1,0:T(8,128)(2,1)S(1)} %copy-done.3, bf16[64,192]{1,0:T(8,128)(2,1)S(1)} %get-tuple-element.41.qkv_t_ref, ...), custom_call_target="tpu_custom_call" | custom-call | flops 8589934592 | bytes 1048576 | tf_op jit(solution)/shard_map/pallas_call | solution.py:581
  94.7 19.0 %all_to_all.20.arrived_ref = bf16[128,8,128]{2,1,0:T(8,128)(2,1)S(1)} all-to-all(bf16[128,8,128]{2,1,0:T(8,128)(2,1)S(1)} %get-tuple-element.60), channel_id=1, replica_groups={{0,32,64,96,128,160,192,224,2,34,66,98,130,162,194,226,4,36,68,100,132,..., dimensions={0} | all-to-all | bytes 524288 | tf_op jit(solution)/shard_map/all_to_all | solution.py:482
  113.6 0.2 shard_map.142
  113.9 13.8 %all_to_all.21 = bf16[64,8,128]{2,1,0:T(8,128)(2,1)S(1)} all-to-all(bf16[64,8,128]{2,1,0:T(8,128)(2,1)S(1)} %shard_map.142), channel_id=1, replica_groups={{0,32,64,96,128,160,192,224,2,34,66,98,130,162,194,226,4,36,68,100,132,..., dimensions={0} | all-to-all | bytes 262144 | tf_op jit(solution)/shard_map/all_to_all | solution.py:482
  127.7 4.8 %collective-permute-start = (bf16[512,128]{1,0:T(8,128)(2,1)S(1)}, bf16[512,128]{1,0:T(8,128)(2,1)S(1)}, u32[]{:S(2)}, u32[]{:S(2)}) collective-permute-start(bf16[512,128]{1,0:T(8,128)(2,1)S(1)} %bitcast.15), channel_id=1, source_target_pairs={{0,1},{1,0},{2,3},{3,2},{4,5},{5,4},{6,7},{7,6},{8,9},{9,8},{10,11... | collective-permute-start | bytes 393224 | tf_op jit(solution)/shard_map/ppermute | solution.py:612
  132.4 1.2 shard_map.141
  133.7 0.0 collective-permute-done.other_ref
  133.7 0.9 shard_map.143
  (12 shorter events, 0.0 us)
Async XLA Ops:
  4.2 29.9 %all-to-all-start = ((bf16[128,8,128]{2,1,0:T(8,128)(2,1)}), bf16[128,8,128]{2,1,0:T(8,128)(2,1)S(1)}, u32[]{:S(2)}, u32[]{:S(2)}) async-start(bf16[128,8,128]{2,1,0:T(8,128)(2,1)} %get-tuple-element.36), calls=%async_computation | async-start | bytes 524288 | tf_op jit(solution)/shard_map/all_to_all | solution.py:482
  21.7 21.1 %copy-start.2 = (bf16[1024,1024]{1,0:T(8,128)(2,1)}, bf16[1024,1024]{1,0:T(8,128)(2,1)S(1)}, u32[]{:S(2)}) copy-start(bf16[1024,1024]{1,0:T(8,128)(2,1)S(1)} %get-tuple-element.40.slot_map_ref) | copy-start | bytes 6291460
  42.9 3.3 %copy-start = (bf16[4,1024,1024]{2,1,0:T(8,128)(2,1)}, bf16[4,1024,1024]{2,1,0:T(8,128)(2,1)S(1)}, u32[]{:S(2)}) copy-start(bf16[4,1024,1024]{2,1,0:T(8,128)(2,1)S(1)} %get-tuple-element.47.probs_ref) | copy-start | bytes 25165828
  46.2 0.7 copy-start.16
  46.8 0.7 copy-start.18
  47.5 24.9 %all-to-all-start.1 = ((bf16[128,16,128]{2,1,0:T(8,128)(2,1)}), bf16[128,16,128]{2,1,0:T(8,128)(2,1)S(1)}, u32[]{:S(2)}, u32[]{:S(2)}) async-start(bf16[128,16,128]{2,1,0:T(8,128)(2,1)} %get-tuple-element.45), calls=%async_computation.1 | async-start | bytes 1048576 | tf_op jit(solution)/shard_map/all_to_all | solution.py:482
  54.4 0.9 copy-start.17
  56.7 1.0 copy-start.4
  57.7 0.8 copy-start.6
  58.5 0.7 copy-start.8
  59.2 0.7 copy-start.10
  59.9 0.7 copy-start.12
  60.6 0.6 copy-start.14
  61.2 0.6 copy-start.20
  72.4 3.4 %copy-start.1 = (bf16[4,1024,1024]{2,1,0:T(8,128)(2,1)S(1)}, bf16[4,1024,1024]{2,1,0:T(8,128)(2,1)}, u32[]{:S(2)}) copy-start(bf16[4,1024,1024]{2,1,0:T(8,128)(2,1)} %copy-done) | copy-start | bytes 25165828
  75.8 1.6 %copy-start.3 = (bf16[1024,1024]{1,0:T(8,128)(2,1)S(1)}, bf16[1024,1024]{1,0:T(8,128)(2,1)}, u32[]{:S(2)}) copy-start(bf16[1024,1024]{1,0:T(8,128)(2,1)} %copy-done.2) | copy-start | bytes 6291460
  77.4 1.2 copy-start.5
  78.6 1.0 copy-start.7
  79.7 0.9 copy-start.9
  80.6 0.9 copy-start.11
  81.6 0.9 copy-start.13
  82.5 0.9 copy-start.15
  83.4 0.9 copy-start.19
  84.3 0.7 copy-start.21
  127.7 6.0 %collective-permute-start = (bf16[512,128]{1,0:T(8,128)(2,1)S(1)}, bf16[512,128]{1,0:T(8,128)(2,1)S(1)}, u32[]{:S(2)}, u32[]{:S(2)}) collective-permute-start(bf16[512,128]{1,0:T(8,128)(2,1)S(1)} %bitcast.15), channel_id=1, source_target_pairs={{0,1},{1,0},{2,3},{3,2},{4,5},{5,4},{6,7},{7,6},{8,9},{9,8},{10,11... | collective-permute-start | bytes 393224 | tf_op jit(solution)/shard_map/ppermute | solution.py:612

commit v6 on v4

--- a/solution.py
+++ b/solution.py
@@ -12,7 +12,9 @@
 CHANNELS = 64
 NORM_EPS = 1e-05
 CHUNK = 256
-GROUP = 64
+GROUP = 32
+PLANE = 16
+LAYERS = 8
 
 F32 = jnp.float32
 BF16 = jnp.bfloat16
@@ -63,6 +65,12 @@
         seen = running[:, 127:128]
         ranks.append(jnp.sum(block.astype(F32) * running, axis=0, keepdims=True) - 1.0)
     return jnp.concatenate(ranks, axis=1).astype(I32)
+
+
+def exchange_place(shard):
+    plane_place = lax.bitwise_and(shard, PLANE - 1)
+    layer = lax.shift_right_logical(shard, PLANE.bit_length() - 1)
+    return plane_place * LAYERS + layer
 
 
 def send_kernel(
@@ -113,9 +121,9 @@
     shards = out_ref.shape[0]
     per_peer = length // shards
     positions = pos_ref[...]
-    owners = owner_ref[...]
+    owners = exchange_place(owner_ref[...])
     shift = length.bit_length() - 1
-    target = lax.shift_right_logical(positions, shift)
+    target = exchange_place(lax.shift_right_logical(positions, shift))
     local = lax.bitwise_and(positions, length - 1)
     z_slot = target * per_peer + rank_in_group(target, shards)
     o_slot = owners * (2 * per_peer) + rank_in_group(owners, shards)
@@ -248,6 +256,7 @@
 
 
 def backward_kernel(
+    core_ref,
     returned_ref,
     arrived_ref,
     o_slot_ref,
@@ -259,8 +268,13 @@
     hilbert_ref,
     attended_ref,
     probs_ref,
-    out_ref,
+    keep_ref,
+    give_ref,
     pooled_ref,
+    grad_qkv_ref,
+    grad_mixed_ref,
+    normed_ref,
+    inverse_std_ref,
     key_rows_ref,
     upstream_ref,
     value_ref,
@@ -270,11 +284,11 @@
     grad_key_ref,
     grad_value_ref,
 ):
-    shards = out_ref.shape[0]
+    shards = returned_ref.shape[0]
     length = arrived_ref.shape[0]
     clusters = pool_grad_ref.shape[1]
     per_peer = length // shards
-    place, first_cell, second_cell = arrived_columns(arrived_ref[...])
+    _, first_cell, second_cell = arrived_columns(arrived_ref[...])
     blank = jnp.zeros((CHANNELS, length), BF16)
     blank_clusters = jnp.zeros((CHANNELS, clusters), BF16)
 
@@ -292,6 +306,8 @@
 
     gain = gain_column(gain_ref)
     normed, inverse_std, hidden = layer_norm(hilbert_ref[...].astype(F32), gain)
+    normed_ref[...] = normed
+    inverse_std_ref[...] = inverse_std
     qkv = dot_tn(qkv_t_ref[...], hidden).astype(BF16)
     query_ref[...] = qkv[:CHANNELS]
     key_rows = turned(qkv[CHANNELS : 2 * CHANNELS])
@@ -307,6 +323,7 @@
     both = dot(slots, on_rows(lax.shift_right_logical(o_slot, 1), length))
     grad_mixed = jnp.where(odd, both[CHANNELS:], both[:CHANNELS])
     grad_mixed_low = grad_mixed.astype(BF16)
+    grad_mixed_ref[...] = grad_mixed_low
     attended = attended_ref[...]
     attended_low = attended.astype(BF16)
     out_part = dot_nt(grad_mixed_low, jnp.concatenate([blank, attended_low], axis=0))
@@ -358,30 +375,53 @@
         dot_nt(hidden, jnp.concatenate([blank, grad_qkv[start : start + CHANNELS]], axis=0))
         for start in (0, CHANNELS, 2 * CHANNELS)
     ]
-    grad_hidden = dot(qkv_t_ref[...], grad_qkv)
-    grad_normed = grad_hidden * gain
-    grad_norm_in = inverse_std * (
+    grad_qkv_ref[...] = grad_qkv
+    projections = jnp.concatenate(qkv_parts, axis=0)
+    others = jnp.concatenate([out_part] + pool_parts, axis=0)
+    leads = core_ref[0] == 0
+    keep_ref[...] = jnp.where(leads, projections, others)
+    give_ref[...] = jnp.where(leads, others, projections)
+
+
+def input_grad_kernel(
+    arrived_ref,
+    qkv_t_ref,
+    gain_ref,
+    grad_qkv_ref,
+    grad_mixed_ref,
+    normed_ref,
+    inverse_std_ref,
+    out_ref,
+):
+    length = arrived_ref.shape[0]
+    place, _, _ = arrived_columns(arrived_ref[...])
+    normed = normed_ref[...]
+    grad_hidden = dot(qkv_t_ref[...], grad_qkv_ref[...])
+    grad_normed = grad_hidden * gain_column(gain_ref)
+    grad_norm_in = inverse_std_ref[...] * (
         grad_normed
         - jnp.mean(grad_normed, axis=0, keepdims=True)
         - normed * jnp.mean(grad_normed * normed, axis=0, keepdims=True)
     )
-    grad_rows = (grad_mixed + grad_norm_in).astype(BF16)
+    grad_rows = (grad_mixed_ref[...].astype(F32) + grad_norm_in).astype(BF16)
+    blank = jnp.zeros((CHANNELS, length), BF16)
     back = dot_nt(on_columns(place, length), jnp.concatenate([grad_rows, blank], axis=0))
-    parts = qkv_parts + [out_part] + pool_parts
-    unused = jnp.zeros((GROUP * per_peer - len(parts) * CHANNELS, 2 * CHANNELS), F32)
-    side = jnp.concatenate(parts + [unused], axis=0)
+    out_ref[...] = back.astype(BF16)
+
+
+def pack_kernel(back_ref, keep_ref, other_ref, out_ref):
+    per_peer = out_ref.shape[1]
+    parts = keep_ref[...] + other_ref[...]
     span = GROUP * per_peer
-    for start in range(0, shards, GROUP):
-        rows = back[start * per_peer : start * per_peer + span] + side
+    unused = jnp.zeros((span - parts.shape[0], 2 * CHANNELS), F32)
+    side = jnp.concatenate([parts, unused], axis=0)
+    for start in range(0, out_ref.shape[0], GROUP):
+        rows = back_ref[start * per_peer : start * per_peer + span, :].astype(F32) + side
         out_ref[start : start + GROUP] = rows.astype(BF16).reshape(GROUP, per_peer, 2 * CHANNELS)
 
 
 def total_kernel(arrived_ref, out_ref):
-    out_ref[...] = jnp.sum(arrived_ref[...].astype(F32), axis=0)
-
-
-def spread_kernel(own_ref, other_ref, out_ref):
-    total = own_ref[...] + other_ref[...]
+    total = jnp.sum(arrived_ref[...].astype(F32), axis=0)
     high = total.astype(BF16).astype(F32)
     low = pltpu.roll(total - high, CHANNELS, 1)
     chosen = jnp.where(iota(total.shape, 1) >= CHANNELS, high, low)
@@ -394,10 +434,27 @@
     out_ref[...] = dot(rows, on_rows(z_slot_ref[...], length)).astype(BF16)
 
 
-def finish_kernel(factor, total_ref, qkv_t_ref, gain_in_ref, qkv_ref, out_ref, pool_ref, gain_ref):
-    both = total_ref[...].astype(F32)
-    both = (both[:, CHANNELS:] + both[:, :CHANNELS]) * factor
-    piece = [both[k * CHANNELS : (k + 1) * CHANNELS] for k in range(6)]
+def finish_kernel(
+    factor,
+    core_ref,
+    own_ref,
+    other_ref,
+    qkv_t_ref,
+    gain_in_ref,
+    qkv_ref,
+    out_ref,
+    pool_ref,
+    gain_ref,
+):
+    own = own_ref[...].astype(F32)
+    other = other_ref[...].astype(F32)
+    own = (own[:, CHANNELS:] + own[:, :CHANNELS]) * factor
+    other = (other[:, CHANNELS:] + other[:, :CHANNELS]) * factor
+    leads = core_ref[0] == 0
+    first = jnp.where(leads, own, other)
+    second = jnp.where(leads, other, own)
+    both = (first, second)
+    piece = [one[k * CHANNELS : (k + 1) * CHANNELS] for one in both for k in range(3)]
     qkv = jnp.concatenate(piece[:3], axis=1)
     qkv_ref[...] = qkv
     out_ref[...] = piece[3]
@@ -422,8 +479,16 @@
     )
 
 
-def exchange(blocks):
-    return lax.all_to_all(blocks, "pts", split_axis=0, concat_axis=0, tiled=True)
+def exchange(blocks, size):
+    order = [layer * PLANE + place for place in range(PLANE) for layer in range(LAYERS)]
+    return lax.all_to_all(
+        blocks,
+        "pts",
+        split_axis=0,
+        concat_axis=0,
+        tiled=True,
+        axis_index_groups=[order[start : start + size] for start in range(0, len(order), size)],
+    )
 
 
 def body(
@@ -474,7 +539,7 @@
         flops=1 << 30,
         in_specs=[pl.BlockSpec(memory_space=pltpu.HBM)] * len(arguments),
     )(*arguments)
-    arrived = exchange(outgoing).reshape(length, lanes)
+    arrived = exchange(outgoing, shards).reshape(length, lanes)
 
     both_ways, hilbert_rows, attended, probs = call(
         forward_kernel,
@@ -492,11 +557,24 @@
         ),
         flops=1 << 32,
     )(arrived, o_slot, qkv_t, out_weight, pool_t, gain, upstream_pool)
-    returned = exchange(both_ways)
-
-    last, pooled = call(
+    returned = exchange(both_ways, shards)
+
+    core = lax.axis_index("rep").astype(I32).reshape(1)
+    scalar = pl.BlockSpec(memory_space=pltpu.SMEM)
+    block = pl.BlockSpec(memory_space=pltpu.VMEM)
+    swap = [(0, 1), (1, 0)]
+
+    keep, give, pooled, grad_qkv, grad_mixed, normed, inverse_std = call(
         backward_kernel,
-        (shape((shards, per_peer, lanes), BF16), shape((2 * CHANNELS, clusters), BF16)),
+        (
+            shape((3 * CHANNELS, lanes), F32),
+            shape((3 * CHANNELS, lanes), F32),
+            shape((2 * CHANNELS, clusters), BF16),
+            shape((3 * CHANNELS, length), BF16),
+            shape((CHANNELS, length), BF16),
+            shape((CHANNELS, length), F32),
+            shape((1, length), F32),
+        ),
         scratch=(
             pltpu.VMEM((HEADS, length, CHANNELS), BF16),
             pltpu.VMEM((length, lanes), BF16),
@@ -508,7 +586,9 @@
             pltpu.VMEM((CHANNELS, length), F32),
         ),
         flops=1 << 33,
+        in_specs=[scalar] + [block] * 11,
     )(
+        core,
         returned,
         arrived,
         o_slot,
@@ -521,24 +601,19 @@
         attended,
         probs,
     )
-    final = exchange(last)
-
-    own = call(total_kernel, shape((per_peer, lanes), F32))(final)
-    other = lax.ppermute(own, "rep", [(0, 1), (1, 0)])
+    taken = lax.ppermute(give, "rep", swap)
+    back = call(input_grad_kernel, shape((length, lanes), BF16), flops=1 << 31)(
+        arrived, qkv_t, gain, grad_qkv, grad_mixed, normed, inverse_std
+    )
+    last = call(pack_kernel, shape((shards, per_peer, lanes), BF16))(back, keep, taken)
+    final = exchange(last, shards)
+
+    total = call(total_kernel, shape((GROUP, per_peer, lanes), BF16))(final)
+    gathered = exchange(total, GROUP).reshape(GROUP * per_peer, lanes)
+    other = lax.ppermute(gathered, "rep", swap)
     feat_grad = call(feat_grad_kernel, shape((CHANNELS, length), BF16), flops=1 << 28)(
         final.reshape(length, lanes), z_slot
     )
-    total = call(spread_kernel, shape((GROUP, per_peer, lanes), BF16))(own, other)
-    gathered = lax.all_to_all(
-        total,
-        "pts",
-        split_axis=0,
-        concat_axis=0,
-        tiled=True,
-        axis_index_groups=[
-            list(range(start, start + GROUP)) for start in range(0, shards, GROUP)
-        ],
-    ).reshape(GROUP * per_peer, lanes)
     factor = float(lax.axis_size("rep") * shards * length) ** (-0.5)
     qkv_total, out_total, pool_total, gain_total = call(
         functools.partial(finish_kernel, factor),
@@ -548,7 +623,8 @@
             shape((CHANNELS, lanes), F32),
             shape((1, CHANNELS), F32),
         ),
-    )(gathered, qkv_t, gain)
+        in_specs=[scalar] + [block] * 4,
+    )(core, gathered, other, qkv_t, gain)
     return (
         pooled[None],
         feat_grad[None],

time: 115 us -> 124 us (1.078)
  blocking collectives: 73 us -> 61.7 us
  waiting for transfers between devices: 9.47 us -> 18.3 us
  local copies, waits for them, and re-layouts: 0 us -> 6.61 us
  starting transfers between devices: 8.61 us -> 13 us
    all_to_all x3, blocking collectives: 73 us -> 61.7 us  [exchange(): lax.all_to_all(blocks, 'pts', split_axis=0, concat_axis=0, tiled=True, ax...]
    all_to_all x1, waiting for transfers between devices: 8.64 us -> 18.2 us  [exchange(): lax.all_to_all(blocks, 'pts', split_axis=0, concat_axis=0, tiled=True, ax...]
    unnamed x0 -> x4, local copies, waits for them, and re-layouts: none -> 6.61 us
    all_to_all x1, starting transfers between devices: 4.62 us -> 6.92 us  [exchange(): lax.all_to_all(blocks, 'pts', split_axis=0, concat_axis=0, tiled=True, ax...]
    ppermute x1 -> x2, starting transfers between devices: 3.99 us -> 6.08 us  [the longest x1 3.47 us: body(): taken = lax.ppermute(give, 'rep', swap)]
    pallas_call x3 -> x4, Pallas kernels: 10.4 us -> 9.95 us  [the longest x1 8.5 us: body(): call(backward_kernel, (shape((3 * CHANNELS, lanes), F32), shape((3 * CHAN...]
  transfers between devices with their start and end apart: 2 -> 3, of which waited for: 2 -> 1; matrix products, arithmetic and copies ran while one was open for 0% -> 0% of each run, Pallas kernels for 1% -> 2%
where the time goes in v6:
time: 124 us
  blocking collectives  61.7 us (50%)
  Pallas kernels  23.7 us (19%)
  waiting for transfers between devices  18.3 us (15%)
  starting transfers between devices  13 us (10%)
  local copies, waits for them, and re-layouts  6.61 us (5%)
    all_to_all x3, blocking collectives, exchange(): lax.all_to_all(blocks, 'pts', split_axis=0, concat_axis=0, tiled=True, ax...  61.7 us
    all_to_all x1, waiting for transfers between devices, exchange(): lax.all_to_all(blocks, 'pts', split_axis=0, concat_axis=0, tiled=True, ax...  18.2 us
    pallas_call x1, Pallas kernels, body(): call(forward_kernel, (shape((shards, 2 * per_peer, lanes), BF16), shape((...  8.87 us
    pallas_call x1, Pallas kernels, body(): call(backward_kernel, (shape((3 * CHANNELS, lanes), F32), shape((3 * CHAN...  8.5 us
    all_to_all x1, starting transfers between devices, exchange(): lax.all_to_all(blocks, 'pts', split_axis=0, concat_axis=0, tiled=True, ax...  6.92 us
    unnamed x4, local copies, waits for them, and re-layouts  6.61 us
    ppermute x1, starting transfers between devices, body(): taken = lax.ppermute(give, 'rep', swap)  3.47 us
    pallas_call x1, Pallas kernels, body(): call(send_kernel, (shape((shards, per_peer, lanes), BF16), shape((1, leng...  2.83 us
  transfers between devices with their start and end apart: 3, of which 1 were waited for; matrix products, arithmetic and copies ran while one was open for 0% of the time, Pallas kernels for 2%

profile of v6, /device:TPU:1, one launch (start us, length us, event | category | flops | bytes accessed | tf_op | source)
XLA Modules:
  0.0 124.0 jit_solution(13557809467232509279)
XLA Ops:
  0.6 2.8 %shard_map.136 = (bf16[128,8,128]{2,1,0:T(8,128)(2,1)S(1)}, s32[1,1024]{1,0:T(1,128)S(1)}, s32[1,1024]{1,0:T(1,128)S(1)}, bf16[128,256]{1,0:T(8,128)(2,1)S(1)}, ...) custom-call(s32[1,1024]{1,0:T(1,128)} %pos_hbm.1, ...), custom_call_target="tpu_custom_call" | custom-call | flops 1073741824 | bytes 1048576 | tf_op jit(solution)/shard_map/pallas_call | solution.py:529
  3.5 29.6 %all_to_all.20 = bf16[128,8,128]{2,1,0:T(8,128)(2,1)S(1)} all-to-all(bf16[128,8,128]{2,1,0:T(8,128)(2,1)S(1)} %get-tuple-element.29), channel_id=1, replica_groups={{0,32,64,96,128,160,192,224,2,34,66,98,130,162,194,226,4,36,68,100,132,..., dimensions={0} | all-to-all | bytes 524288 | tf_op jit(solution)/shard_map/all_to_all | solution.py:484
  33.1 8.9 %shard_map.137 = (bf16[128,16,128]{2,1,0:T(8,128)(2,1)}, bf16[64,1024]{1,0:T(8,128)(2,1)S(1)}, f32[64,1024]{1,0:T(8,128)S(1)}, bf16[4,1024,1024]{2,1,0:T(8,128)(2,1)S(1)}) custom-call(bf16[1024,128]{1,0:T(8,128)(2,1)S(1)} %bitcast.16, s32[1,1024]{1,0:T(1,128)S(1)} %get-tuple-element.30.o_slot_ref, bf16[64,192]{1,0:T(8,128)(2,1)S(1)} %get-tuple-element.31.qkv_t_ref, ...), custom_call_target="tpu_custom_call" | custom-call | flops 4294967296 | bytes 1048576 | tf_op jit(solution)/shard_map/pallas_call | solution.py:544
  41.9 0.0 copy-start
  41.9 3.2 %copy-done = bf16[4,1024,1024]{2,1,0:T(8,128)(2,1)} copy-done((bf16[4,1024,1024]{2,1,0:T(8,128)(2,1)}, bf16[4,1024,1024]{2,1,0:T(8,128)(2,1)S(1)}, u32[]{:S(2)}) %copy-start) | copy-done | bytes 8388632
  45.2 6.9 %all-to-all-start.1 = ((bf16[128,16,128]{2,1,0:T(8,128)(2,1)}), bf16[128,16,128]{2,1,0:T(8,128)(2,1)S(1)}, u32[]{:S(2)}, u32[]{:S(2)}) async-start(bf16[128,16,128]{2,1,0:T(8,128)(2,1)} %get-tuple-element.36), calls=%async_computation.1 | async-start | bytes 1048576 | tf_op jit(solution)/shard_map/all_to_all | solution.py:484
  52.1 18.2 %all-to-all-done.1.returned_ref = bf16[128,16,128]{2,1,0:T(8,128)(2,1)S(1)} async-done(((bf16[128,16,128]{2,1,0:T(8,128)(2,1)}), bf16[128,16,128]{2,1,0:T(8,128)(2,1)S(1)}, u32[]{:S(2)}, u32[]{:S(2)}) %all-to-all-start.1) | async-done | bytes 524320 | tf_op jit(solution)/shard_map/all_to_all | solution.py:484
  70.3 0.0 copy-start.1
  70.3 3.4 %copy-done.1 = bf16[4,1024,1024]{2,1,0:T(8,128)(2,1)S(1)} copy-done((bf16[4,1024,1024]{2,1,0:T(8,128)(2,1)S(1)}, bf16[4,1024,1024]{2,1,0:T(8,128)(2,1)}, u32[]{:S(2)}) %copy-start.1) | copy-done | bytes 8388632
  73.7 8.5 %shard_map.138 = (f32[192,128]{1,0:T(8,128)S(1)}, f32[192,128]{1,0:T(8,128)S(1)}, bf16[128,256]{1,0:T(8,128)(2,1)}, bf16[192,1024]{1,0:T(8,128)(2,1)S(1)}, bf16[...) custom-call(s32[1]{0:T(128)} %bitcast.core_ref, ...), custom_call_target="tpu_custom_call" | custom-call | flops 8589934592 | bytes 1048576 | tf_op jit(solution)/shard_map/pallas_call | solution.py:567
  82.2 3.5 %collective-permute-start = (f32[192,128]{1,0:T(8,128)S(1)}, f32[192,128]{1,0:T(8,128)S(1)}, u32[]{:S(2)}, u32[]{:S(2)}) collective-permute-start(f32[192,128]{1,0:T(8,128)S(1)} %get-tuple-element.46), channel_id=1, source_target_pairs={{0,1},{1,0},{2,3},{3,2},{4,5},{5,4},{6,7},{7,6},{8,9},{9,8},{10,11... | collective-permute-start | bytes 294920 | tf_op jit(solution)/shard_map/ppermute | solution.py:604
  85.7 1.2 shard_map.139.back_ref
  86.9 0.0 collective-permute-done.other_ref
  87.0 20.3 %all_to_all.21.arrived_ref = bf16[128,8,128]{2,1,0:T(8,128)(2,1)S(1)} all-to-all(bf16[128,8,128]{2,1,0:T(8,128)(2,1)S(1)} %shard_map.140), channel_id=1, replica_groups={{0,32,64,96,128,160,192,224,2,34,66,98,130,162,194,226,4,36,68,100,132,..., dimensions={0} | all-to-all | bytes 524288 | tf_op jit(solution)/shard_map/all_to_all | solution.py:484
  107.2 0.2 shard_map.142
  107.4 11.9 %all_to_all.22 = bf16[32,8,128]{2,1,0:T(8,128)(2,1)S(1)} all-to-all(bf16[32,8,128]{2,1,0:T(8,128)(2,1)S(1)} %shard_map.142), channel_id=1, replica_groups={{0,32,64,96,128,160,192,224,2,34,66,98,130,162,194,226,4,36,68,100,132,..., dimensions={0} | all-to-all | bytes 131072 | tf_op jit(solution)/shard_map/all_to_all | solution.py:484
  119.3 2.6 %collective-permute-start.1 = (bf16[256,128]{1,0:T(8,128)(2,1)S(1)}, bf16[256,128]{1,0:T(8,128)(2,1)S(1)}, u32[]{:S(2)}, u32[]{:S(2)}) collective-permute-start(bf16[256,128]{1,0:T(8,128)(2,1)S(1)} %bitcast.19), channel_id=1, source_target_pairs={{0,1},{1,0},{2,3},{3,2},{4,5},{5,4},{6,7},{7,6},{8,9},{9,8},{10,11... | collective-permute-start | bytes 196616 | tf_op jit(solution)/shard_map/ppermute | solution.py:613
  121.9 1.2 shard_map.141
  123.2 0.0 collective-permute-done.1.other_ref
  123.2 0.9 shard_map.143
  (1 shorter events, 0.0 us)
Async XLA Ops:
  41.9 3.2 %copy-start = (bf16[4,1024,1024]{2,1,0:T(8,128)(2,1)}, bf16[4,1024,1024]{2,1,0:T(8,128)(2,1)S(1)}, u32[]{:S(2)}) copy-start(bf16[4,1024,1024]{2,1,0:T(8,128)(2,1)S(1)} %get-tuple-element.39.probs_ref) | copy-start | bytes 25165828
  45.2 25.2 %all-to-all-start.1 = ((bf16[128,16,128]{2,1,0:T(8,128)(2,1)}), bf16[128,16,128]{2,1,0:T(8,128)(2,1)S(1)}, u32[]{:S(2)}, u32[]{:S(2)}) async-start(bf16[128,16,128]{2,1,0:T(8,128)(2,1)} %get-tuple-element.36), calls=%async_computation.1 | async-start | bytes 1048576 | tf_op jit(solution)/shard_map/all_to_all | solution.py:484
  70.3 3.4 %copy-start.1 = (bf16[4,1024,1024]{2,1,0:T(8,128)(2,1)S(1)}, bf16[4,1024,1024]{2,1,0:T(8,128)(2,1)}, u32[]{:S(2)}) copy-start(bf16[4,1024,1024]{2,1,0:T(8,128)(2,1)} %copy-done) | copy-start | bytes 25165828
  82.2 4.7 %collective-permute-start = (f32[192,128]{1,0:T(8,128)S(1)}, f32[192,128]{1,0:T(8,128)S(1)}, u32[]{:S(2)}, u32[]{:S(2)}) collective-permute-start(f32[192,128]{1,0:T(8,128)S(1)} %get-tuple-element.46), channel_id=1, source_target_pairs={{0,1},{1,0},{2,3},{3,2},{4,5},{5,4},{6,7},{7,6},{8,9},{9,8},{10,11... | collective-permute-start | bytes 294920 | tf_op jit(solution)/shard_map/ppermute | solution.py:604
  119.3 3.8 %collective-permute-start.1 = (bf16[256,128]{1,0:T(8,128)(2,1)S(1)}, bf16[256,128]{1,0:T(8,128)(2,1)S(1)}, u32[]{:S(2)}, u32[]{:S(2)}) collective-permute-start(bf16[256,128]{1,0:T(8,128)(2,1)S(1)} %bitcast.19), channel_id=1, source_target_pairs={{0,1},{1,0},{2,3},{3,2},{4,5},{5,4},{6,7},{7,6},{8,9},{9,8},{10,11... | collective-permute-start | bytes 196616 | tf_op jit(solution)/shard_map/ppermute | solution.py:613

commit v7 on v4

--- a/solution.py
+++ b/solution.py
@@ -176,51 +176,80 @@
     gain_ref,
     pool_grad_ref,
     out_ref,
-    hilbert_ref,
     attended_ref,
     probs_ref,
+    slot_map_ref,
+    hidden_ref,
+    normed_ref,
+    inverse_std_ref,
     query_ref,
     key_ref,
     value_ref,
-    rows_ref,
+    query_rows_ref,
 ):
     shards = out_ref.shape[0]
     length = arrived_ref.shape[0]
     clusters = pool_grad_ref.shape[1]
+    per_peer = length // shards
     arrived = arrived_ref[...]
     place, first_cell, second_cell = arrived_columns(arrived)
-    first = on_columns(first_cell, clusters)
-    second = on_columns(second_cell, clusters)
-    denom = cluster_counts(first, second)
-    grad_mean = (dot(pool_t_ref[...], pool_grad_ref[...]) / denom).astype(BF16)
-    blank = jnp.zeros_like(grad_mean)
-    back = dot_nt(first, jnp.concatenate([grad_mean, blank], axis=0))
-    back = back + dot_nt(second, jnp.concatenate([blank, grad_mean], axis=0))
-    per_peer = length // shards
-    out_ref[:, per_peer:, :] = back.astype(BF16).reshape(shards, per_peer, 2 * CHANNELS)
     turned_rows = turned(arrived)[:CHANNELS].astype(BF16)
     floats = dot(turned_rows, on_columns(place, length))
-    hilbert_ref[...] = floats.astype(BF16)
-    _, _, hidden = layer_norm(floats, gain_column(gain_ref))
+    normed, inverse_std, hidden = layer_norm(floats, gain_column(gain_ref))
     qkv = dot_tn(qkv_t_ref[...], hidden).astype(BF16)
-    query_ref[...] = (turned(qkv[:CHANNELS]) * HEAD_DIM ** (-0.5)).astype(BF16)
+    query_rows_ref[...] = (turned(qkv[:CHANNELS]) * HEAD_DIM ** (-0.5)).astype(BF16)
     key_ref[...] = qkv[CHANNELS : 2 * CHANNELS]
-    values = turned(qkv[2 * CHANNELS :])
-    for head in range(HEADS):
-        mask = head_lanes((length, CHANNELS), head)
-        value_ref[head] = jnp.where(mask, values, 0.0).astype(BF16)
+    value_ref[:CHANNELS, :] = qkv[2 * CHANNELS :]
+    value_ref[CHANNELS:, :] = jnp.ones((CHANNELS, length), BF16)
+    half_slot = lax.shift_right_logical(o_slot_ref[...], 1)
+    kept = {}
+
+    def cluster_grads():
+        first = on_columns(first_cell, clusters)
+        second = on_columns(second_cell, clusters)
+        denom = cluster_counts(first, second)
+        grad_mean = (dot(pool_t_ref[...], pool_grad_ref[...]) / denom).astype(BF16)
+        blank = jnp.zeros_like(grad_mean)
+        kept["cells"] = (first, second)
+        kept["means"] = (
+            jnp.concatenate([grad_mean, blank], axis=0),
+            jnp.concatenate([blank, grad_mean], axis=0),
+        )
+
+    def send_back(start, count):
+        first, second = (one[start : start + count] for one in kept["cells"])
+        back = dot_nt(first, kept["means"][0]) + dot_nt(second, kept["means"][1])
+        peers = slice(start // per_peer, (start + count) // per_peer)
+        out_ref[peers, per_peer:, :] = back.astype(BF16).reshape(-1, per_peer, 2 * CHANNELS)
+
+    def map_slots(start, count):
+        rows = iota((count, length), 0) + start
+        slot_map_ref[start : start + count, :] = onehot(rows == half_slot)
+
+    def hand_over():
+        hidden_ref[...] = hidden
+        normed_ref[...] = normed
+        inverse_std_ref[...] = inverse_std
+        query_ref[...] = qkv[:CHANNELS]
+
+    chores = [hand_over, cluster_grads]
+    quarter = length // 4
+    chores += [functools.partial(send_back, k * quarter, quarter) for k in range(4)]
+    eighth = length // 8
+    chores += [functools.partial(map_slots, k * eighth, eighth) for k in range(8)]
 
     units = [(start, head) for start in range(0, length, CHUNK) for head in range(HEADS)]
 
     def scores(unit):
         start, head = unit
-        queries = query_ref[start : start + CHUNK, :].astype(F32)
+        queries = query_rows_ref[start : start + CHUNK, :].astype(F32)
         mask = head_lanes((CHUNK, CHANNELS), head)
         return dot(jnp.where(mask, queries, 0.0).astype(BF16), key_ref[...])
 
     def mix(unit):
         start, head = unit
-        return dot(probs_ref[head, start : start + CHUNK, :], value_ref[head])
+        own = slice(head * HEAD_DIM, (head + 1) * HEAD_DIM)
+        return dot_nt(value_ref[own, :], probs_ref[head, start : start + CHUNK, :])
 
     totals = []
     ready = scores(units[0])
@@ -230,20 +259,22 @@
             ready = scores(units[number + 1])
         if number > 0:
             totals.append(mix(units[number - 1]))
+        if number < len(chores):
+            chores[number]()
         weights = jnp.exp(now)
         share = 1.0 / jnp.sum(weights, axis=1, keepdims=True)
         probs_ref[head, start : start + CHUNK, :] = (weights * share).astype(BF16)
     totals.append(mix(units[-1]))
     for number in range(0, len(units), HEADS):
         start = units[number][0]
-        rows_ref[start : start + CHUNK, :] = sum(totals[number : number + HEADS])
-    attended = rows_ref[...].T
-    attended_ref[...] = attended
+        attended_ref[:, start : start + CHUNK] = jnp.concatenate(
+            totals[number : number + HEADS], axis=0
+        )
+    attended = attended_ref[...]
     mixed = (floats + dot(out_w_ref[...], attended.astype(BF16))).astype(BF16).astype(F32)
-    o_slot = o_slot_ref[...]
-    odd = lax.bitwise_and(o_slot, 1) == 1
+    odd = lax.bitwise_and(o_slot_ref[...], 1) == 1
     pair = jnp.concatenate([jnp.where(odd, 0.0, mixed), jnp.where(odd, mixed, 0.0)], axis=0)
-    picked = dot_nt(on_rows(lax.shift_right_logical(o_slot, 1), length), pair.astype(BF16))
+    picked = dot_nt(slot_map_ref[...], pair.astype(BF16))
     out_ref[:, :per_peer, :] = picked.astype(BF16).reshape(shards, per_peer, 2 * CHANNELS)
 
 
@@ -256,60 +287,35 @@
     pool_t_ref,
     gain_ref,
     pool_grad_ref,
-    hilbert_ref,
     attended_ref,
     probs_ref,
+    slot_map_ref,
+    hidden_ref,
+    normed_ref,
+    inverse_std_ref,
+    query_ref,
+    key_ref,
+    value_ref,
     out_ref,
     pooled_ref,
-    key_rows_ref,
     upstream_ref,
-    value_ref,
-    query_ref,
     grad_out_ref,
     grad_query_ref,
     grad_key_ref,
     grad_value_ref,
+    place_ref,
 ):
     shards = out_ref.shape[0]
     length = arrived_ref.shape[0]
     clusters = pool_grad_ref.shape[1]
     per_peer = length // shards
-    place, first_cell, second_cell = arrived_columns(arrived_ref[...])
     blank = jnp.zeros((CHANNELS, length), BF16)
-    blank_clusters = jnp.zeros((CHANNELS, clusters), BF16)
-
-    first = on_columns(first_cell, clusters)
-    second = on_columns(second_cell, clusters)
-    denom = cluster_counts(first, second)
-    mixed_rows = turned(returned_ref[:, :per_peer, :].reshape(length, 2 * CHANNELS)).astype(BF16)
-    sums = dot(mixed_rows[:CHANNELS], first) + dot(mixed_rows[CHANNELS:], second)
-    pooled_mean = (sums / denom).astype(BF16)
-    pooled_ref[...] = dot_tn(pool_t_ref[...], pooled_mean).astype(BF16)
-    pool_parts = [
-        dot_nt(pooled_mean, jnp.concatenate([blank_clusters, half], axis=0))
-        for half in (pool_grad_ref[:CHANNELS, :], pool_grad_ref[CHANNELS:, :])
-    ]
-
-    gain = gain_column(gain_ref)
-    normed, inverse_std, hidden = layer_norm(hilbert_ref[...].astype(F32), gain)
-    qkv = dot_tn(qkv_t_ref[...], hidden).astype(BF16)
-    query_ref[...] = qkv[:CHANNELS]
-    key_rows = turned(qkv[CHANNELS : 2 * CHANNELS])
-    for head in range(HEADS):
-        mask = head_lanes((length, CHANNELS), head)
-        key_rows_ref[head] = jnp.where(mask, key_rows, 0.0).astype(BF16)
-    value_ref[:CHANNELS, :] = qkv[2 * CHANNELS :]
-    value_ref[CHANNELS:, :] = jnp.ones((CHANNELS, length), BF16)
-
-    o_slot = o_slot_ref[...]
-    odd = lax.bitwise_and(o_slot, 1) == 1
+    odd = lax.bitwise_and(o_slot_ref[...], 1) == 1
     slots = turned(returned_ref[:, per_peer:, :].reshape(length, 2 * CHANNELS)).astype(BF16)
-    both = dot(slots, on_rows(lax.shift_right_logical(o_slot, 1), length))
+    both = dot(slots, slot_map_ref[...])
     grad_mixed = jnp.where(odd, both[CHANNELS:], both[:CHANNELS])
     grad_mixed_low = grad_mixed.astype(BF16)
     attended = attended_ref[...]
-    attended_low = attended.astype(BF16)
-    out_part = dot_nt(grad_mixed_low, jnp.concatenate([blank, attended_low], axis=0))
     grad_attended = dot_tn(out_w_ref[...], grad_mixed_low).astype(BF16)
     grad_out_ref[...] = grad_attended
     scaled = grad_attended.astype(F32) * HEAD_DIM ** (-0.5)
@@ -319,8 +325,37 @@
         [delta_high, delta - delta_high, jnp.zeros((CHANNELS - 2 * HEADS, length), F32)], axis=0
     )
     upstream_ref[...] = jnp.concatenate([scaled, rest], axis=0).T.astype(BF16)
-    grad_key_ref[...] = jnp.zeros_like(grad_key_ref)
-    grad_value_ref[...] = jnp.zeros_like(grad_value_ref)
+    place, first_cell, second_cell = arrived_columns(arrived_ref[...])
+    kept = {}
+
+    def cells():
+        kept["cells"] = (on_columns(first_cell, clusters), on_columns(second_cell, clusters))
+        kept["denom"] = cluster_counts(*kept["cells"])
+
+    def pool():
+        rows = turned(returned_ref[:, :per_peer, :].reshape(length, 2 * CHANNELS)).astype(BF16)
+        first, second = kept["cells"]
+        sums = dot(rows[:CHANNELS], first) + dot(rows[CHANNELS:], second)
+        kept["mean"] = (sums / kept["denom"]).astype(BF16)
+
+    def pool_out():
+        pooled_ref[...] = dot_tn(pool_t_ref[...], kept["mean"]).astype(BF16)
+        empty = jnp.zeros((CHANNELS, clusters), BF16)
+        kept["pool"] = [
+            dot_nt(kept["mean"], jnp.concatenate([empty, half], axis=0))
+            for half in (pool_grad_ref[:CHANNELS, :], pool_grad_ref[CHANNELS:, :])
+        ]
+
+    def out_grad():
+        attended_low = attended.astype(BF16)
+        kept["out"] = dot_nt(grad_mixed_low, jnp.concatenate([blank, attended_low], axis=0))
+
+    def map_places(start, count):
+        place_ref[start : start + count, :] = on_columns(place[start : start + count], length)
+
+    chores = [cells, pool, pool_out, out_grad]
+    eighth = length // 8
+    chores += [functools.partial(map_places, k * eighth, eighth) for k in range(8)]
 
     units = [(start, head) for start in range(0, length, CHUNK) for head in range(HEADS)]
     lane = iota((CHUNK, 2 * CHANNELS), 1)
@@ -343,31 +378,43 @@
         now = ready
         if number + 1 < len(units):
             ready = change(units[number + 1])
+        if number < len(chores):
+            chores[number]()
         probs = probs_ref[head, rows, :]
-        grad_value_ref[own, :] += dot(grad_out_ref[own, rows], probs)
+        more_values = dot(grad_out_ref[own, rows], probs)
         grad_scores = (probs.astype(F32) * now).astype(BF16)
-        totals.append(dot(grad_scores, key_rows_ref[head]))
-        grad_key_ref[own, :] += dot(query_ref[own, rows], grad_scores)
+        totals.append(dot_nt(key_ref[own, :], grad_scores))
+        more_keys = dot(query_ref[own, rows], grad_scores)
+        if start == 0:
+            grad_value_ref[own, :] = more_values
+            grad_key_ref[own, :] = more_keys
+        else:
+            grad_value_ref[own, :] += more_values
+            grad_key_ref[own, :] += more_keys
     for number in range(0, len(units), HEADS):
         start = units[number][0]
-        grad_query_ref[start : start + CHUNK, :] = sum(totals[number : number + HEADS])
+        grad_query_ref[:, start : start + CHUNK] = jnp.concatenate(
+            totals[number : number + HEADS], axis=0
+        )
     grad_qkv = jnp.concatenate(
-        [grad_query_ref[...].T, grad_key_ref[...], grad_value_ref[...]], axis=0
+        [grad_query_ref[...], grad_key_ref[...], grad_value_ref[...]], axis=0
     ).astype(BF16)
+    grad_hidden = dot(qkv_t_ref[...], grad_qkv)
+    hidden = hidden_ref[...]
+    normed = normed_ref[...]
     qkv_parts = [
         dot_nt(hidden, jnp.concatenate([blank, grad_qkv[start : start + CHANNELS]], axis=0))
         for start in (0, CHANNELS, 2 * CHANNELS)
     ]
-    grad_hidden = dot(qkv_t_ref[...], grad_qkv)
-    grad_normed = grad_hidden * gain
-    grad_norm_in = inverse_std * (
+    grad_normed = grad_hidden * gain_column(gain_ref)
+    grad_norm_in = inverse_std_ref[...] * (
         grad_normed
         - jnp.mean(grad_normed, axis=0, keepdims=True)
         - normed * jnp.mean(grad_normed * normed, axis=0, keepdims=True)
     )
     grad_rows = (grad_mixed + grad_norm_in).astype(BF16)
-    back = dot_nt(on_columns(place, length), jnp.concatenate([grad_rows, blank], axis=0))
-    parts = qkv_parts + [out_part] + pool_parts
+    back = dot_nt(place_ref[...], jnp.concatenate([grad_rows, blank], axis=0))
+    parts = qkv_parts + [kept["out"]] + kept["pool"]
     unused = jnp.zeros((GROUP * per_peer - len(parts) * CHANNELS, 2 * CHANNELS), F32)
     side = jnp.concatenate(parts + [unused], axis=0)
     span = GROUP * per_peer
@@ -394,7 +441,16 @@
     out_ref[...] = dot(rows, on_rows(z_slot_ref[...], length)).astype(BF16)
 
 
-def finish_kernel(factor, total_ref, qkv_t_ref, gain_in_ref, qkv_ref, out_ref, pool_ref, gain_ref):
+def finish_kernel(
+    factor,
+    total_ref,
+    qkv_t_ref,
+    gain_in_ref,
+    qkv_ref,
+    out_ref,
+    pool_ref,
+    gain_ref,
+):
     both = total_ref[...].astype(F32)
     both = (both[:, CHANNELS:] + both[:, :CHANNELS]) * factor
     piece = [both[k * CHANNELS : (k + 1) * CHANNELS] for k in range(6)]
@@ -476,20 +532,21 @@
     )(*arguments)
     arrived = exchange(outgoing).reshape(length, lanes)
 
-    both_ways, hilbert_rows, attended, probs = call(
+    both_ways, *saved = call(
         forward_kernel,
         (
             shape((shards, 2 * per_peer, lanes), BF16),
+            shape((CHANNELS, length), F32),
+            shape((HEADS, length, length), BF16),
+            shape((length, length), BF16),
             shape((CHANNELS, length), BF16),
             shape((CHANNELS, length), F32),
-            shape((HEADS, length, length), BF16),
+            shape((1, length), F32),
+            shape((CHANNELS, length), BF16),
+            shape((CHANNELS, length), BF16),
+            shape((lanes, length), BF16),
         ),
-        scratch=(
-            pltpu.VMEM((length, CHANNELS), BF16),
-            pltpu.VMEM((CHANNELS, length), BF16),
-            pltpu.VMEM((HEADS, length, CHANNELS), BF16),
-            pltpu.VMEM((length, CHANNELS), F32),
-        ),
+        scratch=(pltpu.VMEM((length, CHANNELS), BF16),),
         flops=1 << 32,
     )(arrived, o_slot, qkv_t, out_weight, pool_t, gain, upstream_pool)
     returned = exchange(both_ways)
@@ -498,14 +555,12 @@
         backward_kernel,
         (shape((shards, per_peer, lanes), BF16), shape((2 * CHANNELS, clusters), BF16)),
         scratch=(
-            pltpu.VMEM((HEADS, length, CHANNELS), BF16),
             pltpu.VMEM((length, lanes), BF16),
-            pltpu.VMEM((lanes, length), BF16),
             pltpu.VMEM((CHANNELS, length), BF16),
-            pltpu.VMEM((CHANNELS, length), BF16),
-            pltpu.VMEM((length, CHANNELS), F32),
             pltpu.VMEM((CHANNELS, length), F32),
             pltpu.VMEM((CHANNELS, length), F32),
+            pltpu.VMEM((CHANNELS, length), F32),
+            pltpu.VMEM((length, length), BF16),
         ),
         flops=1 << 33,
     )(
@@ -517,17 +572,16 @@
         pool_t,
         gain,
         upstream_pool,
-        hilbert_rows,
-        attended,
-        probs,
+        *saved,
     )
     final = exchange(last)
 
     own = call(total_kernel, shape((per_peer, lanes), F32))(final)
     other = lax.ppermute(own, "rep", [(0, 1), (1, 0)])
-    feat_grad = call(feat_grad_kernel, shape((CHANNELS, length), BF16), flops=1 << 28)(
+    feat_grad = call(feat_grad_kernel, shape((CHANNELS, length), BF16), flops=1 << 30)(
         final.reshape(length, lanes), z_slot
     )
+    other, feat_grad = lax.optimization_barrier((other, feat_grad))
     total = call(spread_kernel, shape((GROUP, per_peer, lanes), BF16))(own, other)
     gathered = lax.all_to_all(
         total,

time: 115 us -> 113 us (0.983)
  blocking collectives: 73 us -> 86.5 us
  waiting for transfers between devices: 9.47 us -> 0.01 us
  starting transfers between devices: 8.61 us -> 4.06 us
  Pallas kernels: 23.3 us -> 21.3 us
    all_to_all x0 -> x1, blocking collectives: none -> 14 us  [body(): lax.all_to_all(total, 'pts', split_axis=0, concat_axis=0, tiled=True, axi...]
    all_to_all x1 -> x0, waiting for transfers between devices: 8.64 us -> none  [body(): lax.all_to_all(total, 'pts', split_axis=0, concat_axis=0, tiled=True, axi...]
    all_to_all x1 -> x0, starting transfers between devices: 4.62 us -> none  [body(): lax.all_to_all(total, 'pts', split_axis=0, concat_axis=0, tiled=True, axi...]
  transfers between devices with their start and end apart: 2 -> 1, of which waited for: 2 -> 0; matrix products, arithmetic and copies ran while one was open for 0% -> 0% of each run, Pallas kernels for 1% -> 1%
where the time goes in v7:
time: 113 us
  blocking collectives  86.5 us (77%)
  Pallas kernels  21.3 us (19%)
  starting transfers between devices  4.06 us (4%)
    all_to_all x3, blocking collectives, exchange(): lax.all_to_all(blocks, 'pts', split_axis=0, concat_axis=0, tiled=True)  72.5 us
    all_to_all x1, blocking collectives, body(): lax.all_to_all(total, 'pts', split_axis=0, concat_axis=0, tiled=True, axi...  14 us
    pallas_call x1, Pallas kernels, body(): call(backward_kernel, (shape((shards, per_peer, lanes), BF16), shape((2 *...  8.9 us
    pallas_call x1, Pallas kernels, body(): call(forward_kernel, (shape((shards, 2 * per_peer, lanes), BF16), shape((...  7.22 us
    ppermute x1, starting transfers between devices, body(): other = lax.ppermute(own, 'rep', [(0, 1), (1, 0)])  4.06 us
    pallas_call x1, Pallas kernels, body(): call(send_kernel, (shape((shards, per_peer, lanes), BF16), shape((1, leng...  2.83 us
  transfers between devices with their start and end apart: 1, of which 0 were waited for; matrix products, arithmetic and copies ran while one was open for 0% of the time, Pallas kernels for 1%

profile of v7, /device:TPU:1, one launch (start us, length us, event | category | flops | bytes accessed | tf_op | source)
XLA Modules:
  0.0 112.5 jit_solution(9894972255248539178)
XLA Ops:
  0.6 2.8 %shard_map.136 = (bf16[128,8,128]{2,1,0:T(8,128)(2,1)S(1)}, s32[1,1024]{1,0:T(1,128)S(1)}, s32[1,1024]{1,0:T(1,128)S(1)}, bf16[128,256]{1,0:T(8,128)(2,1)S(1)}, ...) custom-call(s32[1,1024]{1,0:T(1,128)} %pos_hbm.1, ...), custom_call_target="tpu_custom_call" | custom-call | flops 1073741824 | bytes 1048576 | tf_op jit(solution)/shard_map/pallas_call | solution.py:520
  3.5 29.4 %all_to_all.20 = bf16[128,8,128]{2,1,0:T(8,128)(2,1)S(1)} all-to-all(bf16[128,8,128]{2,1,0:T(8,128)(2,1)S(1)} %get-tuple-element.32), channel_id=1, replica_groups=mesh['pts'=128,'rep'=2] {'pts'}, dimensions={0} | all-to-all | bytes 524288 | tf_op jit(solution)/shard_map/all_to_all | solution.py:482
  32.9 7.2 %shard_map.137 = (bf16[128,16,128]{2,1,0:T(8,128)(2,1)S(1)}, f32[64,1024]{1,0:T(8,128)S(1)}, bf16[4,1024,1024]{2,1,0:T(8,128)(2,1)S(1)}, bf16[1024,1024]{1,0:T(8...) custom-call(bf16[1024,128]{1,0:T(8,128)(2,1)S(1)} %bitcast.16, ...), custom_call_target="tpu_custom_call" | custom-call | flops 4294967296 | bytes 1048576 | tf_op jit(solution)/shard_map/pallas_call | solution.py:535
  40.1 23.4 %all_to_all.21.returned_ref = bf16[128,16,128]{2,1,0:T(8,128)(2,1)S(1)} all-to-all(bf16[128,16,128]{2,1,0:T(8,128)(2,1)S(1)} %get-tuple-element.39), channel_id=1, replica_groups=mesh['pts'=128,'rep'=2] {'pts'}, dimensions={0} | all-to-all | bytes 1048576 | tf_op jit(solution)/shard_map/all_to_all | solution.py:482
  63.5 8.9 %shard_map.138 = (bf16[128,8,128]{2,1,0:T(8,128)(2,1)S(1)}, bf16[128,256]{1,0:T(8,128)(2,1)}) custom-call(bf16[128,16,128]{2,1,0:T(8,128)(2,1)S(1)} %all_to_all.21.returned_ref, bf16[1024,128]{1,0:T(8,128)(2,1)S(1)} %bitcast.17, s32[1,1024]{1,0:T(1,128)S(1)} %get-tuple-element.33.o_slot_ref, bf16[64,192]{1,0:T(8,128)(2,1)S(1)} %get-tuple-element.34.qkv_t_ref, ...), custom_call_target="tpu_custom_call" | custom-call | flops 8589934592 | bytes 1048576 | tf_op jit(solution)/shard_map/pallas_call | solution.py:554
  72.4 19.7 %all_to_all.22.arrived_ref = bf16[128,8,128]{2,1,0:T(8,128)(2,1)S(1)} all-to-all(bf16[128,8,128]{2,1,0:T(8,128)(2,1)S(1)} %get-tuple-element.50), channel_id=1, replica_groups=mesh['pts'=128,'rep'=2] {'pts'}, dimensions={0} | all-to-all | bytes 524288 | tf_op jit(solution)/shard_map/all_to_all | solution.py:482
  92.1 0.1 shard_map.139.own_ref
  92.3 4.1 %collective-permute-start = (f32[8,128]{1,0:T(8,128)S(1)}, f32[8,128]{1,0:T(8,128)S(1)}, u32[]{:S(2)}, u32[]{:S(2)}) collective-permute-start(f32[8,128]{1,0:T(8,128)S(1)} %shard_map.139.own_ref), channel_id=1, source_target_pairs={{0,1},{1,0},{2,3},{3,2},{4,5},{5,4},{6,7},{7,6},{8,9},{9,8},{10,11... | collective-permute-start | bytes 12296 | tf_op jit(solution)/shard_map/ppermute | solution.py:580
  96.3 1.2 %shard_map.140 = bf16[64,1024]{1,0:T(8,128)(2,1)} custom-call(bf16[1024,128]{1,0:T(8,128)(2,1)S(1)} %bitcast.14, s32[1,1024]{1,0:T(1,128)S(1)} %get-tuple-element.51.z_slot_ref), custom_call_target="tpu_custom_call" | custom-call | flops 1073741824 | bytes 1048576 | tf_op jit(solution)/shard_map/pallas_call | solution.py:581
  97.6 0.0 collective-permute-done.other_ref
  97.6 0.1 shard_map.141
  97.7 14.0 %all_to_all.23 = bf16[64,8,128]{2,1,0:T(8,128)(2,1)S(1)} all-to-all(bf16[64,8,128]{2,1,0:T(8,128)(2,1)S(1)} %shard_map.141), channel_id=1, replica_groups={{0,2,4,6,8,10,12,14,16,18,20,22,24,26,28,30,32,34,36,38,40,42,44,46,48,..., dimensions={0} | all-to-all | bytes 262144 | tf_op jit(solution)/shard_map/all_to_all | solution.py:586
  111.7 0.9 shard_map.142
Async XLA Ops:
  92.3 5.3 %collective-permute-start = (f32[8,128]{1,0:T(8,128)S(1)}, f32[8,128]{1,0:T(8,128)S(1)}, u32[]{:S(2)}, u32[]{:S(2)}) collective-permute-start(f32[8,128]{1,0:T(8,128)S(1)} %shard_map.139.own_ref), channel_id=1, source_target_pairs={{0,1},{1,0},{2,3},{3,2},{4,5},{5,4},{6,7},{7,6},{8,9},{9,8},{10,11... | collective-permute-start | bytes 12296 | tf_op jit(solution)/shard_map/ppermute | solution.py:580

commit v8 on v7

--- a/solution.py
+++ b/solution.py
@@ -12,6 +12,9 @@
 CHANNELS = 64
 NORM_EPS = 1e-05
 CHUNK = 256
+AHEAD = 1
+LAG = 2
+LATE = 0
 GROUP = 64
 
 F32 = jnp.float32
@@ -55,14 +58,14 @@
     length = groups.shape[1]
     member = on_rows(groups, count)
     upto = onehot(iota((128, 128), 0) <= iota((128, 128), 1))
-    seen = jnp.zeros((count, 1), F32)
+    entry, block = iota((length, 128), 0), iota((length, 128), 1)
+    seen = dot(member, onehot(lax.shift_right_logical(entry, 7) < block))
     ranks = []
-    for start in range(0, length, 128):
-        block = member[:, start : start + 128]
-        running = dot(block, upto) + seen
-        seen = running[:, 127:128]
-        ranks.append(jnp.sum(block.astype(F32) * running, axis=0, keepdims=True) - 1.0)
-    return jnp.concatenate(ranks, axis=1).astype(I32)
+    for number in range(length // 128):
+        part = member[:, number * 128 : (number + 1) * 128]
+        running = dot(part, upto) + seen[:, number : number + 1]
+        ranks.append(jnp.sum(part.astype(F32) * running, axis=0, keepdims=True) - 1.0)
+    return jnp.concatenate(ranks, axis=1).astype(I32), member
 
 
 def send_kernel(
@@ -117,8 +120,10 @@
     shift = length.bit_length() - 1
     target = lax.shift_right_logical(positions, shift)
     local = lax.bitwise_and(positions, length - 1)
-    z_slot = target * per_peer + rank_in_group(target, shards)
-    o_slot = owners * (2 * per_peer) + rank_in_group(owners, shards)
+    z_rank, _ = rank_in_group(target, shards)
+    o_rank, owned = rank_in_group(owners, shards)
+    z_slot = target * per_peer + z_rank
+    o_slot = owners * (2 * per_peer) + o_rank
     z_slot_ref[...] = z_slot
     o_slot_ref[...] = o_slot
     row = iota((CHANNELS, length), 0)
@@ -126,13 +131,20 @@
     low = lax.bitwise_and(local, 31).astype(F32)
     place = jnp.where(row == 0, high, jnp.where(row == 1, low, 0.0)).astype(BF16)
     cell = (cell_ref[...] + 1).astype(F32)
-    odd = lax.bitwise_and(o_slot, 1)
-    cells = jnp.where(row - 2 == odd, cell, 0.0).astype(BF16)
+    rank = iota((2 * per_peer, length), 0)
+    cells = dot_nt(owned, jnp.where(rank == o_rank, cell, 0.0).astype(BF16)).astype(BF16)
+    peer = lax.shift_right_logical(iota((length, shards), 0), per_peer.bit_length() - 1)
+    listed = dot(onehot(peer == iota((length, shards), 1)), cells)
+    row = iota(listed.shape, 0)
+    place_in_list = iota(listed.shape, 1)
+    mine = lax.shift_right_logical(place_in_list, 1) == lax.bitwise_and(row, per_peer - 1)
+    listed = jnp.where(mine, listed, 0.0).astype(BF16)
+    lane = iota((2 * per_peer, 2 * CHANNELS), 1)
+    parity = lax.bitwise_and(iota((2 * per_peer, 2 * CHANNELS), 0), 1)
+    out = dot(listed, onehot(lane == parity + CHANNELS + 2))
     loads[3].wait()
     first = jnp.concatenate([feats_ref[...], place], axis=0)
-    second = jnp.concatenate([jnp.zeros((CHANNELS, length), BF16), cells], axis=0)
-    out = dot_nt(on_rows(z_slot, length), first)
-    out = out + dot_nt(on_rows(lax.shift_right_logical(o_slot, 1), length), second)
+    out = out + dot_nt(on_rows(z_slot, length), first)
     out_ref[...] = out.astype(BF16).reshape(out_ref.shape)
     for load in loads[4:]:
         load.wait()
@@ -161,10 +173,6 @@
     return jnp.maximum(
         jnp.sum(first.astype(F32) + second.astype(F32), axis=0, keepdims=True), 1.0
     )
-
-
-def head_lanes(shape, head):
-    return lax.shift_right_logical(iota(shape, 1), 4) == head
 
 
 def forward_kernel(
@@ -185,7 +193,7 @@
     query_ref,
     key_ref,
     value_ref,
-    query_rows_ref,
+    scaled_query_ref,
 ):
     shards = out_ref.shape[0]
     length = arrived_ref.shape[0]
@@ -193,14 +201,12 @@
     per_peer = length // shards
     arrived = arrived_ref[...]
     place, first_cell, second_cell = arrived_columns(arrived)
-    turned_rows = turned(arrived)[:CHANNELS].astype(BF16)
-    floats = dot(turned_rows, on_columns(place, length))
+    floats = dot_tn(arrived, on_columns(place, length))[:CHANNELS]
     normed, inverse_std, hidden = layer_norm(floats, gain_column(gain_ref))
     qkv = dot_tn(qkv_t_ref[...], hidden).astype(BF16)
-    query_rows_ref[...] = (turned(qkv[:CHANNELS]) * HEAD_DIM ** (-0.5)).astype(BF16)
+    scaled_query_ref[...] = (qkv[:CHANNELS].astype(F32) * HEAD_DIM ** (-0.5)).astype(BF16)
     key_ref[...] = qkv[CHANNELS : 2 * CHANNELS]
-    value_ref[:CHANNELS, :] = qkv[2 * CHANNELS :]
-    value_ref[CHANNELS:, :] = jnp.ones((CHANNELS, length), BF16)
+    value_ref[...] = qkv[2 * CHANNELS :]
     half_slot = lax.shift_right_logical(o_slot_ref[...], 1)
     kept = {}
 
@@ -242,9 +248,8 @@
 
     def scores(unit):
         start, head = unit
-        queries = query_rows_ref[start : start + CHUNK, :].astype(F32)
-        mask = head_lanes((CHUNK, CHANNELS), head)
-        return dot(jnp.where(mask, queries, 0.0).astype(BF16), key_ref[...])
+        own = slice(head * HEAD_DIM, (head + 1) * HEAD_DIM)
+        return dot_tn(scaled_query_ref[own, start : start + CHUNK], key_ref[own, :])
 
     def mix(unit):
         start, head = unit
@@ -252,19 +257,18 @@
         return dot_nt(value_ref[own, :], probs_ref[head, start : start + CHUNK, :])
 
     totals = []
-    ready = scores(units[0])
+    ready = [scores(unit) for unit in units[:AHEAD]]
     for number, (start, head) in enumerate(units):
-        now = ready
-        if number + 1 < len(units):
-            ready = scores(units[number + 1])
-        if number > 0:
-            totals.append(mix(units[number - 1]))
-        if number < len(chores):
-            chores[number]()
-        weights = jnp.exp(now)
+        if number + AHEAD < len(units):
+            ready.append(scores(units[number + AHEAD]))
+        if number >= LAG:
+            totals.append(mix(units[number - LAG]))
+        for chore in chores[number :: len(units)]:
+            chore()
+        weights = jnp.exp(ready.pop(0))
         share = 1.0 / jnp.sum(weights, axis=1, keepdims=True)
         probs_ref[head, start : start + CHUNK, :] = (weights * share).astype(BF16)
-    totals.append(mix(units[-1]))
+    totals += [mix(unit) for unit in units[len(units) - LAG :]]
     for number in range(0, len(units), HEADS):
         start = units[number][0]
         attended_ref[:, start : start + CHUNK] = jnp.concatenate(
@@ -311,8 +315,7 @@
     per_peer = length // shards
     blank = jnp.zeros((CHANNELS, length), BF16)
     odd = lax.bitwise_and(o_slot_ref[...], 1) == 1
-    slots = turned(returned_ref[:, per_peer:, :].reshape(length, 2 * CHANNELS)).astype(BF16)
-    both = dot(slots, slot_map_ref[...])
+    both = dot_tn(returned_ref[:, per_peer:, :].reshape(length, 2 * CHANNELS), slot_map_ref[...])
     grad_mixed = jnp.where(odd, both[CHANNELS:], both[:CHANNELS])
     grad_mixed_low = grad_mixed.astype(BF16)
     attended = attended_ref[...]
@@ -321,10 +324,12 @@
     scaled = grad_attended.astype(F32) * HEAD_DIM ** (-0.5)
     delta = -jnp.sum((scaled * attended).reshape(HEADS, HEAD_DIM, length), axis=1)
     delta_high = delta.astype(BF16).astype(F32)
-    rest = jnp.concatenate(
-        [delta_high, delta - delta_high, jnp.zeros((CHANNELS - 2 * HEADS, length), F32)], axis=0
-    )
-    upstream_ref[...] = jnp.concatenate([scaled, rest], axis=0).T.astype(BF16)
+    for head in range(HEADS):
+        own = slice(head * HEAD_DIM, (head + 1) * HEAD_DIM)
+        high, whole = delta_high[head : head + 1], delta[head : head + 1]
+        row = iota((HEAD_DIM, length), 0)
+        extra = jnp.where(row == 0, high, jnp.where(row == 1, whole - high, 0.0))
+        upstream_ref[head] = jnp.concatenate([scaled[own], extra], axis=0).astype(BF16)
     place, first_cell, second_cell = arrived_columns(arrived_ref[...])
     kept = {}
 
@@ -333,9 +338,9 @@
         kept["denom"] = cluster_counts(*kept["cells"])
 
     def pool():
-        rows = turned(returned_ref[:, :per_peer, :].reshape(length, 2 * CHANNELS)).astype(BF16)
+        rows = returned_ref[:, :per_peer, :].reshape(length, 2 * CHANNELS)
         first, second = kept["cells"]
-        sums = dot(rows[:CHANNELS], first) + dot(rows[CHANNELS:], second)
+        sums = dot_tn(rows, first)[:CHANNELS] + dot_tn(rows, second)[CHANNELS:]
         kept["mean"] = (sums / kept["denom"]).astype(BF16)
 
     def pool_out():
@@ -357,45 +362,39 @@
     eighth = length // 8
     chores += [functools.partial(map_places, k * eighth, eighth) for k in range(8)]
 
-    units = [(start, head) for start in range(0, length, CHUNK) for head in range(HEADS)]
-    lane = iota((CHUNK, 2 * CHANNELS), 1)
+    units = [(start, head) for head in range(HEADS) for start in range(0, length, CHUNK)]
 
     def change(unit):
         start, head = unit
-        mask = (
-            (lax.shift_right_logical(lane, 4) == head)
-            | (lane == CHANNELS + head)
-            | (lane == CHANNELS + HEADS + head)
-        )
-        upstream = upstream_ref[start : start + CHUNK, :].astype(F32)
-        return dot(jnp.where(mask, upstream, 0.0).astype(BF16), value_ref[...])
-
-    totals = []
-    ready = change(units[0])
+        own = slice(head * HEAD_DIM, (head + 1) * HEAD_DIM)
+        values = jnp.concatenate([value_ref[own, :], jnp.ones((HEAD_DIM, length), BF16)], axis=0)
+        return dot_tn(upstream_ref[head, :, start : start + CHUNK], values)
+
+    def use(unit, grad_scores):
+        start, head = unit
+        own = slice(head * HEAD_DIM, (head + 1) * HEAD_DIM)
+        rows = slice(start, start + CHUNK)
+        grad_query_ref[own, rows] = dot_nt(key_ref[own, :], grad_scores)
+        more = dot(query_ref[own, rows], grad_scores)
+        grad_key_ref[own, :] = more if start == 0 else grad_key_ref[own, :] + more
+
+    waiting = []
+    ready = [change(unit) for unit in units[:AHEAD]]
     for number, (start, head) in enumerate(units):
         own = slice(head * HEAD_DIM, (head + 1) * HEAD_DIM)
         rows = slice(start, start + CHUNK)
-        now = ready
-        if number + 1 < len(units):
-            ready = change(units[number + 1])
-        if number < len(chores):
-            chores[number]()
+        if number + AHEAD < len(units):
+            ready.append(change(units[number + AHEAD]))
+        if len(waiting) > LATE:
+            use(*waiting.pop(0))
+        for chore in chores[number :: len(units)]:
+            chore()
         probs = probs_ref[head, rows, :]
-        more_values = dot(grad_out_ref[own, rows], probs)
-        grad_scores = (probs.astype(F32) * now).astype(BF16)
-        totals.append(dot_nt(key_ref[own, :], grad_scores))
-        more_keys = dot(query_ref[own, rows], grad_scores)
-        if start == 0:
-            grad_value_ref[own, :] = more_values
-            grad_key_ref[own, :] = more_keys
-        else:
-            grad_value_ref[own, :] += more_values
-            grad_key_ref[own, :] += more_keys
-    for number in range(0, len(units), HEADS):
-        start = units[number][0]
-        grad_query_ref[:, start : start + CHUNK] = jnp.concatenate(
-            totals[number : number + HEADS], axis=0
-        )
+        more = dot(grad_out_ref[own, rows], probs)
+        grad_value_ref[own, :] = more if start == 0 else grad_value_ref[own, :] + more
+        waiting.append(((start, head), (probs.astype(F32) * ready.pop(0)).astype(BF16)))
+    for one in waiting:
+        use(*one)
     grad_qkv = jnp.concatenate(
         [grad_query_ref[...], grad_key_ref[...], grad_value_ref[...]], axis=0
     ).astype(BF16)
@@ -544,9 +543,9 @@
             shape((1, length), F32),
             shape((CHANNELS, length), BF16),
             shape((CHANNELS, length), BF16),
-            shape((lanes, length), BF16),
+            shape((CHANNELS, length), BF16),
         ),
-        scratch=(pltpu.VMEM((length, CHANNELS), BF16),),
+        scratch=(pltpu.VMEM((CHANNELS, length), BF16),),
         flops=1 << 32,
     )(arrived, o_slot, qkv_t, out_weight, pool_t, gain, upstream_pool)
     returned = exchange(both_ways)
@@ -555,7 +554,7 @@
         backward_kernel,
         (shape((shards, per_peer, lanes), BF16), shape((2 * CHANNELS, clusters), BF16)),
         scratch=(
-            pltpu.VMEM((length, lanes), BF16),
+            pltpu.VMEM((HEADS, 2 * HEAD_DIM, length), BF16),
             pltpu.VMEM((CHANNELS, length), BF16),
             pltpu.VMEM((CHANNELS, length), F32),
             pltpu.VMEM((CHANNELS, length), F32),

time: 113 us -> 112 us (level)
  no operation moved by 1% of the time
where the time goes in v8:
time: 112 us; the launch traced here: 111 us
  blocking collectives  86.6 us (77%)
  Pallas kernels  20.2 us (18%)
  starting transfers between devices  4.06 us (4%)
    all_to_all x3, blocking collectives, exchange(): lax.all_to_all(blocks, 'pts', split_axis=0, concat_axis=0, tiled=True)  72.6 us
    all_to_all x1, blocking collectives, body(): lax.all_to_all(total, 'pts', split_axis=0, concat_axis=0, tiled=True, axi...  14 us
    pallas_call x1, Pallas kernels, body(): call(backward_kernel, (shape((shards, per_peer, lanes), BF16), shape((2 *...  8.21 us
    pallas_call x1, Pallas kernels, body(): call(forward_kernel, (shape((shards, 2 * per_peer, lanes), BF16), shape((...  6.97 us
    ppermute x1, starting transfers between devices, body(): other = lax.ppermute(own, 'rep', [(0, 1), (1, 0)])  4.06 us
    pallas_call x1, Pallas kernels, body(): call(send_kernel, (shape((shards, per_peer, lanes), BF16), shape((1, leng...  2.66 us
  transfers between devices with their start and end apart: 1, of which 0 were waited for; matrix products, arithmetic and copies ran while one was open for 0% of the time, Pallas kernels for 1%

profile of v8, /device:TPU:1, one launch (start us, length us, event | category | flops | bytes accessed | tf_op | source)
XLA Modules:
  0.0 111.5 jit_solution(6761858904571654366)
XLA Ops:
  0.6 2.7 %shard_map.136 = (bf16[128,8,128]{2,1,0:T(8,128)(2,1)S(1)}, s32[1,1024]{1,0:T(1,128)S(1)}, s32[1,1024]{1,0:T(1,128)S(1)}, bf16[128,256]{1,0:T(8,128)(2,1)S(1)}, ...) custom-call(s32[1,1024]{1,0:T(1,128)} %pos_hbm.1, ...), custom_call_target="tpu_custom_call" | custom-call | flops 1073741824 | bytes 1048576 | tf_op jit(solution)/shard_map/pallas_call | solution.py:519
  3.3 29.4 %all_to_all.20 = bf16[128,8,128]{2,1,0:T(8,128)(2,1)S(1)} all-to-all(bf16[128,8,128]{2,1,0:T(8,128)(2,1)S(1)} %get-tuple-element.32), channel_id=1, replica_groups=mesh['pts'=128,'rep'=2] {'pts'}, dimensions={0} | all-to-all | bytes 524288 | tf_op jit(solution)/shard_map/all_to_all | solution.py:481
  32.7 7.0 %shard_map.137 = (bf16[128,16,128]{2,1,0:T(8,128)(2,1)S(1)}, f32[64,1024]{1,0:T(8,128)S(1)}, bf16[4,1024,1024]{2,1,0:T(8,128)(2,1)S(1)}, bf16[1024,1024]{1,0:T(8...) custom-call(bf16[1024,128]{1,0:T(8,128)(2,1)S(1)} %bitcast.16, ...), custom_call_target="tpu_custom_call" | custom-call | flops 4294967296 | bytes 1048576 | tf_op jit(solution)/shard_map/pallas_call | solution.py:534
  39.7 23.4 %all_to_all.21.returned_ref = bf16[128,16,128]{2,1,0:T(8,128)(2,1)S(1)} all-to-all(bf16[128,16,128]{2,1,0:T(8,128)(2,1)S(1)} %get-tuple-element.39), channel_id=1, replica_groups=mesh['pts'=128,'rep'=2] {'pts'}, dimensions={0} | all-to-all | bytes 1048576 | tf_op jit(solution)/shard_map/all_to_all | solution.py:481
  63.1 8.2 %shard_map.138 = (bf16[128,8,128]{2,1,0:T(8,128)(2,1)S(1)}, bf16[128,256]{1,0:T(8,128)(2,1)}) custom-call(bf16[128,16,128]{2,1,0:T(8,128)(2,1)S(1)} %all_to_all.21.returned_ref, bf16[1024,128]{1,0:T(8,128)(2,1)S(1)} %bitcast.17, s32[1,1024]{1,0:T(1,128)S(1)} %get-tuple-element.33.o_slot_ref, bf16[64,192]{1,0:T(8,128)(2,1)S(1)} %get-tuple-element.34.qkv_t_ref, ...), custom_call_target="tpu_custom_call" | custom-call | flops 8589934592 | bytes 1048576 | tf_op jit(solution)/shard_map/pallas_call | solution.py:553
  71.3 19.8 %all_to_all.22.arrived_ref = bf16[128,8,128]{2,1,0:T(8,128)(2,1)S(1)} all-to-all(bf16[128,8,128]{2,1,0:T(8,128)(2,1)S(1)} %get-tuple-element.50), channel_id=1, replica_groups=mesh['pts'=128,'rep'=2] {'pts'}, dimensions={0} | all-to-all | bytes 524288 | tf_op jit(solution)/shard_map/all_to_all | solution.py:481
  91.0 0.1 shard_map.139.own_ref
  91.2 4.1 %collective-permute-start = (f32[8,128]{1,0:T(8,128)S(1)}, f32[8,128]{1,0:T(8,128)S(1)}, u32[]{:S(2)}, u32[]{:S(2)}) collective-permute-start(f32[8,128]{1,0:T(8,128)S(1)} %shard_map.139.own_ref), channel_id=1, source_target_pairs={{0,1},{1,0},{2,3},{3,2},{4,5},{5,4},{6,7},{7,6},{8,9},{9,8},{10,11... | collective-permute-start | bytes 12296 | tf_op jit(solution)/shard_map/ppermute | solution.py:579
  95.2 1.2 %shard_map.140 = bf16[64,1024]{1,0:T(8,128)(2,1)} custom-call(bf16[1024,128]{1,0:T(8,128)(2,1)S(1)} %bitcast.14, s32[1,1024]{1,0:T(1,128)S(1)} %get-tuple-element.51.z_slot_ref), custom_call_target="tpu_custom_call" | custom-call | flops 1073741824 | bytes 1048576 | tf_op jit(solution)/shard_map/pallas_call | solution.py:580
  96.5 0.0 collective-permute-done.other_ref
  96.5 0.1 shard_map.141
  96.6 14.0 %all_to_all.23 = bf16[64,8,128]{2,1,0:T(8,128)(2,1)S(1)} all-to-all(bf16[64,8,128]{2,1,0:T(8,128)(2,1)S(1)} %shard_map.141), channel_id=1, replica_groups={{0,2,4,6,8,10,12,14,16,18,20,22,24,26,28,30,32,34,36,38,40,42,44,46,48,..., dimensions={0} | all-to-all | bytes 262144 | tf_op jit(solution)/shard_map/all_to_all | solution.py:585
  110.6 0.9 shard_map.142
Async XLA Ops:
  91.2 5.3 %collective-permute-start = (f32[8,128]{1,0:T(8,128)S(1)}, f32[8,128]{1,0:T(8,128)S(1)}, u32[]{:S(2)}, u32[]{:S(2)}) collective-permute-start(f32[8,128]{1,0:T(8,128)S(1)} %shard_map.139.own_ref), channel_id=1, source_target_pairs={{0,1},{1,0},{2,3},{3,2},{4,5},{5,4},{6,7},{7,6},{8,9},{9,8},{10,11... | collective-permute-start | bytes 12296 | tf_op jit(solution)/shard_map/ppermute | solution.py:579

commit v9 on v8

--- a/solution.py
+++ b/solution.py
@@ -301,7 +301,9 @@
     key_ref,
     value_ref,
     out_ref,
+    pooled_hbm,
     pooled_ref,
+    pooled_sem,
     upstream_ref,
     grad_out_ref,
     grad_query_ref,
@@ -331,6 +333,7 @@
         extra = jnp.where(row == 0, high, jnp.where(row == 1, whole - high, 0.0))
         upstream_ref[head] = jnp.concatenate([scaled[own], extra], axis=0).astype(BF16)
     place, first_cell, second_cell = arrived_columns(arrived_ref[...])
+    pooled_copy = pltpu.make_async_copy(pooled_ref, pooled_hbm, pooled_sem)
     kept = {}
 
     def cells():
@@ -345,6 +348,7 @@
 
     def pool_out():
         pooled_ref[...] = dot_tn(pool_t_ref[...], kept["mean"]).astype(BF16)
+        pooled_copy.start()
         empty = jnp.zeros((CHANNELS, clusters), BF16)
         kept["pool"] = [
             dot_nt(kept["mean"], jnp.concatenate([empty, half], axis=0))
@@ -420,6 +424,7 @@
     for start in range(0, shards, GROUP):
         rows = back[start * per_peer : start * per_peer + span] + side
         out_ref[start : start + GROUP] = rows.astype(BF16).reshape(GROUP, per_peer, 2 * CHANNELS)
+    pooled_copy.wait()
 
 
 def total_kernel(arrived_ref, out_ref):
@@ -428,9 +433,9 @@
 
 def spread_kernel(own_ref, other_ref, out_ref):
     total = own_ref[...] + other_ref[...]
-    high = total.astype(BF16).astype(F32)
-    low = pltpu.roll(total - high, CHANNELS, 1)
-    chosen = jnp.where(iota(total.shape, 1) >= CHANNELS, high, low)
+    half = total.shape[0] // 2
+    lower = pltpu.roll(total, CHANNELS, 1)[half:]
+    chosen = jnp.where(iota(lower.shape, 1) >= CHANNELS, total[:half], lower)
     out_ref[...] = jnp.broadcast_to(chosen[None], out_ref.shape).astype(BF16)
 
 
@@ -445,13 +450,19 @@
     total_ref,
     qkv_t_ref,
     gain_in_ref,
+    feat_ref,
     qkv_ref,
     out_ref,
     pool_ref,
     gain_ref,
+    feat_hbm,
+    feat_sem,
 ):
-    both = total_ref[...].astype(F32)
-    both = (both[:, CHANNELS:] + both[:, :CHANNELS]) * factor
+    feat_copy = pltpu.make_async_copy(feat_ref, feat_hbm, feat_sem)
+    feat_copy.start()
+    both = total_ref[...].astype(F32) * factor
+    both = jnp.concatenate([both[:, :, CHANNELS:], both[:, :, :CHANNELS]], axis=1)
+    both = both.reshape(both.shape[0] * both.shape[1], CHANNELS)
     piece = [both[k * CHANNELS : (k + 1) * CHANNELS] for k in range(6)]
     qkv = jnp.concatenate(piece[:3], axis=1)
     qkv_ref[...] = qkv
@@ -460,6 +471,7 @@
     column = jnp.sum(qkv * qkv_t_ref[...].astype(F32), axis=1, keepdims=True)
     eye = iota((CHANNELS, CHANNELS), 0) == iota((CHANNELS, CHANNELS), 1)
     gain_ref[...] = jnp.sum(jnp.where(eye, column, 0.0), axis=0, keepdims=True) / gain_in_ref[...]
+    feat_copy.wait()
 
 
 def shape(dims, dtype):
@@ -550,10 +562,15 @@
     )(arrived, o_slot, qkv_t, out_weight, pool_t, gain, upstream_pool)
     returned = exchange(both_ways)
 
+    block = pl.BlockSpec(memory_space=pltpu.VMEM)
+    outside = pl.BlockSpec(memory_space=pl.ANY)
     last, pooled = call(
         backward_kernel,
         (shape((shards, per_peer, lanes), BF16), shape((2 * CHANNELS, clusters), BF16)),
+        out_specs=(block, outside),
         scratch=(
+            pltpu.VMEM((2 * CHANNELS, clusters), BF16),
+            pltpu.SemaphoreType.DMA,
             pltpu.VMEM((HEADS, 2 * HEAD_DIM, length), BF16),
             pltpu.VMEM((CHANNELS, length), BF16),
             pltpu.VMEM((CHANNELS, length), F32),
@@ -581,7 +598,7 @@
         final.reshape(length, lanes), z_slot
     )
     other, feat_grad = lax.optimization_barrier((other, feat_grad))
-    total = call(spread_kernel, shape((GROUP, per_peer, lanes), BF16))(own, other)
+    total = call(spread_kernel, shape((GROUP, per_peer // 2, lanes), BF16))(own, other)
     gathered = lax.all_to_all(
         total,
         "pts",
@@ -591,17 +608,20 @@
         axis_index_groups=[
             list(range(start, start + GROUP)) for start in range(0, shards, GROUP)
         ],
-    ).reshape(GROUP * per_peer, lanes)
+    )
     factor = float(lax.axis_size("rep") * shards * length) ** (-0.5)
-    qkv_total, out_total, pool_total, gain_total = call(
+    qkv_total, out_total, pool_total, gain_total, feat_grad = call(
         functools.partial(finish_kernel, factor),
         (
             shape((CHANNELS, 3 * CHANNELS), F32),
             shape((CHANNELS, CHANNELS), F32),
             shape((CHANNELS, lanes), F32),
             shape((1, CHANNELS), F32),
+            shape((CHANNELS, length), BF16),
         ),
-    )(gathered, qkv_t, gain)
+        out_specs=(block, block, block, block, outside),
+        scratch=(pltpu.SemaphoreType.DMA,),
+    )(gathered, qkv_t, gain, feat_grad)
     return (
         pooled[None],
         feat_grad[None],

time: 112 us -> 111 us (level)
  transfers between devices with their start and end apart: 1 -> 1, of which waited for: 0 -> 1; matrix products, arithmetic and copies ran while one was open for 0% -> 0% of each run, Pallas kernels for 1% -> 1%
where the time goes in v9:
time: 111 us
  blocking collectives  85.5 us (77%)
  Pallas kernels  20.2 us (18%)
  starting transfers between devices  4.06 us (4%)
    all_to_all x3, blocking collectives, exchange(): lax.all_to_all(blocks, 'pts', split_axis=0, concat_axis=0, tiled=True)  72.5 us
    all_to_all x1, blocking collectives, body(): lax.all_to_all(total, 'pts', split_axis=0, concat_axis=0, tiled=True, axi...  13 us
    pallas_call x1, Pallas kernels, body(): call(backward_kernel, (shape((shards, per_peer, lanes), BF16), shape((2 *...  8.24 us
    pallas_call x1, Pallas kernels, body(): call(forward_kernel, (shape((shards, 2 * per_peer, lanes), BF16), shape((...  6.97 us
    ppermute x1, starting transfers between devices, body(): other = lax.ppermute(own, 'rep', [(0, 1), (1, 0)])  4.06 us
    pallas_call x1, Pallas kernels, body(): call(send_kernel, (shape((shards, per_peer, lanes), BF16), shape((1, leng...  2.66 us
  transfers between devices with their start and end apart: 1, of which 1 were waited for; matrix products, arithmetic and copies ran while one was open for 0% of the time, Pallas kernels for 1%

profile of v9, /device:TPU:1, one launch (start us, length us, event | category | flops | bytes accessed | tf_op | source)
XLA Modules:
  0.0 110.8 jit_solution(2325111134738414298)
XLA Ops:
  0.6 2.7 %shard_map.136 = (bf16[128,8,128]{2,1,0:T(8,128)(2,1)S(1)}, s32[1,1024]{1,0:T(1,128)S(1)}, s32[1,1024]{1,0:T(1,128)S(1)}, bf16[128,256]{1,0:T(8,128)(2,1)S(1)}, ...) custom-call(s32[1,1024]{1,0:T(1,128)} %pos_hbm.1, ...), custom_call_target="tpu_custom_call" | custom-call | flops 1073741824 | bytes 1048576 | tf_op jit(solution)/shard_map/pallas_call | solution.py:531
  3.3 29.4 %all_to_all.20 = bf16[128,8,128]{2,1,0:T(8,128)(2,1)S(1)} all-to-all(bf16[128,8,128]{2,1,0:T(8,128)(2,1)S(1)} %get-tuple-element.33), channel_id=1, replica_groups=mesh['pts'=128,'rep'=2] {'pts'}, dimensions={0} | all-to-all | bytes 524288 | tf_op jit(solution)/shard_map/all_to_all | solution.py:493
  32.7 7.0 %shard_map.137 = (bf16[128,16,128]{2,1,0:T(8,128)(2,1)S(1)}, f32[64,1024]{1,0:T(8,128)S(1)}, bf16[4,1024,1024]{2,1,0:T(8,128)(2,1)S(1)}, bf16[1024,1024]{1,0:T(8...) custom-call(bf16[1024,128]{1,0:T(8,128)(2,1)S(1)} %bitcast.14, ...), custom_call_target="tpu_custom_call" | custom-call | flops 4294967296 | bytes 1048576 | tf_op jit(solution)/shard_map/pallas_call | solution.py:546
  39.7 23.4 %all_to_all.21.returned_ref = bf16[128,16,128]{2,1,0:T(8,128)(2,1)S(1)} all-to-all(bf16[128,16,128]{2,1,0:T(8,128)(2,1)S(1)} %get-tuple-element.40), channel_id=1, replica_groups=mesh['pts'=128,'rep'=2] {'pts'}, dimensions={0} | all-to-all | bytes 1048576 | tf_op jit(solution)/shard_map/all_to_all | solution.py:493
  63.1 8.2 %shard_map.138 = (bf16[128,8,128]{2,1,0:T(8,128)(2,1)S(1)}, bf16[128,256]{1,0:T(8,128)(2,1)}) custom-call(bf16[128,16,128]{2,1,0:T(8,128)(2,1)S(1)} %all_to_all.21.returned_ref, bf16[1024,128]{1,0:T(8,128)(2,1)S(1)} %bitcast.15, s32[1,1024]{1,0:T(1,128)S(1)} %get-tuple-element.34.o_slot_ref, bf16[64,192]{1,0:T(8,128)(2,1)S(1)} %get-tuple-element.35.qkv_t_ref, ...), custom_call_target="tpu_custom_call" | custom-call | flops 8589934592 | bytes 1048576 | tf_op jit(solution)/shard_map/pallas_call | solution.py:567
  71.3 19.7 %all_to_all.22.arrived_ref = bf16[128,8,128]{2,1,0:T(8,128)(2,1)S(1)} all-to-all(bf16[128,8,128]{2,1,0:T(8,128)(2,1)S(1)} %get-tuple-element.51), channel_id=1, replica_groups=mesh['pts'=128,'rep'=2] {'pts'}, dimensions={0} | all-to-all | bytes 524288 | tf_op jit(solution)/shard_map/all_to_all | solution.py:493
  91.1 0.1 shard_map.139.own_ref
  91.2 4.1 %collective-permute-start = (f32[8,128]{1,0:T(8,128)S(1)}, f32[8,128]{1,0:T(8,128)S(1)}, u32[]{:S(2)}, u32[]{:S(2)}) collective-permute-start(f32[8,128]{1,0:T(8,128)S(1)} %shard_map.139.own_ref), channel_id=1, source_target_pairs={{0,1},{1,0},{2,3},{3,2},{4,5},{5,4},{6,7},{7,6},{8,9},{9,8},{10,11... | collective-permute-start | bytes 12296 | tf_op jit(solution)/shard_map/ppermute | solution.py:596
  95.3 0.6 shard_map.140.feat_ref
  95.8 0.2 collective-permute-done.other_ref
  96.1 0.1 shard_map.141
  96.2 13.0 %all_to_all.23.total_ref = bf16[64,4,128]{2,1,0:T(4,128)(2,1)S(1)} all-to-all(bf16[64,4,128]{2,1,0:T(4,128)(2,1)S(1)} %shard_map.141), channel_id=1, replica_groups={{0,2,4,6,8,10,12,14,16,18,20,22,24,26,28,30,32,34,36,38,40,42,44,46,48,..., dimensions={0} | all-to-all | bytes 131072 | tf_op jit(solution)/shard_map/all_to_all | solution.py:602
  109.2 1.5 %shard_map.142 = (f32[64,192]{1,0:T(8,128)}, f32[64,64]{1,0:T(8,128)}, f32[64,128]{1,0:T(8,128)}, f32[1,64]{1,0:T(1,128)}, bf16[64,1024]{1,0:T(8,128)(2,1)}) custom-call(bf16[64,4,128]{2,1,0:T(4,128)(2,1)S(1)} %all_to_all.23.total_ref, bf16[64,192]{1,0:T(8,128)(2,1)S(1)} %get-tuple-element.35.qkv_t_ref, f32[1,64]{1,0:T(1,128)S(1)} %get-tuple-element.38.gain_ref.gain_in_ref, ...), custom_call_target="tpu_custom_call" | custom-call | bytes 1048576 | tf_op jit(solution)/shard_map/pallas_call | solution.py:613
Async XLA Ops:
  91.2 4.9 %collective-permute-start = (f32[8,128]{1,0:T(8,128)S(1)}, f32[8,128]{1,0:T(8,128)S(1)}, u32[]{:S(2)}, u32[]{:S(2)}) collective-permute-start(f32[8,128]{1,0:T(8,128)S(1)} %shard_map.139.own_ref), channel_id=1, source_target_pairs={{0,1},{1,0},{2,3},{3,2},{4,5},{5,4},{6,7},{7,6},{8,9},{9,8},{10,11... | collective-permute-start | bytes 12296 | tf_op jit(solution)/shard_map/ppermute | solution.py:596

commit v10 on v9

--- a/solution.py
+++ b/solution.py
@@ -441,8 +441,8 @@
 
 def feat_grad_kernel(arrived_ref, z_slot_ref, out_ref):
     length = arrived_ref.shape[0]
-    rows = turned(arrived_ref[...])[:CHANNELS].astype(BF16)
-    out_ref[...] = dot(rows, on_rows(z_slot_ref[...], length)).astype(BF16)
+    z_map = on_rows(z_slot_ref[...], length)
+    out_ref[...] = dot_tn(arrived_ref[...], z_map)[:CHANNELS].astype(BF16)
 
 
 def finish_kernel(
@@ -450,16 +450,11 @@
     total_ref,
     qkv_t_ref,
     gain_in_ref,
-    feat_ref,
     qkv_ref,
     out_ref,
     pool_ref,
     gain_ref,
-    feat_hbm,
-    feat_sem,
 ):
-    feat_copy = pltpu.make_async_copy(feat_ref, feat_hbm, feat_sem)
-    feat_copy.start()
     both = total_ref[...].astype(F32) * factor
     both = jnp.concatenate([both[:, :, CHANNELS:], both[:, :, :CHANNELS]], axis=1)
     both = both.reshape(both.shape[0] * both.shape[1], CHANNELS)
@@ -471,7 +466,6 @@
     column = jnp.sum(qkv * qkv_t_ref[...].astype(F32), axis=1, keepdims=True)
     eye = iota((CHANNELS, CHANNELS), 0) == iota((CHANNELS, CHANNELS), 1)
     gain_ref[...] = jnp.sum(jnp.where(eye, column, 0.0), axis=0, keepdims=True) / gain_in_ref[...]
-    feat_copy.wait()
 
 
 def shape(dims, dtype):
@@ -610,18 +604,15 @@
         ],
     )
     factor = float(lax.axis_size("rep") * shards * length) ** (-0.5)
-    qkv_total, out_total, pool_total, gain_total, feat_grad = call(
+    qkv_total, out_total, pool_total, gain_total = call(
         functools.partial(finish_kernel, factor),
         (
             shape((CHANNELS, 3 * CHANNELS), F32),
             shape((CHANNELS, CHANNELS), F32),
             shape((CHANNELS, lanes), F32),
             shape((1, CHANNELS), F32),
-            shape((CHANNELS, length), BF16),
         ),
-        out_specs=(block, block, block, block, outside),
-        scratch=(pltpu.SemaphoreType.DMA,),
-    )(gathered, qkv_t, gain, feat_grad)
+    )(gathered, qkv_t, gain)
     return (
         pooled[None],
         feat_grad[None],

time: 111 us -> 111 us (level)
  transfers between devices with their start and end apart: 1 -> 1, of which waited for: 1 -> 0; matrix products, arithmetic and copies ran while one was open for 0% -> 0% of each run, Pallas kernels for 1% -> 1%
where the time goes in v10:
time: 111 us; the launch traced here: 110 us
  blocking collectives  85.5 us (77%)
  Pallas kernels  20.3 us (18%)
  starting transfers between devices  4.06 us (4%)
    all_to_all x3, blocking collectives, exchange(): lax.all_to_all(blocks, 'pts', split_axis=0, concat_axis=0, tiled=True)  72.6 us
    all_to_all x1, blocking collectives, body(): lax.all_to_all(total, 'pts', split_axis=0, concat_axis=0, tiled=True, axi...  13 us
    pallas_call x1, Pallas kernels, body(): call(backward_kernel, (shape((shards, per_peer, lanes), BF16), shape((2 *...  8.24 us
    pallas_call x1, Pallas kernels, body(): call(forward_kernel, (shape((shards, 2 * per_peer, lanes), BF16), shape((...  6.97 us
    ppermute x1, starting transfers between devices, body(): other = lax.ppermute(own, 'rep', [(0, 1), (1, 0)])  4.06 us
    pallas_call x1, Pallas kernels, body(): call(send_kernel, (shape((shards, per_peer, lanes), BF16), shape((1, leng...  2.66 us
  transfers between devices with their start and end apart: 1, of which 0 were waited for; matrix products, arithmetic and copies ran while one was open for 0% of the time, Pallas kernels for 1%

profile of v10, /device:TPU:1, one launch (start us, length us, event | category | flops | bytes accessed | tf_op | source)
XLA Modules:
  0.0 110.5 jit_solution(5346693734683547841)
XLA Ops:
  0.6 2.7 %shard_map.136 = (bf16[128,8,128]{2,1,0:T(8,128)(2,1)S(1)}, s32[1,1024]{1,0:T(1,128)S(1)}, s32[1,1024]{1,0:T(1,128)S(1)}, bf16[128,256]{1,0:T(8,128)(2,1)S(1)}, ...) custom-call(s32[1,1024]{1,0:T(1,128)} %pos_hbm.1, ...), custom_call_target="tpu_custom_call" | custom-call | flops 1073741824 | bytes 1048576 | tf_op jit(solution)/shard_map/pallas_call | solution.py:525
  3.3 29.4 %all_to_all.20 = bf16[128,8,128]{2,1,0:T(8,128)(2,1)S(1)} all-to-all(bf16[128,8,128]{2,1,0:T(8,128)(2,1)S(1)} %get-tuple-element.32), channel_id=1, replica_groups=mesh['pts'=128,'rep'=2] {'pts'}, dimensions={0} | all-to-all | bytes 524288 | tf_op jit(solution)/shard_map/all_to_all | solution.py:487
  32.7 7.0 %shard_map.137 = (bf16[128,16,128]{2,1,0:T(8,128)(2,1)S(1)}, f32[64,1024]{1,0:T(8,128)S(1)}, bf16[4,1024,1024]{2,1,0:T(8,128)(2,1)S(1)}, bf16[1024,1024]{1,0:T(8...) custom-call(bf16[1024,128]{1,0:T(8,128)(2,1)S(1)} %bitcast.14, ...), custom_call_target="tpu_custom_call" | custom-call | flops 4294967296 | bytes 1048576 | tf_op jit(solution)/shard_map/pallas_call | solution.py:540
  39.7 23.4 %all_to_all.21.returned_ref = bf16[128,16,128]{2,1,0:T(8,128)(2,1)S(1)} all-to-all(bf16[128,16,128]{2,1,0:T(8,128)(2,1)S(1)} %get-tuple-element.39), channel_id=1, replica_groups=mesh['pts'=128,'rep'=2] {'pts'}, dimensions={0} | all-to-all | bytes 1048576 | tf_op jit(solution)/shard_map/all_to_all | solution.py:487
  63.1 8.2 %shard_map.138 = (bf16[128,8,128]{2,1,0:T(8,128)(2,1)S(1)}, bf16[128,256]{1,0:T(8,128)(2,1)}) custom-call(bf16[128,16,128]{2,1,0:T(8,128)(2,1)S(1)} %all_to_all.21.returned_ref, bf16[1024,128]{1,0:T(8,128)(2,1)S(1)} %bitcast.15, s32[1,1024]{1,0:T(1,128)S(1)} %get-tuple-element.33.o_slot_ref, bf16[64,192]{1,0:T(8,128)(2,1)S(1)} %get-tuple-element.34.qkv_t_ref, ...), custom_call_target="tpu_custom_call" | custom-call | flops 8589934592 | bytes 1048576 | tf_op jit(solution)/shard_map/pallas_call | solution.py:561
  71.3 19.7 %all_to_all.22.arrived_ref = bf16[128,8,128]{2,1,0:T(8,128)(2,1)S(1)} all-to-all(bf16[128,8,128]{2,1,0:T(8,128)(2,1)S(1)} %get-tuple-element.50), channel_id=1, replica_groups=mesh['pts'=128,'rep'=2] {'pts'}, dimensions={0} | all-to-all | bytes 524288 | tf_op jit(solution)/shard_map/all_to_all | solution.py:487
  91.1 0.1 shard_map.139.own_ref
  91.2 4.1 %collective-permute-start = (f32[8,128]{1,0:T(8,128)S(1)}, f32[8,128]{1,0:T(8,128)S(1)}, u32[]{:S(2)}, u32[]{:S(2)}) collective-permute-start(f32[8,128]{1,0:T(8,128)S(1)} %shard_map.139.own_ref), channel_id=1, source_target_pairs={{0,1},{1,0},{2,3},{3,2},{4,5},{5,4},{6,7},{7,6},{8,9},{9,8},{10,11... | collective-permute-start | bytes 12296 | tf_op jit(solution)/shard_map/ppermute | solution.py:590
  95.3 1.3 %shard_map.140 = bf16[64,1024]{1,0:T(8,128)(2,1)} custom-call(bf16[1024,128]{1,0:T(8,128)(2,1)S(1)} %bitcast.13, s32[1,1024]{1,0:T(1,128)S(1)} %get-tuple-element.51.z_slot_ref), custom_call_target="tpu_custom_call" | custom-call | flops 1073741824 | bytes 1048576 | tf_op jit(solution)/shard_map/pallas_call | solution.py:591
  96.6 0.0 collective-permute-done.other_ref
  96.6 0.1 shard_map.141
  96.7 13.0 %all_to_all.23.total_ref = bf16[64,4,128]{2,1,0:T(4,128)(2,1)S(1)} all-to-all(bf16[64,4,128]{2,1,0:T(4,128)(2,1)S(1)} %shard_map.141), channel_id=1, replica_groups={{0,2,4,6,8,10,12,14,16,18,20,22,24,26,28,30,32,34,36,38,40,42,44,46,48,..., dimensions={0} | all-to-all | bytes 131072 | tf_op jit(solution)/shard_map/all_to_all | solution.py:596
  109.6 0.9 shard_map.142
Async XLA Ops:
  91.2 5.4 %collective-permute-start = (f32[8,128]{1,0:T(8,128)S(1)}, f32[8,128]{1,0:T(8,128)S(1)}, u32[]{:S(2)}, u32[]{:S(2)}) collective-permute-start(f32[8,128]{1,0:T(8,128)S(1)} %shard_map.139.own_ref), channel_id=1, source_target_pairs={{0,1},{1,0},{2,3},{3,2},{4,5},{5,4},{6,7},{7,6},{8,9},{9,8},{10,11... | collective-permute-start | bytes 12296 | tf_op jit(solution)/shard_map/ppermute | solution.py:590
